TPU v7x, 256 devices: a whole 4x4x8 slice. The times are simulated.
256 devices in a mesh: ctx: 64 (over y, z, core), head: 4 (over x).
Axes of the slice: x: 4, y: 4, z: 8, core: 2. Of those that a mesh axis runs over, the one named last changes fastest.
Arguments:
- queries: bfloat16 [16384, 2048], P('ctx', 'head'), may hold values from -6 to 6
- keys: bfloat16 [16384, 2048], P('ctx', 'head'), may hold values from -6 to 6
- values: bfloat16 [16384, 2048], P('ctx', 'head'), may hold values from -6 to 6
- out_grad: bfloat16 [16384, 2048], P('ctx', 'head'), may hold values from -6 to 6
- doc_lengths: int32 [32], replicated, may hold values from 1 to 768, as said below
Outputs:
- attended: float32 [16384, 2048], P('ctx', 'head')
- query_grad: float32 [16384, 2048], P('ctx', 'head')
- key_grad: float32 [16384, 2048], P('ctx', 'head')
- value_grad: float32 [16384, 2048], P('ctx', 'head')
Inputs may be any that keep to these rules, and one draw needn't show every extreme that they name: `doc_lengths`: the first document has exactly 768 tokens, every other one 1 to 768, and all lengths sum to 16384.
All inputs are finite; a program needn't handle non-finite values.
Results may differ from a plain program's by a relative error of at most 0.0095.
Values may be sent and summed in bfloat16 or wider, within the bound.
No kernel may reach another device: no remote copies, remote signals or barrier semaphores. Data moves between devices by JAX's collectives and lax.ppermute only.
A program may use at most 64 MiB of HBM per device.

v0:
```python
import math

import jax
import jax.numpy as jnp
from jax import lax
from jax.sharding import PartitionSpec as P

HD = 128
PROMPT = 64


NEG_FILL = -1e30


def from_root(value, axis, source):
    kept = jnp.where(lax.axis_index(axis) == source, value, 0).astype(value.dtype)
    return lax.psum(kept, axis)


def passed_along(block, axis, distance):
    devices = range(lax.axis_size(axis))
    route = [(i - distance, i) for i in devices if i - distance in devices]
    return lax.ppermute(block, axis, route)


def shifted(value, axis, by):
    length = lax.axis_size(axis)
    return lax.ppermute(value, axis, [(i, (i + by) % length) for i in range(length)])


def on_device(queries, keys, values, out_grad, doc_lengths):
    tok_rows = queries.shape[0]
    feat_width = queries.shape[1]
    heads_here = feat_width // HD
    ctx_count = lax.axis_size("ctx")
    reach = min(3, ctx_count // 2 - 1)
    own_block = lax.axis_index("ctx")
    score_scale = 1.0 / math.sqrt(HD)
    doc_ends = jnp.cumsum(doc_lengths)
    offsets = jnp.arange(tok_rows, dtype=jnp.int32)
    prompt_pos = jnp.arange(PROMPT, dtype=jnp.int32)
    q_three = queries.reshape(tok_rows, heads_here, HD)
    k_three = keys.reshape(tok_rows, heads_here, HD)
    v_three = values.reshape(tok_rows, heads_here, HD)
    dout_three = out_grad.reshape(tok_rows, heads_here, HD)
    prompt_k, prompt_v = (
        from_root(k_three[:PROMPT], "ctx", 0),
        from_root(v_three[:PROMPT], "ctx", 0),
    )

    def block_segments(block):
        positions = block * tok_rows + offsets
        return jnp.sum((doc_ends[None, :] <= positions[:, None]).astype(jnp.int32), axis=1)

    def tile_scores(query_rows, key_rows, query_block, key_block):
        scores = (
            jnp.einsum("thd,uhd->htu", query_rows, key_rows, preferred_element_type=jnp.float32)
            * score_scale
        )
        query_pos = query_block * tok_rows + offsets
        key_pos = key_block * tok_rows + offsets
        same_doc = block_segments(query_block)[:, None] == block_segments(key_block)[None, :]
        allowed = (key_pos[None, :] <= query_pos[:, None]) & same_doc & (key_pos[None, :] >= PROMPT)
        return (scores, allowed)

    def fold_scored(partial_value, scores, allowed, value_rows):
        running, totals, accum = partial_value
        row_top = jnp.max(jnp.where(allowed[None], scores, NEG_FILL), axis=2)
        newest = jnp.maximum(running, row_top)
        fading = jnp.exp(running - newest)
        weights = jnp.where(allowed[None], jnp.exp(scores - newest[:, :, None]), 0.0)
        totals = totals * fading + jnp.sum(weights, axis=2)
        added = jnp.einsum(
            "htu,uhd->thd", weights, value_rows.astype(jnp.float32), precision=lax.Precision.HIGHEST
        )
        accum = accum * fading.T[:, :, None] + added
        return (newest, totals, accum)

    def fold_tile(partial_value, query_rows, key_rows, value_rows, query_block, key_block):
        scores, allowed = tile_scores(query_rows, key_rows, query_block, key_block)
        return fold_scored(partial_value, scores, allowed, value_rows)

    def guarded_fold(partial_value, query_rows, key_rows, value_rows, query_block, key_block):
        return fold_tile(partial_value, query_rows, key_rows, value_rows, query_block, key_block)

    empty_partial = (
        jnp.full((heads_here, tok_rows), NEG_FILL, jnp.float32),
        jnp.zeros((heads_here, tok_rows), jnp.float32),
        jnp.zeros((tok_rows, heads_here, HD), jnp.float32),
    )
    scores = (
        jnp.einsum("thd,uhd->htu", q_three, prompt_k, preferred_element_type=jnp.float32)
        * score_scale
    )
    query_pos = own_block * tok_rows + offsets
    allowed = prompt_pos[None, :] <= query_pos[:, None]
    p_scores = scores
    p_allowed = allowed
    prompt_partial = fold_scored(empty_partial, p_scores, p_allowed, prompt_v)
    partial_value = fold_tile(prompt_partial, q_three, k_three, v_three, own_block, own_block)

    def forward_turn(distance, carried):
        key_rows, value_rows, running, totals, accum = carried
        key_rows, value_rows = passed_along((key_rows, value_rows), "ctx", 1)
        key_block = (own_block - distance) % ctx_count
        running, totals, accum = guarded_fold(
            (running, totals, accum), q_three, key_rows, value_rows, own_block, key_block
        )
        return (key_rows, value_rows, running, totals, accum)

    looped = lax.fori_loop(1, reach + 1, forward_turn, (k_three, v_three) + partial_value)
    running, totals, accum = (looped[2], looped[3], looped[4])
    attended_three = accum / totals.T[:, :, None]
    lse_rows = running + jnp.log(totals)
    delta_rows = jnp.sum(dout_three.astype(jnp.float32) * attended_three, axis=2).T

    def grad_scored(
        query_rows, dout_rows, lse_part, delta_part, key_rows, value_rows, scores, allowed
    ):
        weights = jnp.where(allowed[None], jnp.exp(scores - lse_part[:, :, None]), 0.0)
        rounded = weights.astype(jnp.bfloat16)
        value_part = jnp.einsum(
            "htu,thd->uhd", rounded, dout_rows, preferred_element_type=jnp.float32
        )
        dprob = jnp.einsum(
            "thd,uhd->htu", dout_rows, value_rows, preferred_element_type=jnp.float32
        )
        dscore = (weights * (dprob - delta_part[:, :, None])).astype(jnp.bfloat16)
        query_part = jnp.einsum(
            "htu,uhd->thd", dscore, key_rows, preferred_element_type=jnp.float32
        )
        key_part = jnp.einsum(
            "htu,thd->uhd", dscore, query_rows, preferred_element_type=jnp.float32
        )
        return (query_part, key_part, value_part)

    def grad_tile(
        query_rows, dout_rows, lse_part, delta_part, key_rows, value_rows, query_block, key_block
    ):
        scores, allowed = tile_scores(query_rows, key_rows, query_block, key_block)
        return grad_scored(
            query_rows, dout_rows, lse_part, delta_part, key_rows, value_rows, scores, allowed
        )

    def guarded_grad(
        query_rows, dout_rows, lse_part, delta_part, key_rows, value_rows, query_block, key_block
    ):
        return grad_tile(
            query_rows,
            dout_rows,
            lse_part,
            delta_part,
            key_rows,
            value_rows,
            query_block,
            key_block,
        )

    prompt_q, prompt_dk, prompt_dv = grad_scored(
        q_three, dout_three, lse_rows, delta_rows, prompt_k, prompt_v, p_scores, p_allowed
    )
    prompt_dk, prompt_dv = lax.psum((prompt_dk, prompt_dv), "ctx")
    own_grads = grad_tile(
        q_three, dout_three, lse_rows, delta_rows, k_three, v_three, own_block, own_block
    )
    home_grads = (own_grads[0] + prompt_q, own_grads[1], own_grads[2])

    def key_turn(distance, carried):
        key_rows, value_rows, query_acc, key_acc, value_acc = carried
        key_rows, value_rows = passed_along((key_rows, value_rows), "ctx", 1)
        key_acc, value_acc = (
            shifted(key_acc.astype(jnp.bfloat16), "ctx", 1).astype(key_acc.dtype),
            shifted(value_acc.astype(jnp.bfloat16), "ctx", 1).astype(value_acc.dtype),
        )
        key_block = (own_block - distance) % ctx_count
        parts = guarded_grad(
            q_three, dout_three, lse_rows, delta_rows, key_rows, value_rows, own_block, key_block
        )
        return (
            key_rows,
            value_rows,
            query_acc + parts[0],
            key_acc + parts[1],
            value_acc + parts[2],
        )

    looped = lax.fori_loop(1, reach + 1, key_turn, (k_three, v_three) + home_grads)
    query_acc = looped[2]
    key_acc, value_acc = (
        shifted(looped[3].astype(jnp.bfloat16), "ctx", -reach).astype(jnp.float32),
        shifted(looped[4].astype(jnp.bfloat16), "ctx", -reach).astype(jnp.float32),
    )
    first_block = own_block == 0
    key_acc = key_acc.at[:PROMPT].add(jnp.where(first_block, prompt_dk, 0.0))
    value_acc = value_acc.at[:PROMPT].add(jnp.where(first_block, prompt_dv, 0.0))
    attended = attended_three.reshape(tok_rows, feat_width)
    query_grad = (query_acc * score_scale).reshape(tok_rows, feat_width)
    key_grad = (key_acc * score_scale).reshape(tok_rows, feat_width)
    value_grad = value_acc.reshape(tok_rows, feat_width)
    return (attended, query_grad, key_grad, value_grad)


def solution(mesh):
    in_specs = (P("ctx", "head"), P("ctx", "head"), P("ctx", "head"), P("ctx", "head"), P())
    out_specs = (P("ctx", "head"), P("ctx", "head"), P("ctx", "head"), P("ctx", "head"))
    return jax.shard_map(
        on_device, mesh=mesh, in_specs=in_specs, out_specs=out_specs, check_vma=False
    )
```

profile of v0, /device:TPU:1, one launch (start us, length us, event | category | flops | bytes accessed | tf_op | source)
XLA Modules:
  0.0 486.1 jit_solution(2423387103848889004)
XLA Ops:
  14.9 173.8 %all-reduce.7.cloned.1.call-done = (bf16[64,4,128]{2,0,1:T(8,128)(2,1)}, bf16[64,4,128]{2,0,1:T(8,128)(2,1)}) async-done(((bf16[64,4,128]{2,0,1:T(8,128)(2,1)}, bf16[64,4,128]{2,0,1:T(8,128)(2,1)}), (bf16[64,4,128]{2,0,1:T(8,128)(2,1)}, bf16[64,4,128]{2,0,1:T(8,128)(2,1)})) %all-reduce.7.cloned.1.call-update) | async-done | bytes 131088 | tf_op jit(solution)/shard_map/psum | solution.py:17
  192.2 35.3 %while.52 = (s32[]{:T(128)}, bf16[256,4,128]{2,0,1:T(8,128)(2,1)}, bf16[256,4,128]{2,0,1:T(8,128)(2,1)}, f32[4,256]{1,0:T(4,128)S(1)}, f32[4,256]{1,0:T(4,128)S(...) while((s32[]{:T(128)}, bf16[256,4,128]{2,0,1:T(8,128)(2,1)}, ...), condition=%wide.region_13.14_spmd.clone.clone, body=%wide.region_8.13_spmd.clone.clone.sunk | while | flops 472436224 | bytes 8465390 | solution.py:111
  192.2 1.9 collective-permute-start
  194.1 1.9 collective-permute-start.1
  202.4 4.3 collective-permute-start
  206.7 1.9 collective-permute-start.1
  215.0 4.3 collective-permute-start
  219.3 1.9 collective-permute-start.1
  234.8 51.5 %while.53 = (s32[]{:T(128)}, bf16[256,4,128]{2,0,1:T(8,128)(2,1)S(1)}, bf16[256,4,128]{2,0,1:T(8,128)(2,1)S(1)}, f32[256,4,128]{2,0,1:T(8,128)S(1)}, bf16[256,4,...) while((s32[]{:T(128)}, ...), condition=%wide.region_18.19_spmd.clone.clone, body=%wide.region_15.18_spmd.clone.clone.sunk | while | flops 338608640 | bytes 14044246 | solution.py:187
  234.8 4.3 collective-permute-start.2
  239.1 1.9 collective-permute-start.3
  242.8 2.4 collective-permute-done.3
  245.8 2.3 collective-permute-done.4
  251.9 4.3 collective-permute-start.2
  256.2 1.9 collective-permute-start.3
  263.0 2.2 collective-permute-done.4
  266.3 1.8 collective-permute-done.5
  269.1 4.3 collective-permute-start.2
  273.4 1.9 collective-permute-start.3
  276.3 2.1 collective-permute-start.5
  280.1 2.2 collective-permute-done.4
  286.2 3.1 collective-permute-start.7
  292.6 5.5 %collective-permute-done.7 = bf16[256,4,128]{2,0,1:T(8,128)(2,1)S(1)} collective-permute-done((bf16[256,4,128]{2,0,1:T(8,128)(2,1)}, bf16[256,4,128]{2,0,1:T(8,128)(2,1)S(1)}, u32[]{:S(2)}, u32[]{:S(2)}) %collective-permute-start.7) | collective-permute-done | bytes 262176 | tf_op jit(solution)/shard_map/ppermute | solution.py:28
  298.1 177.6 %all-reduce.5.cloned.1.call-done = (f32[64,4,128]{2,0,1:T(8,128)}, f32[64,4,128]{2,0,1:T(8,128)}) async-done(((f32[64,4,128]{2,0,1:T(8,128)}, f32[64,4,128]{2,0,1:T(8,128)}), (f32[64,4,128]{2,0,1:T(8,128)}, f32[64,4,128]{2,0,1:T(8,128)})) %all-reduce.5.cloned.1.call-update) | async-done | bytes 262160 | tf_op jit(solution)/shard_map/psum | solution.py:162
  (187 shorter events, 63.1 us)
Async XLA Ops:
  7.2 181.6 %all-reduce.7.cloned.1.call-start = ((), (), s32[]{:S(2)}) async-start(), calls=%async_computation.1 | async-start | bytes 262144 | tf_op jit(solution)/shard_map/psum | solution.py:17
  9.4 466.4 %all-reduce.5.cloned.1.call-start = ((), (), s32[]{:S(2)}) async-start(), calls=%async_computation | async-start | bytes 524288 | tf_op jit(solution)/shard_map/psum | solution.py:162
  12.1 179.2 %copy-start.2 = (bf16[256,512]{0,1:T(8,128)(2,1)}, bf16[256,512]{0,1:T(8,128)(2,1)S(1)}, u32[]{:S(2)}) copy-start(bf16[256,512]{0,1:T(8,128)(2,1)S(1)} %copy.67) | copy-start | bytes 786436
  192.2 5.5 %collective-permute-start = (bf16[256,4,128]{2,0,1:T(8,128)(2,1)}, bf16[256,4,128]{2,0,1:T(8,128)(2,1)S(1)}, u32[]{:S(2)}, u32[]{:S(2)}) collective-permute-start(bf16[256,4,128]{2,0,1:T(8,128)(2,1)} %get-tuple-element.1028), channel_id=1, source_target_pairs={{0,4},{4,8},{8,12},{12,16},{16,20},{20,24},{24,28},{28,32},{32,36}... | collective-permute-start | bytes 786440 | tf_op jit(solution)/shard_map/while/body/eval_jaxpr/ppermute | solution.py:23
  194.1 6.4 %collective-permute-start.1 = (bf16[256,4,128]{2,0,1:T(8,128)(2,1)}, bf16[256,4,128]{2,0,1:T(8,128)(2,1)S(1)}, u32[]{:S(2)}, u32[]{:S(2)}) collective-permute-start(bf16[256,4,128]{2,0,1:T(8,128)(2,1)} %get-tuple-element.1029), channel_id=1, source_target_pairs={{0,4},{4,8},{8,12},{12,16},{16,20},{20,24},{24,28},{28,32},{32,36}... | collective-permute-start | bytes 786440 | tf_op jit(solution)/shard_map/while/body/eval_jaxpr/ppermute | solution.py:23
  202.4 7.9 %collective-permute-start = (bf16[256,4,128]{2,0,1:T(8,128)(2,1)}, bf16[256,4,128]{2,0,1:T(8,128)(2,1)S(1)}, u32[]{:S(2)}, u32[]{:S(2)}) collective-permute-start(bf16[256,4,128]{2,0,1:T(8,128)(2,1)} %get-tuple-element.1028), channel_id=1, source_target_pairs={{0,4},{4,8},{8,12},{12,16},{16,20},{20,24},{24,28},{28,32},{32,36}... | collective-permute-start | bytes 786440 | tf_op jit(solution)/shard_map/while/body/eval_jaxpr/ppermute | solution.py:23
  206.7 6.4 %collective-permute-start.1 = (bf16[256,4,128]{2,0,1:T(8,128)(2,1)}, bf16[256,4,128]{2,0,1:T(8,128)(2,1)S(1)}, u32[]{:S(2)}, u32[]{:S(2)}) collective-permute-start(bf16[256,4,128]{2,0,1:T(8,128)(2,1)} %get-tuple-element.1029), channel_id=1, source_target_pairs={{0,4},{4,8},{8,12},{12,16},{16,20},{20,24},{24,28},{28,32},{32,36}... | collective-permute-start | bytes 786440 | tf_op jit(solution)/shard_map/while/body/eval_jaxpr/ppermute | solution.py:23
  215.0 7.9 %collective-permute-start = (bf16[256,4,128]{2,0,1:T(8,128)(2,1)}, bf16[256,4,128]{2,0,1:T(8,128)(2,1)S(1)}, u32[]{:S(2)}, u32[]{:S(2)}) collective-permute-start(bf16[256,4,128]{2,0,1:T(8,128)(2,1)} %get-tuple-element.1028), channel_id=1, source_target_pairs={{0,4},{4,8},{8,12},{12,16},{16,20},{20,24},{24,28},{28,32},{32,36}... | collective-permute-start | bytes 786440 | tf_op jit(solution)/shard_map/while/body/eval_jaxpr/ppermute | solution.py:23
  219.3 6.4 %collective-permute-start.1 = (bf16[256,4,128]{2,0,1:T(8,128)(2,1)}, bf16[256,4,128]{2,0,1:T(8,128)(2,1)S(1)}, u32[]{:S(2)}, u32[]{:S(2)}) collective-permute-start(bf16[256,4,128]{2,0,1:T(8,128)(2,1)} %get-tuple-element.1029), channel_id=1, source_target_pairs={{0,4},{4,8},{8,12},{12,16},{16,20},{20,24},{24,28},{28,32},{32,36}... | collective-permute-start | bytes 786440 | tf_op jit(solution)/shard_map/while/body/eval_jaxpr/ppermute | solution.py:23
  234.8 7.6 %collective-permute-start.2 = (bf16[256,4,128]{2,0,1:T(8,128)(2,1)S(1)}, bf16[256,4,128]{2,0,1:T(8,128)(2,1)S(1)}, u32[]{:S(2)}, u32[]{:S(2)}) collective-permute-start(bf16[256,4,128]{2,0,1:T(8,128)(2,1)S(1)} %get-tuple-element.1076), channel_id=1, source_target_pairs={{0,4},{4,8},{8,12},{12,16},{16,20},{20,24},{24,28},{28,32},{32,36}... | collective-permute-start | bytes 786440 | tf_op jit(solution)/shard_map/while/body/eval_jaxpr/ppermute | solution.py:23
  239.1 6.1 %collective-permute-start.3 = (bf16[256,4,128]{2,0,1:T(8,128)(2,1)S(1)}, bf16[256,4,128]{2,0,1:T(8,128)(2,1)S(1)}, u32[]{:S(2)}, u32[]{:S(2)}) collective-permute-start(bf16[256,4,128]{2,0,1:T(8,128)(2,1)S(1)} %get-tuple-element.1077), channel_id=1, source_target_pairs={{0,4},{4,8},{8,12},{12,16},{16,20},{20,24},{24,28},{28,32},{32,36}... | collective-permute-start | bytes 786440 | tf_op jit(solution)/shard_map/while/body/eval_jaxpr/ppermute | solution.py:23
  241.0 7.1 %collective-permute-start.4 = (bf16[256,4,128]{2,0,1:T(8,128)(2,1)}, bf16[256,4,128]{2,0,1:T(8,128)(2,1)S(1)}, u32[]{:S(2)}, u32[]{:S(2)}) collective-permute-start(bf16[256,4,128]{2,0,1:T(8,128)(2,1)} %get-tuple-element.1079), channel_id=1, source_target_pairs={{0,4},{4,8},{8,12},{12,16},{16,20},{20,24},{24,28},{28,32},{32,36}... | collective-permute-start | bytes 786440 | tf_op jit(solution)/shard_map/while/body/eval_jaxpr/ppermute | solution.py:28
  241.7 9.2 %collective-permute-start.5 = (bf16[256,4,128]{2,0,1:T(8,128)(2,1)}, bf16[256,4,128]{2,0,1:T(8,128)(2,1)S(1)}, u32[]{:S(2)}, u32[]{:S(2)}) collective-permute-start(bf16[256,4,128]{2,0,1:T(8,128)(2,1)} %get-tuple-element.1080), channel_id=1, source_target_pairs={{0,4},{4,8},{8,12},{12,16},{16,20},{20,24},{24,28},{28,32},{32,36}... | collective-permute-start | bytes 786440 | tf_op jit(solution)/shard_map/while/body/eval_jaxpr/ppermute | solution.py:28
  251.9 8.3 %collective-permute-start.2 = (bf16[256,4,128]{2,0,1:T(8,128)(2,1)S(1)}, bf16[256,4,128]{2,0,1:T(8,128)(2,1)S(1)}, u32[]{:S(2)}, u32[]{:S(2)}) collective-permute-start(bf16[256,4,128]{2,0,1:T(8,128)(2,1)S(1)} %get-tuple-element.1076), channel_id=1, source_target_pairs={{0,4},{4,8},{8,12},{12,16},{16,20},{20,24},{24,28},{28,32},{32,36}... | collective-permute-start | bytes 786440 | tf_op jit(solution)/shard_map/while/body/eval_jaxpr/ppermute | solution.py:23
  256.2 6.1 %collective-permute-start.3 = (bf16[256,4,128]{2,0,1:T(8,128)(2,1)S(1)}, bf16[256,4,128]{2,0,1:T(8,128)(2,1)S(1)}, u32[]{:S(2)}, u32[]{:S(2)}) collective-permute-start(bf16[256,4,128]{2,0,1:T(8,128)(2,1)S(1)} %get-tuple-element.1077), channel_id=1, source_target_pairs={{0,4},{4,8},{8,12},{12,16},{16,20},{20,24},{24,28},{28,32},{32,36}... | collective-permute-start | bytes 786440 | tf_op jit(solution)/shard_map/while/body/eval_jaxpr/ppermute | solution.py:23
  258.1 7.1 %collective-permute-start.4 = (bf16[256,4,128]{2,0,1:T(8,128)(2,1)}, bf16[256,4,128]{2,0,1:T(8,128)(2,1)S(1)}, u32[]{:S(2)}, u32[]{:S(2)}) collective-permute-start(bf16[256,4,128]{2,0,1:T(8,128)(2,1)} %get-tuple-element.1079), channel_id=1, source_target_pairs={{0,4},{4,8},{8,12},{12,16},{16,20},{20,24},{24,28},{28,32},{32,36}... | collective-permute-start | bytes 786440 | tf_op jit(solution)/shard_map/while/body/eval_jaxpr/ppermute | solution.py:28
  258.8 9.2 %collective-permute-start.5 = (bf16[256,4,128]{2,0,1:T(8,128)(2,1)}, bf16[256,4,128]{2,0,1:T(8,128)(2,1)S(1)}, u32[]{:S(2)}, u32[]{:S(2)}) collective-permute-start(bf16[256,4,128]{2,0,1:T(8,128)(2,1)} %get-tuple-element.1080), channel_id=1, source_target_pairs={{0,4},{4,8},{8,12},{12,16},{16,20},{20,24},{24,28},{28,32},{32,36}... | collective-permute-start | bytes 786440 | tf_op jit(solution)/shard_map/while/body/eval_jaxpr/ppermute | solution.py:28
  269.1 9.6 %collective-permute-start.2 = (bf16[256,4,128]{2,0,1:T(8,128)(2,1)S(1)}, bf16[256,4,128]{2,0,1:T(8,128)(2,1)S(1)}, u32[]{:S(2)}, u32[]{:S(2)}) collective-permute-start(bf16[256,4,128]{2,0,1:T(8,128)(2,1)S(1)} %get-tuple-element.1076), channel_id=1, source_target_pairs={{0,4},{4,8},{8,12},{12,16},{16,20},{20,24},{24,28},{28,32},{32,36}... | collective-permute-start | bytes 786440 | tf_op jit(solution)/shard_map/while/body/eval_jaxpr/ppermute | solution.py:23
  273.4 6.1 %collective-permute-start.3 = (bf16[256,4,128]{2,0,1:T(8,128)(2,1)S(1)}, bf16[256,4,128]{2,0,1:T(8,128)(2,1)S(1)}, u32[]{:S(2)}, u32[]{:S(2)}) collective-permute-start(bf16[256,4,128]{2,0,1:T(8,128)(2,1)S(1)} %get-tuple-element.1077), channel_id=1, source_target_pairs={{0,4},{4,8},{8,12},{12,16},{16,20},{20,24},{24,28},{28,32},{32,36}... | collective-permute-start | bytes 786440 | tf_op jit(solution)/shard_map/while/body/eval_jaxpr/ppermute | solution.py:23
  275.3 7.1 %collective-permute-start.4 = (bf16[256,4,128]{2,0,1:T(8,128)(2,1)}, bf16[256,4,128]{2,0,1:T(8,128)(2,1)S(1)}, u32[]{:S(2)}, u32[]{:S(2)}) collective-permute-start(bf16[256,4,128]{2,0,1:T(8,128)(2,1)} %get-tuple-element.1079), channel_id=1, source_target_pairs={{0,4},{4,8},{8,12},{12,16},{16,20},{20,24},{24,28},{28,32},{32,36}... | collective-permute-start | bytes 786440 | tf_op jit(solution)/shard_map/while/body/eval_jaxpr/ppermute | solution.py:28
  276.3 8.9 %collective-permute-start.5 = (bf16[256,4,128]{2,0,1:T(8,128)(2,1)}, bf16[256,4,128]{2,0,1:T(8,128)(2,1)S(1)}, u32[]{:S(2)}, u32[]{:S(2)}) collective-permute-start(bf16[256,4,128]{2,0,1:T(8,128)(2,1)} %get-tuple-element.1080), channel_id=1, source_target_pairs={{0,4},{4,8},{8,12},{12,16},{16,20},{20,24},{24,28},{28,32},{32,36}... | collective-permute-start | bytes 786440 | tf_op jit(solution)/shard_map/while/body/eval_jaxpr/ppermute | solution.py:28
  286.2 4.0 copy-start.15
  286.2 11.9 %collective-permute-start.7 = (bf16[256,4,128]{2,0,1:T(8,128)(2,1)}, bf16[256,4,128]{2,0,1:T(8,128)(2,1)S(1)}, u32[]{:S(2)}, u32[]{:S(2)}) collective-permute-start(bf16[256,4,128]{2,0,1:T(8,128)(2,1)} %get-tuple-element.607), channel_id=1, source_target_pairs={{0,244},{4,248},{8,252},{12,0},{16,4},{20,8},{24,12},{28,16},{32,2... | collective-permute-start | bytes 786440 | tf_op jit(solution)/shard_map/ppermute | solution.py:28
  290.2 186.8 %collective-permute-start.6 = (bf16[256,4,128]{2,0,1:T(8,128)(2,1)S(1)}, bf16[256,4,128]{2,0,1:T(8,128)(2,1)S(1)}, u32[]{:S(2)}, u32[]{:S(2)}) collective-permute-start(bf16[256,4,128]{2,0,1:T(8,128)(2,1)S(1)} %copy-done.15), channel_id=1, source_target_pairs={{0,244},{4,248},{8,252},{12,0},{16,4},{20,8},{24,12},{28,16},{32,2... | collective-permute-start | bytes 786440 | tf_op jit(solution)/shard_map/ppermute | solution.py:28
  (16 other events, 17.0 us)
Sparse Core Ops, SparseCore 0:
  11.5 177.1 all-reduce.6
  290.5 185.2 all-reduce.4
where the time goes:
time: 487 us; the launch traced here: 486 us
  waiting for transfers between devices  383 us (79%)
  starting transfers between devices  43.8 us (9%)
  matrix products  21.1 us (4%)
  local copies, waits for them, and re-layouts  19.4 us (4%)
  between operations  14.4 us (3%)
    psum x1, waiting for transfers between devices, on_device(): prompt_dk, prompt_dv = lax.psum((prompt_dk, prompt_dv), 'ctx')  178 us
    psum x1, waiting for transfers between devices, from_root(): return lax.psum(kept, axis)  174 us
    ppermute x12, starting transfers between devices, passed_along(): return lax.ppermute(block, axis, route)  34.8 us
    ppermute x8, waiting for transfers between devices, shifted(): lax.ppermute(value, axis, [(i, (i + by) % length) for i in range(length)])  17.5 us
    ppermute x12, waiting for transfers between devices, passed_along(): return lax.ppermute(block, axis, route)  13.5 us
    unnamed x51, local copies, waits for them, and re-layouts  12.9 us
  transfers between devices with their start and end apart: 22, of which 19 were waited for; matrix products, arithmetic and copies ran while one was open for 4% of the time, Pallas kernels for 0%

commit v1 on v0

v1 whole, which is shorter than its diff:
```python
import math

import jax
import jax.numpy as jnp
from jax import lax
from jax.experimental import pallas as pl
from jax.experimental.pallas import tpu as pltpu
from jax.sharding import PartitionSpec as P

HD = 128
PROMPT = 64
TOK = 256
NCTX = 64
HEADS = 4
SCALE = 1.0 / math.sqrt(HD)
SCALE2 = SCALE * math.log2(math.e)
NEG = -1e30
FAR = 1 << 28
F32 = jnp.float32
BF16 = jnp.bfloat16
VMEM_LIMIT = 40 * 1024 * 1024


def mm_nt(a, b):
    return lax.dot_general(a, b, (((1,), (1,)), ((), ())), preferred_element_type=F32)


def mm_nn(a, b):
    return lax.dot_general(a, b, (((1,), (0,)), ((), ())), preferred_element_type=F32)


def head_cols(h):
    return pl.ds(h * HD, HD)


def column_of(row):
    return jnp.transpose(jnp.broadcast_to(row, (128, TOK)))[:, :1]


def key_tile(base, width):
    return base + lax.broadcasted_iota(jnp.int32, (1, width), 1)


def query_mask(own, lo_col, q_col, d):
    k_row = key_tile((own - d) * TOK, TOK)
    ok = k_row >= lo_col
    if d == 0:
        ok = ok & (k_row <= q_col)
    return ok


def pick(first, a, b):
    return jnp.where(first, a, b)


def forward_kernel(info, lo_ref, q, do, k0, v0, kv1a, kv1b, kv2, kv3, kvp, att, cols, rows, pgrad):
    own = info[0]
    core0 = info[1] == 0
    lo_col = column_of(lo_ref[0:1, :].astype(F32)).astype(jnp.int32)
    q_col = own * TOK + lax.broadcasted_iota(jnp.int32, (TOK, 1), 0)
    masks = [query_mask(own, lo_col, q_col, d) for d in range(4)]
    masks.append(key_tile(0, PROMPT) <= q_col)
    lane = lax.broadcasted_iota(jnp.int32, (TOK, 128), 1)
    packed = jnp.zeros((TOK, 128), F32)
    for h in range(HEADS):
        c = head_cols(h)
        qh = q[:, c]
        doh = do[:, c]
        keys = [
            k0[:, c],
            pick(core0, kv1a[:TOK, c], kv1b[:TOK, c]),
            kv2[:TOK, c],
            kv3[:TOK, c],
            kvp[:PROMPT, c],
        ]
        vals = [
            v0[:, c],
            pick(core0, kv1a[TOK:, c], kv1b[TOK:, c]),
            kv2[TOK:, c],
            kv3[TOK:, c],
            kvp[PROMPT:, c],
        ]
        scores = [jnp.where(ok, mm_nt(qh, kk) * SCALE2, NEG) for ok, kk in zip(masks, keys)]
        top = jnp.max(scores[4], axis=1, keepdims=True)
        for s in scores[:4]:
            top = jnp.maximum(top, jnp.max(s, axis=1, keepdims=True))
        total = jnp.zeros((TOK, 1), F32)
        acc = jnp.zeros((TOK, HD), F32)
        for s, vv in zip(scores, vals):
            p = jnp.exp2(s - top)
            total = total + jnp.sum(p, axis=1, keepdims=True)
            acc = acc + mm_nn(p.astype(BF16), vv)
        out = acc / total
        att[:, c] = out
        delta = jnp.sum(out * doh.astype(F32), axis=1, keepdims=True)
        packed = jnp.where(lane == h, top + jnp.log2(total), packed)
        packed = jnp.where(lane == HEADS + h, delta, packed)
    cols[...] = packed
    turned = jnp.transpose(packed)[:8, :]
    rows[...] = turned
    u_col = lax.broadcasted_iota(jnp.int32, (PROMPT, 1), 0)
    q_row = key_tile(own * TOK, TOK)
    ok = u_col <= q_row
    for h in range(HEADS):
        c = head_cols(h)
        dk, dv = key_side(
            kvp[:PROMPT, c], kvp[PROMPT:, c], q[:, c], do[:, c], turned[h : h + 1], turned[HEADS + h : HEADS + h + 1], ok
        )
        pgrad[:PROMPT, c] = (dk * SCALE).astype(BF16)
        pgrad[PROMPT:, c] = dv.astype(BF16)


def key_side(kk, vv, qq, dd, lse_row, delta_row, ok):
    s = mm_nt(kk, qq) * SCALE2
    p = jnp.where(ok, jnp.exp2(s - lse_row), 0.0)
    dv = mm_nn(p.astype(BF16), dd)
    ds = (p * (mm_nt(vv, dd) - delta_row)).astype(BF16)
    return mm_nn(ds, qq), dv


def query_grad_kernel(info, lo_ref, cols, q, do, k0, v0, kv1a, kv1b, kv2, kv3, kvp, dq):
    own = info[0]
    core0 = info[1] == 0
    lo_col = column_of(lo_ref[0:1, :].astype(F32)).astype(jnp.int32)
    q_col = own * TOK + lax.broadcasted_iota(jnp.int32, (TOK, 1), 0)
    masks = [query_mask(own, lo_col, q_col, d) for d in range(4)]
    masks.append(key_tile(0, PROMPT) <= q_col)
    for h in range(HEADS):
        c = head_cols(h)
        qh = q[:, c]
        doh = do[:, c]
        keys = [
            k0[:, c],
            pick(core0, kv1a[:TOK, c], kv1b[:TOK, c]),
            kv2[:TOK, c],
            kv3[:TOK, c],
            kvp[:PROMPT, c],
        ]
        vals = [
            v0[:, c],
            pick(core0, kv1a[TOK:, c], kv1b[TOK:, c]),
            kv2[TOK:, c],
            kv3[TOK:, c],
            kvp[PROMPT:, c],
        ]
        lse = cols[:, h : h + 1]
        delta = cols[:, HEADS + h : HEADS + h + 1]
        acc = jnp.zeros((TOK, HD), F32)
        for ok, kk, vv in zip(masks, keys, vals):
            p = jnp.where(ok, jnp.exp2(mm_nt(qh, kk) * SCALE2 - lse), 0.0)
            ds = (p * (mm_nt(doh, vv) - delta)).astype(BF16)
            acc = acc + mm_nn(ds, kk)
        dq[:, c] = acc * SCALE


def key_grad_kernel(info, lo_ref, r0, r1, r2, r3, k, v, q0, do0, qd1a, qd1b, qd2, qd3, dk, dv):
    own = info[0]
    core0 = info[1] == 0
    k_col = own * TOK + lax.broadcasted_iota(jnp.int32, (TOK, 1), 0)
    masks = []
    for d in range(4):
        ok = k_col >= lo_ref[d : d + 1, :]
        if d == 0:
            ok = ok & (k_col <= key_tile(own * TOK, TOK))
        masks.append(ok)
    for h in range(HEADS):
        c = head_cols(h)
        qs = [q0[:, c], pick(core0, qd1a[:TOK, c], qd1b[:TOK, c]), qd2[:TOK, c], qd3[:TOK, c]]
        ds = [do0[:, c], pick(core0, qd1a[TOK:, c], qd1b[TOK:, c]), qd2[TOK:, c], qd3[TOK:, c]]
        dk_acc = jnp.zeros((TOK, HD), F32)
        dv_acc = jnp.zeros((TOK, HD), F32)
        for d, r in enumerate((r0, r1, r2, r3)):
            a, b = key_side(
                k[:, c], v[:, c], qs[d], ds[d], r[h : h + 1, :], r[HEADS + h : HEADS + h + 1, :], masks[d]
            )
            dk_acc = dk_acc + a
            dv_acc = dv_acc + b
        dk[:, c] = dk_acc * SCALE
        dv[:, c] = dv_acc


def finish_kernel(info, dk_in, dv_in, pk, pv, dk, dv):
    first = info[0] == 0
    dk[...] = dk_in[...] + jnp.where(first, pk[...], 0.0)
    dv[...] = dv_in[...] + jnp.where(first, pv[...], 0.0)


def call(kernel, outs, scalars, flops, *args):
    smem = pl.BlockSpec(memory_space=pltpu.SMEM)
    vmem = pl.BlockSpec(memory_space=pltpu.VMEM)
    return pl.pallas_call(
        kernel,
        out_shape=[jax.ShapeDtypeStruct(s, t) for s, t in outs],
        in_specs=[smem] * scalars + [vmem] * (len(args) - scalars),
        out_specs=[vmem] * len(outs),
        compiler_params=pltpu.CompilerParams(vmem_limit_bytes=VMEM_LIMIT),
        cost_estimate=pl.CostEstimate(flops=flops, bytes_accessed=4 << 20, transcendentals=1 << 20),
    )(*args)


def shift(x, by):
    return lax.ppermute(x, "ctx", [(i, (i + by) % NCTX) for i in range(NCTX)])


def swap(x):
    return lax.ppermute(x, "ctx", [(i, i ^ 1) for i in range(NCTX)])


def at(y, z, c):
    return (y * 8 + z) * 2 + c


Z_ORDER = (4, 5, 3, 6, 2, 7, 1)


def spread_prompt(mine, own):
    held = jnp.where(own == 0, mine, 0).astype(BF16)
    got = [lax.ppermute(held, "ctx", [(0, at(0, z, 0))]) for z in Z_ORDER]
    held = sum(got, held)
    got = [
        lax.ppermute(held, "ctx", [(at(0, z, 0), at(y, z, 0)) for z in range(8)]) for y in (2, 3, 1)
    ]
    held = sum(got, held)
    return jnp.where(own % 2 == 0, held, swap(held))


def gather_prompt(pgrad, own):
    core0 = own % 2 == 0
    dk, dv = pgrad[:PROMPT], pgrad[PROMPT:]
    other = swap(jnp.where(core0, dv, dk))
    part = jnp.where(core0, dk, dv).astype(F32) + other.astype(F32)
    sent = part.astype(BF16)
    got = [
        lax.ppermute(sent, "ctx", [(at(y, z, c), at(y, 0, c)) for y in range(4) for c in range(2)])
        for z in Z_ORDER
    ]
    part = sum([g.astype(F32) for g in got], part)
    sent = part.astype(BF16)
    got = [lax.ppermute(sent, "ctx", [(at(y, 0, c), at(0, 0, c)) for c in range(2)]) for y in (2, 3, 1)]
    part = sum([g.astype(F32) for g in got], part)
    other = swap(part.astype(BF16)).astype(F32)
    return part, other


def on_device(q, k, v, do, doc_lengths):
    own = lax.axis_index("ctx")
    core0 = own % 2 == 0
    info = jnp.stack([own, own % 2]).astype(jnp.int32)
    ends = jnp.cumsum(doc_lengths).astype(jnp.int32)
    blocks = own + jnp.arange(8, dtype=jnp.int32)
    pos = blocks[:, None] * TOK + jnp.arange(TOK, dtype=jnp.int32)[None, :]
    starts = jnp.max(jnp.where(ends[:, None, None] <= pos[None], ends[:, None, None], 0), axis=0)
    lo = jnp.where(blocks[:, None] < NCTX, jnp.maximum(starts, PROMPT), FAR)

    kv = jnp.concatenate([k, v], axis=0)
    qd = jnp.concatenate([q, do], axis=0)
    kv2 = shift(kv, 2)
    qd2 = shift(qd, -2)
    first = swap(jnp.where(core0, kv, qd))
    kvp = spread_prompt(jnp.concatenate([k[:PROMPT], v[:PROMPT]], axis=0), own)
    second = swap(jnp.where(core0, qd2, kv2))
    kv3 = shift(kv2, 1)
    qd3 = shift(qd2, -1)

    tok = (TOK, HEADS * HD)
    att, cols, rows, pgrad = call(
        forward_kernel,
        [(tok, F32), ((TOK, 128), F32), ((8, TOK), F32), ((2 * PROMPT, HEADS * HD), BF16)],
        1,
        600_000_000,
        info, lo, q, do, k, v, second, first, kv2, kv3, kvp,
    )
    r1, r2, r3 = shift(rows, -1), shift(rows, -2), shift(rows, -3)
    part, other = gather_prompt(pgrad, own)
    (dq,) = call(
        query_grad_kernel, [(tok, F32)], 1, 850_000_000,
        info, lo, cols, q, do, k, v, second, first, kv2, kv3, kvp,
    )
    dk, dv = call(
        key_grad_kernel, [(tok, F32), (tok, F32)], 1, 1_100_000_000,
        info, lo, rows, r1, r2, r3, k, v, q, do, first, second, qd2, qd3,
    )
    head_block = pl.BlockSpec((PROMPT, HEADS * HD), lambda i: (0, 0))
    dk, dv = pl.pallas_call(
        finish_kernel,
        grid=(1,),
        out_shape=[jax.ShapeDtypeStruct(tok, F32)] * 2,
        in_specs=[pl.BlockSpec(memory_space=pltpu.SMEM)] + [head_block] * 4,
        out_specs=[head_block] * 2,
        input_output_aliases={1: 0, 2: 1},
    )(info, dk, dv, part, other)
    return att, dq, dk, dv


def solution(mesh):
    spec = P("ctx", "head")
    return jax.shard_map(
        on_device, mesh=mesh, in_specs=(spec,) * 4 + (P(),), out_specs=(spec,) * 4, check_vma=False
    )
```

time: 487 us -> 95.3 us (0.20)
  waiting for transfers between devices: 383 us -> 11.9 us
  matrix products: 21.1 us -> 0 us
  Pallas kernels: 0 us -> 15.8 us
  local copies, waits for them, and re-layouts: 19.4 us -> 4.45 us
  between operations: 14.4 us -> 0.99 us
  starting transfers between devices: 43.8 us -> 55.3 us
    psum x2 -> x0, waiting for transfers between devices: 351 us -> none  [the longest x1 178 us: on_device(): prompt_dk, prompt_dv = lax.psum((prompt_dk, prompt_dv), 'ctx')]
    dot_general x33 -> x0, matrix products: 21.1 us -> none  [the longest x5 5.03 us: grad_scored(): jnp.einsum('htu,thd->uhd', rounded, dout_rows, preferred_element_type=jnp...]
    ppermute x20 -> x32, waiting for transfers between devices: 31 us -> 11.9 us  [the longest x7 4.84 us: gather_prompt(): lax.ppermute(sent, 'ctx', [(at(y, z, c), at(y, 0, c)) for y in range(4) f...]
    pallas_call x0 -> x4, Pallas kernels: none -> 15.8 us  [the longest x3 13.9 us: call(): pl.pallas_call(kernel, out_shape=[jax.ShapeDtypeStruct(s, t) for s, t in...]
    ppermute x20 -> x32, starting transfers between devices: 43.8 us -> 55.3 us  [the longest x5 20.6 us: swap(): return lax.ppermute(x, 'ctx', [(i, i ^ 1) for i in range(NCTX)])]
    unnamed x51 -> x18, local copies, waits for them, and re-layouts: 12.9 us -> 3.48 us
  transfers between devices with their start and end apart: 22 -> 32, of which waited for: 19 -> 7; matrix products, arithmetic and copies ran while one was open for 4% -> 5% of each run, Pallas kernels for 0% -> 10%
where the time goes in v1:
time: 95.3 us; the launch traced here: 93.6 us
  starting transfers between devices  55.3 us (58%)
  Pallas kernels  15.8 us (17%)
  waiting for transfers between devices  11.9 us (12%)
  other arithmetic  5.17 us (5%)
  local copies, waits for them, and re-layouts  4.45 us (5%)
  between operations  0.99 us (1%)
    ppermute x5, starting transfers between devices, swap(): return lax.ppermute(x, 'ctx', [(i, i ^ 1) for i in range(NCTX)])  20.6 us
    pallas_call x3, Pallas kernels, call(): pl.pallas_call(kernel, out_shape=[jax.ShapeDtypeStruct(s, t) for s, t in...  13.9 us
    ppermute x7, starting transfers between devices, shift(): return lax.ppermute(x, 'ctx', [(i, (i + by) % NCTX) for i in range(NCTX)])  11.8 us
    ppermute x7, starting transfers between devices, gather_prompt(): lax.ppermute(sent, 'ctx', [(at(y, z, c), at(y, 0, c)) for y in range(4) f...  9.04 us
    ppermute x7, starting transfers between devices, spread_prompt(): got = [lax.ppermute(held, 'ctx', [(0, at(0, z, 0))]) for z in Z_ORDER]  6.63 us
    ppermute x7, waiting for transfers between devices, gather_prompt(): lax.ppermute(sent, 'ctx', [(at(y, z, c), at(y, 0, c)) for y in range(4) f...  4.84 us
    ppermute x7, waiting for transfers between devices, shift(): return lax.ppermute(x, 'ctx', [(i, (i + by) % NCTX) for i in range(NCTX)])  4.61 us
    ppermute x3, starting transfers between devices, gather_prompt(): lax.ppermute(sent, 'ctx', [(at(y, 0, c), at(0, 0, c)) for c in range(2)])  4.06 us
  transfers between devices with their start and end apart: 32, of which 7 were waited for; matrix products, arithmetic and copies ran while one was open for 5% of the time, Pallas kernels for 10%

profile of v1, /device:TPU:1, one launch (start us, length us, event | category | flops | bytes accessed | tf_op | source)
XLA Modules:
  0.0 93.6 jit_solution(5097933038136162691)
XLA Ops:
  2.9 1.3 %collective-permute-start.9 = (bf16[128,512]{1,0:T(8,128)(2,1)S(1)}, bf16[128,512]{1,0:T(8,128)(2,1)}, u32[]{:S(2)}, u32[]{:S(2)}) collective-permute-start(bf16[128,512]{1,0:T(8,128)(2,1)S(1)} %maximum_select_fusion), channel_id=1, source_target_pairs={{0,16},{1,17},{2,18},{3,19}} | collective-permute-start | bytes 393224 | tf_op jit(solution)/shard_map/ppermute | solution.py:218
  4.2 1.3 %collective-permute-start.8 = (bf16[128,512]{1,0:T(8,128)(2,1)S(1)}, bf16[128,512]{1,0:T(8,128)(2,1)}, u32[]{:S(2)}, u32[]{:S(2)}) collective-permute-start(bf16[128,512]{1,0:T(8,128)(2,1)S(1)} %maximum_select_fusion), channel_id=1, source_target_pairs={{0,48},{1,49},{2,50},{3,51}} | collective-permute-start | bytes 393224 | tf_op jit(solution)/shard_map/ppermute | solution.py:218
  5.5 1.3 %collective-permute-start.7 = (bf16[128,512]{1,0:T(8,128)(2,1)S(1)}, bf16[128,512]{1,0:T(8,128)(2,1)}, u32[]{:S(2)}, u32[]{:S(2)}) collective-permute-start(bf16[128,512]{1,0:T(8,128)(2,1)S(1)} %maximum_select_fusion), channel_id=1, source_target_pairs={{0,24},{1,25},{2,26},{3,27}} | collective-permute-start | bytes 393224 | tf_op jit(solution)/shard_map/ppermute | solution.py:218
  12.0 8.9 %collective-permute-start = (bf16[512,512]{1,0:T(8,128)(2,1)S(1)}, bf16[512,512]{1,0:T(8,128)(2,1)S(1)}, u32[]{:S(2)}, u32[]{:S(2)}) collective-permute-start(bf16[512,512]{1,0:T(8,128)(2,1)S(1)} %constant_dynamic-update-slice_fusion), channel_id=1, source_target_pairs={{0,248},{4,252},{8,0},{12,4},{16,8},{20,12},{24,16},{28,20},{32,24... | collective-permute-start | bytes 1572872 | tf_op jit(solution)/shard_map/ppermute | solution.py:202
  22.9 1.3 %collective-permute-start.13 = (bf16[128,512]{1,0:T(8,128)(2,1)S(1)}, bf16[128,512]{1,0:T(8,128)(2,1)}, u32[]{:S(2)}, u32[]{:S(2)}) collective-permute-start(bf16[128,512]{1,0:T(8,128)(2,1)S(1)} %add_add_fusion.1), channel_id=1, source_target_pairs={{0,192},{8,200},{16,208},{24,216},{32,224},{40,232},{48,240},{56,2... | collective-permute-start | bytes 393224 | tf_op jit(solution)/shard_map/ppermute | solution.py:221
  24.2 1.3 %collective-permute-start.12 = (bf16[128,512]{1,0:T(8,128)(2,1)S(1)}, bf16[128,512]{1,0:T(8,128)(2,1)}, u32[]{:S(2)}, u32[]{:S(2)}) collective-permute-start(bf16[128,512]{1,0:T(8,128)(2,1)S(1)} %add_add_fusion.1), channel_id=1, source_target_pairs={{0,128},{8,136},{16,144},{24,152},{32,160},{40,168},{48,176},{56,1... | collective-permute-start | bytes 393224 | tf_op jit(solution)/shard_map/ppermute | solution.py:221
  26.6 8.7 %collective-permute-start.3 = (bf16[512,512]{1,0:T(8,128)(2,1)}, bf16[512,512]{1,0:T(8,128)(2,1)S(1)}, u32[]{:S(2)}, u32[]{:S(2)}) collective-permute-start(bf16[512,512]{1,0:T(8,128)(2,1)} %broadcast_select_fusion), channel_id=1, source_target_pairs={{0,4},{4,0},{8,12},{12,8},{16,20},{20,16},{24,28},{28,24},{32,36},... | collective-permute-start | bytes 1572872 | tf_op jit(solution)/shard_map/ppermute | solution.py:206
  36.3 1.5 %collective-permute-start.15 = (bf16[128,512]{1,0:T(8,128)(2,1)S(1)}, bf16[128,512]{1,0:T(8,128)(2,1)S(1)}, u32[]{:S(2)}, u32[]{:S(2)}) collective-permute-start(bf16[128,512]{1,0:T(8,128)(2,1)S(1)} %add_add_fusion), channel_id=1, source_target_pairs={{0,4},{4,0},{8,12},{12,8},{16,20},{20,16},{24,28},{28,24},{32,36},... | collective-permute-start | bytes 393224 | tf_op jit(solution)/shard_map/ppermute | solution.py:206
  38.9 1.4 %collective-permute-done.2.kv1a.qd1b = bf16[512,512]{1,0:T(8,128)(2,1)S(1)} collective-permute-done((bf16[512,512]{1,0:T(8,128)(2,1)S(1)}, bf16[512,512]{1,0:T(8,128)(2,1)S(1)}, u32[]{:S(2)}, u32[]{:S(2)}) %collective-permute-start.2) | collective-permute-done | bytes 524320 | tf_op jit(solution)/shard_map/ppermute | solution.py:206
  40.3 4.6 %collective-permute-done.4.kv3 = bf16[512,512]{1,0:T(8,128)(2,1)S(1)} collective-permute-done((bf16[512,512]{1,0:T(8,128)(2,1)S(1)}, bf16[512,512]{1,0:T(8,128)(2,1)S(1)}, u32[]{:S(2)}, u32[]{:S(2)}) %collective-permute-start.4) | collective-permute-done | bytes 524320 | tf_op jit(solution)/shard_map/ppermute | solution.py:202
  44.9 5.0 %shard_map.84 = (f32[256,512]{1,0:T(8,128)}, f32[256,128]{1,0:T(8,128)S(1)}, f32[8,256]{1,0:T(8,128)S(1)}, bf16[128,512]{1,0:T(8,128)(2,1)S(1)}) custom-call(s32[2]{0:T(128)S(1)} %pad_add_fusion.info, s32[8,256]{1,0:T(8,128)S(1)} %maximum_select_fusion.1.lo_ref, bf16[256,512]{1,0:T(8,128)(2,1)S(1)} %copy-done.2, bf16[256,512]{1,0:T(8,128)(2,1)S(1)} %copy-done.3, ...), custom_call_target="tpu_custom_call" | custom-call | flops 600000000 | bytes 4194304 | tf_op jit(solution)/shard_map/pallas_call | solution.py:191
  49.9 6.0 %collective-permute-start.20 = (bf16[64,512]{1,0:T(8,128)(2,1)S(1)}, bf16[64,512]{1,0:T(8,128)(2,1)S(1)}, u32[]{:S(2)}, u32[]{:S(2)}) collective-permute-start(bf16[64,512]{1,0:T(8,128)(2,1)S(1)} %broadcast_select_fusion.3), channel_id=1, source_target_pairs={{0,4},{4,0},{8,12},{12,8},{16,20},{20,16},{24,28},{28,24},{32,36},... | collective-permute-start | bytes 196616 | tf_op jit(solution)/shard_map/ppermute | solution.py:206
  56.8 1.3 %collective-permute-start.27 = (bf16[64,512]{1,0:T(8,128)(2,1)S(1)}, bf16[64,512]{1,0:T(8,128)(2,1)S(1)}, u32[]{:S(2)}, u32[]{:S(2)}) collective-permute-start(bf16[64,512]{1,0:T(8,128)(2,1)S(1)} %fusion), channel_id=1, source_target_pairs={{8,0},{12,4},{72,64},{76,68},{136,128},{140,132},{200,192},{204,19... | collective-permute-start | bytes 196616 | tf_op jit(solution)/shard_map/ppermute | solution.py:234
  58.1 1.3 %collective-permute-start.26 = (bf16[64,512]{1,0:T(8,128)(2,1)S(1)}, bf16[64,512]{1,0:T(8,128)(2,1)S(1)}, u32[]{:S(2)}, u32[]{:S(2)}) collective-permute-start(bf16[64,512]{1,0:T(8,128)(2,1)S(1)} %fusion), channel_id=1, source_target_pairs={{56,0},{60,4},{120,64},{124,68},{184,128},{188,132},{248,192},{252... | collective-permute-start | bytes 196616 | tf_op jit(solution)/shard_map/ppermute | solution.py:234
  59.4 1.3 %collective-permute-start.25 = (bf16[64,512]{1,0:T(8,128)(2,1)S(1)}, bf16[64,512]{1,0:T(8,128)(2,1)S(1)}, u32[]{:S(2)}, u32[]{:S(2)}) collective-permute-start(bf16[64,512]{1,0:T(8,128)(2,1)S(1)} %fusion), channel_id=1, source_target_pairs={{16,0},{20,4},{80,64},{84,68},{144,128},{148,132},{208,192},{212,1... | collective-permute-start | bytes 196616 | tf_op jit(solution)/shard_map/ppermute | solution.py:234
  60.7 1.3 %collective-permute-start.24 = (bf16[64,512]{1,0:T(8,128)(2,1)S(1)}, bf16[64,512]{1,0:T(8,128)(2,1)S(1)}, u32[]{:S(2)}, u32[]{:S(2)}) collective-permute-start(bf16[64,512]{1,0:T(8,128)(2,1)S(1)} %fusion), channel_id=1, source_target_pairs={{48,0},{52,4},{112,64},{116,68},{176,128},{180,132},{240,192},{244... | collective-permute-start | bytes 196616 | tf_op jit(solution)/shard_map/ppermute | solution.py:234
  67.8 1.5 %collective-permute-start.16 = (f32[8,256]{1,0:T(8,128)S(1)}, f32[8,256]{1,0:T(8,128)S(1)}, u32[]{:S(2)}, u32[]{:S(2)}) collective-permute-start(f32[8,256]{1,0:T(8,128)S(1)} %get-tuple-element.14.r0), channel_id=1, source_target_pairs={{0,252},{4,0},{8,4},{12,8},{16,12},{20,16},{24,20},{28,24},{32,28}... | collective-permute-start | bytes 24584 | tf_op jit(solution)/shard_map/ppermute | solution.py:202
  69.3 2.0 %collective-permute-done.22 = bf16[64,512]{1,0:T(8,128)(2,1)S(1)} collective-permute-done((bf16[64,512]{1,0:T(8,128)(2,1)S(1)}, bf16[64,512]{1,0:T(8,128)(2,1)S(1)}, u32[]{:S(2)}, u32[]{:S(2)}) %collective-permute-start.22) | collective-permute-done | bytes 65568 | tf_op jit(solution)/shard_map/ppermute | solution.py:234
  71.3 2.2 %collective-permute-done.21 = bf16[64,512]{1,0:T(8,128)(2,1)S(1)} collective-permute-done((bf16[64,512]{1,0:T(8,128)(2,1)S(1)}, bf16[64,512]{1,0:T(8,128)(2,1)S(1)}, u32[]{:S(2)}, u32[]{:S(2)}) %collective-permute-start.21) | collective-permute-done | bytes 65568 | tf_op jit(solution)/shard_map/ppermute | solution.py:234
  76.2 1.5 %collective-permute-start.28 = (bf16[64,512]{1,0:T(8,128)(2,1)S(1)}, bf16[64,512]{1,0:T(8,128)(2,1)S(1)}, u32[]{:S(2)}, u32[]{:S(2)}) collective-permute-start(bf16[64,512]{1,0:T(8,128)(2,1)S(1)} %get-tuple-element.22), channel_id=1, source_target_pairs={{128,0},{132,4},{129,1},{133,5},{130,2},{134,6},{131,3},{135,7}} | collective-permute-start | bytes 196616 | tf_op jit(solution)/shard_map/ppermute | solution.py:239
  77.7 4.8 %shard_map.85 = f32[256,512]{1,0:T(8,128)} custom-call(s32[2]{0:T(128)S(1)} %pad_add_fusion.info, s32[8,256]{1,0:T(8,128)S(1)} %maximum_select_fusion.1.lo_ref, f32[256,128]{1,0:T(8,128)S(1)} %get-tuple-element.13.cols, bf16[256,512]{1,0:T(8,128)(2,1)S(1)} %copy-done.2, bf16[256,512]{1,0:T(8,128)(2,1)S(1)} %copy-done.3, bf16[256,512]{1,0:T(8,128)(2,1)S(1)} %copy-done, ...), custom_call_target="tpu_custom_call" | custom-call | flops 850000000 | bytes 4194304 | tf_op jit(solution)/shard_map/pallas_call | solution.py:191
  83.4 3.5 %collective-permute-start.31 = (bf16[64,512]{1,0:T(8,128)(2,1)S(1)}, bf16[64,512]{1,0:T(8,128)(2,1)S(1)}, u32[]{:S(2)}, u32[]{:S(2)}) collective-permute-start(bf16[64,512]{1,0:T(8,128)(2,1)S(1)} %get-tuple-element.20), channel_id=1, source_target_pairs={{0,4},{4,0},{8,12},{12,8},{16,20},{20,16},{24,28},{28,24},{32,36},... | collective-permute-start | bytes 196616 | tf_op jit(solution)/shard_map/ppermute | solution.py:206
  86.9 4.2 %shard_map.86 = (f32[256,512]{1,0:T(8,128)}, f32[256,512]{1,0:T(8,128)}) custom-call(s32[2]{0:T(128)S(1)} %pad_add_fusion.info, s32[8,256]{1,0:T(8,128)S(1)} %maximum_select_fusion.1.lo_ref, f32[8,256]{1,0:T(8,128)S(1)} %get-tuple-element.14.r0, f32[8,256]{1,0:T(8,128)S(1)} %collective-permute-done.16.r1, f32[8,256]{1,0:T(8,128)S(1)} %collective-permute-done.17.r2, ...), custom_call_target="tpu_custom_call" | custom-call | flops 1100000000 | bytes 4194304 | tf_op jit(solution)/shard_map/pallas_call | solution.py:191
  91.8 1.8 %shard_map.87 = (f32[256,512]{1,0:T(8,128)}, f32[256,512]{1,0:T(8,128)}) custom-call(s32[2]{0:T(128)} %copy-done.4, f32[256,512]{1,0:T(8,128)} %get-tuple-element.15.dk_in, f32[256,512]{1,0:T(8,128)} %get-tuple-element.16.dv_in, f32[64,512]{1,0:T(8,128)} %get-tuple-element.21.pk, ...), custom_call_target="tpu_custom_call", output_to_operand_aliasing={{0}: (1, {}), {1}: (2, {})} | custom-call | tf_op jit(solution)/shard_map/pallas_call | solution.py:284
  (88 shorter events, 23.4 us)
Async XLA Ops:
  1.5 9.0 %collective-permute-start.11 = (bf16[128,512]{1,0:T(8,128)(2,1)S(1)}, bf16[128,512]{1,0:T(8,128)(2,1)S(1)}, u32[]{:S(2)}, u32[]{:S(2)}) collective-permute-start(bf16[128,512]{1,0:T(8,128)(2,1)S(1)} %maximum_select_fusion), channel_id=1, source_target_pairs={{0,8},{1,9},{2,10},{3,11}} | collective-permute-start | bytes 393224 | tf_op jit(solution)/shard_map/ppermute | solution.py:218
  2.2 9.1 %collective-permute-start.10 = (bf16[128,512]{1,0:T(8,128)(2,1)S(1)}, bf16[128,512]{1,0:T(8,128)(2,1)S(1)}, u32[]{:S(2)}, u32[]{:S(2)}) collective-permute-start(bf16[128,512]{1,0:T(8,128)(2,1)S(1)} %maximum_select_fusion), channel_id=1, source_target_pairs={{0,56},{1,57},{2,58},{3,59}} | collective-permute-start | bytes 393224 | tf_op jit(solution)/shard_map/ppermute | solution.py:218
  2.9 9.2 %collective-permute-start.9 = (bf16[128,512]{1,0:T(8,128)(2,1)S(1)}, bf16[128,512]{1,0:T(8,128)(2,1)}, u32[]{:S(2)}, u32[]{:S(2)}) collective-permute-start(bf16[128,512]{1,0:T(8,128)(2,1)S(1)} %maximum_select_fusion), channel_id=1, source_target_pairs={{0,16},{1,17},{2,18},{3,19}} | collective-permute-start | bytes 393224 | tf_op jit(solution)/shard_map/ppermute | solution.py:218
  4.2 16.7 %collective-permute-start.8 = (bf16[128,512]{1,0:T(8,128)(2,1)S(1)}, bf16[128,512]{1,0:T(8,128)(2,1)}, u32[]{:S(2)}, u32[]{:S(2)}) collective-permute-start(bf16[128,512]{1,0:T(8,128)(2,1)S(1)} %maximum_select_fusion), channel_id=1, source_target_pairs={{0,48},{1,49},{2,50},{3,51}} | collective-permute-start | bytes 393224 | tf_op jit(solution)/shard_map/ppermute | solution.py:218
  5.5 15.4 %collective-permute-start.7 = (bf16[128,512]{1,0:T(8,128)(2,1)S(1)}, bf16[128,512]{1,0:T(8,128)(2,1)}, u32[]{:S(2)}, u32[]{:S(2)}) collective-permute-start(bf16[128,512]{1,0:T(8,128)(2,1)S(1)} %maximum_select_fusion), channel_id=1, source_target_pairs={{0,24},{1,25},{2,26},{3,27}} | collective-permute-start | bytes 393224 | tf_op jit(solution)/shard_map/ppermute | solution.py:218
  10.6 10.4 %collective-permute-start.6 = (bf16[128,512]{1,0:T(8,128)(2,1)S(1)}, bf16[128,512]{1,0:T(8,128)(2,1)S(1)}, u32[]{:S(2)}, u32[]{:S(2)}) collective-permute-start(bf16[128,512]{1,0:T(8,128)(2,1)S(1)} %maximum_select_fusion), channel_id=1, source_target_pairs={{0,40},{1,41},{2,42},{3,43}} | collective-permute-start | bytes 393224 | tf_op jit(solution)/shard_map/ppermute | solution.py:218
  11.3 9.7 %collective-permute-start.5 = (bf16[128,512]{1,0:T(8,128)(2,1)S(1)}, bf16[128,512]{1,0:T(8,128)(2,1)S(1)}, u32[]{:S(2)}, u32[]{:S(2)}) collective-permute-start(bf16[128,512]{1,0:T(8,128)(2,1)S(1)} %maximum_select_fusion), channel_id=1, source_target_pairs={{0,32},{1,33},{2,34},{3,35}} | collective-permute-start | bytes 393224 | tf_op jit(solution)/shard_map/ppermute | solution.py:218
  12.0 25.8 %collective-permute-start = (bf16[512,512]{1,0:T(8,128)(2,1)S(1)}, bf16[512,512]{1,0:T(8,128)(2,1)S(1)}, u32[]{:S(2)}, u32[]{:S(2)}) collective-permute-start(bf16[512,512]{1,0:T(8,128)(2,1)S(1)} %constant_dynamic-update-slice_fusion), channel_id=1, source_target_pairs={{0,248},{4,252},{8,0},{12,4},{16,8},{20,12},{24,16},{28,20},{32,24... | collective-permute-start | bytes 1572872 | tf_op jit(solution)/shard_map/ppermute | solution.py:202
  20.9 16.9 %collective-permute-start.1 = (bf16[512,512]{1,0:T(8,128)(2,1)S(1)}, bf16[512,512]{1,0:T(8,128)(2,1)S(1)}, u32[]{:S(2)}, u32[]{:S(2)}) collective-permute-start(bf16[512,512]{1,0:T(8,128)(2,1)S(1)} %constant_dynamic-update-slice_fusion.2), channel_id=1, source_target_pairs={{0,8},{4,12},{8,16},{12,20},{16,24},{20,28},{24,32},{28,36},{32,40... | collective-permute-start | bytes 1572872 | tf_op jit(solution)/shard_map/ppermute | solution.py:202
  22.9 12.4 %collective-permute-start.13 = (bf16[128,512]{1,0:T(8,128)(2,1)S(1)}, bf16[128,512]{1,0:T(8,128)(2,1)}, u32[]{:S(2)}, u32[]{:S(2)}) collective-permute-start(bf16[128,512]{1,0:T(8,128)(2,1)S(1)} %add_add_fusion.1), channel_id=1, source_target_pairs={{0,192},{8,200},{16,208},{24,216},{32,224},{40,232},{48,240},{56,2... | collective-permute-start | bytes 393224 | tf_op jit(solution)/shard_map/ppermute | solution.py:221
  24.2 11.1 %collective-permute-start.12 = (bf16[128,512]{1,0:T(8,128)(2,1)S(1)}, bf16[128,512]{1,0:T(8,128)(2,1)}, u32[]{:S(2)}, u32[]{:S(2)}) collective-permute-start(bf16[128,512]{1,0:T(8,128)(2,1)S(1)} %add_add_fusion.1), channel_id=1, source_target_pairs={{0,128},{8,136},{16,144},{24,152},{32,160},{40,168},{48,176},{56,1... | collective-permute-start | bytes 393224 | tf_op jit(solution)/shard_map/ppermute | solution.py:221
  26.6 12.3 %collective-permute-start.3 = (bf16[512,512]{1,0:T(8,128)(2,1)}, bf16[512,512]{1,0:T(8,128)(2,1)S(1)}, u32[]{:S(2)}, u32[]{:S(2)}) collective-permute-start(bf16[512,512]{1,0:T(8,128)(2,1)} %broadcast_select_fusion), channel_id=1, source_target_pairs={{0,4},{4,0},{8,12},{12,8},{16,20},{20,16},{24,28},{28,24},{32,36},... | collective-permute-start | bytes 1572872 | tf_op jit(solution)/shard_map/ppermute | solution.py:206
  49.9 6.9 %collective-permute-start.20 = (bf16[64,512]{1,0:T(8,128)(2,1)S(1)}, bf16[64,512]{1,0:T(8,128)(2,1)S(1)}, u32[]{:S(2)}, u32[]{:S(2)}) collective-permute-start(bf16[64,512]{1,0:T(8,128)(2,1)S(1)} %broadcast_select_fusion.3), channel_id=1, source_target_pairs={{0,4},{4,0},{8,12},{12,8},{16,20},{20,16},{24,28},{28,24},{32,36},... | collective-permute-start | bytes 196616 | tf_op jit(solution)/shard_map/ppermute | solution.py:206
  59.4 6.5 %collective-permute-start.25 = (bf16[64,512]{1,0:T(8,128)(2,1)S(1)}, bf16[64,512]{1,0:T(8,128)(2,1)S(1)}, u32[]{:S(2)}, u32[]{:S(2)}) collective-permute-start(bf16[64,512]{1,0:T(8,128)(2,1)S(1)} %fusion), channel_id=1, source_target_pairs={{16,0},{20,4},{80,64},{84,68},{144,128},{148,132},{208,192},{212,1... | collective-permute-start | bytes 196616 | tf_op jit(solution)/shard_map/ppermute | solution.py:234
  60.7 7.1 %collective-permute-start.24 = (bf16[64,512]{1,0:T(8,128)(2,1)S(1)}, bf16[64,512]{1,0:T(8,128)(2,1)S(1)}, u32[]{:S(2)}, u32[]{:S(2)}) collective-permute-start(bf16[64,512]{1,0:T(8,128)(2,1)S(1)} %fusion), channel_id=1, source_target_pairs={{48,0},{52,4},{112,64},{116,68},{176,128},{180,132},{240,192},{244... | collective-permute-start | bytes 196616 | tf_op jit(solution)/shard_map/ppermute | solution.py:234
  62.0 7.3 %collective-permute-start.23 = (bf16[64,512]{1,0:T(8,128)(2,1)S(1)}, bf16[64,512]{1,0:T(8,128)(2,1)S(1)}, u32[]{:S(2)}, u32[]{:S(2)}) collective-permute-start(bf16[64,512]{1,0:T(8,128)(2,1)S(1)} %fusion), channel_id=1, source_target_pairs={{24,0},{28,4},{88,64},{92,68},{152,128},{156,132},{216,192},{220,1... | collective-permute-start | bytes 196616 | tf_op jit(solution)/shard_map/ppermute | solution.py:234
  63.3 8.0 %collective-permute-start.22 = (bf16[64,512]{1,0:T(8,128)(2,1)S(1)}, bf16[64,512]{1,0:T(8,128)(2,1)S(1)}, u32[]{:S(2)}, u32[]{:S(2)}) collective-permute-start(bf16[64,512]{1,0:T(8,128)(2,1)S(1)} %fusion), channel_id=1, source_target_pairs={{40,0},{44,4},{104,64},{108,68},{168,128},{172,132},{232,192},{236... | collective-permute-start | bytes 196616 | tf_op jit(solution)/shard_map/ppermute | solution.py:234
  64.6 8.9 %collective-permute-start.21 = (bf16[64,512]{1,0:T(8,128)(2,1)S(1)}, bf16[64,512]{1,0:T(8,128)(2,1)S(1)}, u32[]{:S(2)}, u32[]{:S(2)}) collective-permute-start(bf16[64,512]{1,0:T(8,128)(2,1)S(1)} %fusion), channel_id=1, source_target_pairs={{32,0},{36,4},{96,64},{100,68},{160,128},{164,132},{224,192},{228,... | collective-permute-start | bytes 196616 | tf_op jit(solution)/shard_map/ppermute | solution.py:234
  65.9 21.0 %collective-permute-start.19 = (bf16[512,512]{1,0:T(8,128)(2,1)S(1)}, bf16[512,512]{1,0:T(8,128)(2,1)S(1)}, u32[]{:S(2)}, u32[]{:S(2)}) collective-permute-start(bf16[512,512]{1,0:T(8,128)(2,1)S(1)} %collective-permute-done.qd2), channel_id=1, source_target_pairs={{0,252},{4,0},{8,4},{12,8},{16,12},{20,16},{24,20},{28,24},{32,28}... | collective-permute-start | bytes 1572872 | tf_op jit(solution)/shard_map/ppermute | solution.py:202
  67.8 19.1 %collective-permute-start.16 = (f32[8,256]{1,0:T(8,128)S(1)}, f32[8,256]{1,0:T(8,128)S(1)}, u32[]{:S(2)}, u32[]{:S(2)}) collective-permute-start(f32[8,256]{1,0:T(8,128)S(1)} %get-tuple-element.14.r0), channel_id=1, source_target_pairs={{0,252},{4,0},{8,4},{12,8},{16,12},{20,16},{24,20},{28,24},{32,28}... | collective-permute-start | bytes 24584 | tf_op jit(solution)/shard_map/ppermute | solution.py:202
  73.6 8.9 %collective-permute-start.30 = (bf16[64,512]{1,0:T(8,128)(2,1)S(1)}, bf16[64,512]{1,0:T(8,128)(2,1)S(1)}, u32[]{:S(2)}, u32[]{:S(2)}) collective-permute-start(bf16[64,512]{1,0:T(8,128)(2,1)S(1)} %get-tuple-element.22), channel_id=1, source_target_pairs={{64,0},{68,4},{65,1},{69,5},{66,2},{70,6},{67,3},{71,7}} | collective-permute-start | bytes 196616 | tf_op jit(solution)/shard_map/ppermute | solution.py:239
  74.9 7.6 %collective-permute-start.29 = (bf16[64,512]{1,0:T(8,128)(2,1)S(1)}, bf16[64,512]{1,0:T(8,128)(2,1)S(1)}, u32[]{:S(2)}, u32[]{:S(2)}) collective-permute-start(bf16[64,512]{1,0:T(8,128)(2,1)S(1)} %get-tuple-element.22), channel_id=1, source_target_pairs={{192,0},{196,4},{193,1},{197,5},{194,2},{198,6},{195,3},{199,7}} | collective-permute-start | bytes 196616 | tf_op jit(solution)/shard_map/ppermute | solution.py:239
  76.2 6.5 %collective-permute-start.28 = (bf16[64,512]{1,0:T(8,128)(2,1)S(1)}, bf16[64,512]{1,0:T(8,128)(2,1)S(1)}, u32[]{:S(2)}, u32[]{:S(2)}) collective-permute-start(bf16[64,512]{1,0:T(8,128)(2,1)S(1)} %get-tuple-element.22), channel_id=1, source_target_pairs={{128,0},{132,4},{129,1},{133,5},{130,2},{134,6},{131,3},{135,7}} | collective-permute-start | bytes 196616 | tf_op jit(solution)/shard_map/ppermute | solution.py:239
  83.4 7.7 %collective-permute-start.31 = (bf16[64,512]{1,0:T(8,128)(2,1)S(1)}, bf16[64,512]{1,0:T(8,128)(2,1)S(1)}, u32[]{:S(2)}, u32[]{:S(2)}) collective-permute-start(bf16[64,512]{1,0:T(8,128)(2,1)S(1)} %get-tuple-element.20), channel_id=1, source_target_pairs={{0,4},{4,0},{8,12},{12,8},{16,20},{20,16},{24,28},{28,24},{32,36},... | collective-permute-start | bytes 196616 | tf_op jit(solution)/shard_map/ppermute | solution.py:206
  (18 other events, 107.9 us)

commit v2 on v1

v2 whole, which is shorter than its diff:
```python
import math

import jax
import jax.numpy as jnp
from jax import lax
from jax.experimental import pallas as pl
from jax.experimental.pallas import tpu as pltpu
from jax.sharding import PartitionSpec as P

HD = 128
PROMPT = 64
TOK = 256
NCTX = 64
HEADS = 4
WIDE = HEADS * HD
SCALE = 1.0 / math.sqrt(HD)
SCALE2 = SCALE * math.log2(math.e)
NEG = -1e30
FAR = 1 << 28
F32 = jnp.float32
BF16 = jnp.bfloat16
VMEM_LIMIT = 40 * 1024 * 1024
GATE_R = False
GATE_DQ = True
GATE_Y = True
GATE_DK = True
SPREAD_GATE = True
HALO_DONE = True
Y_FILL = True
Z_FILL = True
Y_STEPS_FILL = False


def mm_nt(a, b):
    return lax.dot_general(a, b, (((1,), (1,)), ((), ())), preferred_element_type=F32)


def mm_nn(a, b):
    return lax.dot_general(a, b, (((1,), (0,)), ((), ())), preferred_element_type=F32)


def mm_tn(a, b):
    return lax.dot_general(a, b, (((0,), (0,)), ((), ())), preferred_element_type=F32)


def head(h):
    return pl.ds(h * HD, HD)


def key_index(base, count):
    return base + lax.broadcasted_iota(jnp.int32, (count, TOK), 0)


def query_index(own):
    return own * TOK + lax.broadcasted_iota(jnp.int32, (1, TOK), 1)


def fold(state, qh, tiles):
    top, total, acc = state
    scores = [jnp.where(ok, mm_nt(kk, qh) * SCALE2, NEG) for ok, kk, _ in tiles]
    new_top = top
    for s in scores:
        new_top = jnp.maximum(new_top, jnp.max(s, axis=0, keepdims=True))
    fade = jnp.exp2(top - new_top)
    total = total * fade
    acc = acc * fade
    for s, (_, _, vv) in zip(scores, tiles):
        p = jnp.exp2(s - new_top)
        total = total + jnp.sum(p, axis=0, keepdims=True)
        acc = acc + mm_tn(vv, p.astype(BF16))
    return (new_top, total, acc), scores


def load_state(stat, acc, h):
    return stat[h : h + 1, :], stat[HEADS + h : HEADS + h + 1, :], acc[head(h), :]


def store_state(stat, acc, h, state):
    stat[h : h + 1, :], stat[HEADS + h : HEADS + h + 1, :], acc[head(h), :] = state


def pack_kernel(info, k, v, q, do, kv, qd, sel, kvp, sems):
    top, bottom = pl.ds(0, TOK), pl.ds(TOK, TOK)
    jobs = [(k, kv.at[top]), (v, kv.at[bottom]), (q, qd.at[top]), (do, qd.at[bottom])]
    copies = [pltpu.make_async_copy(a, b, sems.at[i]) for i, (a, b) in enumerate(jobs)]
    for copy in copies:
        copy.start()
    copies[0].wait()
    copies[1].wait()
    kvp[:PROMPT, :] = kv[:PROMPT, :]
    kvp[PROMPT:, :] = kv[pl.ds(TOK, PROMPT), :]
    copies[2].wait()
    copies[3].wait()
    sel[...] = jnp.where(info[1] == 0, kv[...], qd[...])


def own_kernel(info, lo_ref, q, k, v, do, stat, acc, do_t):
    own = info[0]
    k_pos = key_index(own * TOK, TOK)
    ok = (k_pos >= lo_ref[0:1, :]) & (k_pos <= query_index(own))
    for h in range(HEADS):
        c = head(h)
        start = (jnp.full((1, TOK), NEG, F32), jnp.zeros((1, TOK), F32), jnp.zeros((HD, TOK), F32))
        state, _ = fold(start, q[:, c], [(ok, k[:, c], v[:, c])])
        store_state(stat, acc, h, state)
        do_t[c, :] = jnp.transpose(do[:, c].astype(F32))


def near_kernel(info, lo_ref, stat_in, acc_in, q, kv1a, kv1b, kv2, stat, acc):
    own = info[0]
    core0 = info[1] == 0
    ok1 = key_index((own - 1) * TOK, TOK) >= lo_ref[0:1, :]
    ok2 = key_index((own - 2) * TOK, TOK) >= lo_ref[0:1, :]
    for h in range(HEADS):
        c = head(h)
        kk = jnp.where(core0, kv1a[:TOK, c], kv1b[:TOK, c])
        vv = jnp.where(core0, kv1a[TOK:, c], kv1b[TOK:, c])
        tiles = [(ok1, kk, vv), (ok2, kv2[:TOK, c], kv2[TOK:, c])]
        state, _ = fold(load_state(stat_in, acc_in, h), q[:, c], tiles)
        store_state(stat, acc, h, state)


def last_kernel(info, lo_ref, stat, acc, q, do, do_t, kv3, kvp, out_t, rows, pk, pv):
    own = info[0]
    ok3 = key_index((own - 3) * TOK, TOK) >= lo_ref[0:1, :]
    okp = key_index(0, PROMPT) <= query_index(own)
    dprobs = [mm_nt(kvp[PROMPT:, head(h)], do[:, head(h)]) for h in range(HEADS)]
    folded = []
    for h in range(HEADS):
        c = head(h)
        tiles = [(ok3, kv3[:TOK, c], kv3[TOK:, c]), (okp, kvp[:PROMPT, c], kvp[PROMPT:, c])]
        folded.append(fold(load_state(stat, acc, h), q[:, c], tiles))
    for h in range(HEADS):
        c = head(h)
        (top, total, done), scores = folded[h]
        out = done * (1.0 / total)
        lse = top + jnp.log2(total)
        delta = jnp.sum(out * do_t[c, :], axis=0, keepdims=True)
        out_t[c, :] = out
        rows[h : h + 1, :] = lse
        rows[HEADS + h : HEADS + h + 1, :] = delta
        p = jnp.exp2(scores[1] - lse)
        ds = (p * (dprobs[h] - delta)).astype(BF16)
        pv[:, c] = mm_nn(p.astype(BF16), do[:, c]).astype(BF16)
        pk[:, c] = (mm_nn(ds, q[:, c]) * SCALE).astype(BF16)


def grads(ok, kk, vv, qh, doh, lse, delta):
    p = jnp.where(ok, jnp.exp2(mm_nt(kk, qh) * SCALE2 - lse), 0.0)
    ds = p * (mm_nt(vv, doh) - delta)
    return p.astype(BF16), ds.astype(BF16)


def query_grad_kernel(
    info, lo_ref, rows, out_t, q, do, k, v, kv1a, kv1b, kv2, kv3, kvp, att, dq, dk, dv
):
    own = info[0]
    core0 = info[1] == 0
    k_pos = key_index(own * TOK, TOK)
    low = lo_ref[0:1, :]
    masks = [(k_pos >= low) & (k_pos <= query_index(own))]
    masks += [key_index((own - d) * TOK, TOK) >= low for d in (1, 2, 3)]
    masks.append(key_index(0, PROMPT) <= query_index(own))
    for h in range(HEADS):
        c = head(h)
        qh, doh = q[:, c], do[:, c]
        lse, delta = rows[h : h + 1, :], rows[HEADS + h : HEADS + h + 1, :]
        keys = [k[:, c], jnp.where(core0, kv1a[:TOK, c], kv1b[:TOK, c]), kv2[:TOK, c], kv3[:TOK, c]]
        vals = [v[:, c], jnp.where(core0, kv1a[TOK:, c], kv1b[TOK:, c]), kv2[TOK:, c], kv3[TOK:, c]]
        keys.append(kvp[:PROMPT, c])
        vals.append(kvp[PROMPT:, c])
        total = jnp.zeros((HD, TOK), F32)
        for i, (ok, kk, vv) in enumerate(zip(masks, keys, vals)):
            p, ds = grads(ok, kk, vv, qh, doh, lse, delta)
            total = total + mm_tn(kk, ds)
            if i == 0:
                dk[:, c] = mm_nn(ds, qh)
                dv[:, c] = mm_nn(p, doh)
        dq[:, c] = jnp.transpose(total * SCALE)
        att[:, c] = jnp.transpose(out_t[c, :])


def key_grad_kernel(
    info, lo_ref, r1, r2, r3, dk_own, dv_own, k, v, qd1a, qd1b, qd2, qd3, dk, dv, dk_top, dv_top
):
    own = info[0]
    core0 = info[1] == 0
    k_pos = key_index(own * TOK, TOK)
    masks = [k_pos >= lo_ref[d : d + 1, :] for d in (1, 2, 3)]
    for h in range(HEADS):
        c = head(h)
        kk, vv = k[:, c], v[:, c]
        qs = [jnp.where(core0, qd1a[:TOK, c], qd1b[:TOK, c]), qd2[:TOK, c], qd3[:TOK, c]]
        dos = [jnp.where(core0, qd1a[TOK:, c], qd1b[TOK:, c]), qd2[TOK:, c], qd3[TOK:, c]]
        dk_sum, dv_sum = dk_own[:, c], dv_own[:, c]
        for ok, qq, dd, r in zip(masks, qs, dos, (r1, r2, r3)):
            lse, delta = r[h : h + 1, :], r[HEADS + h : HEADS + h + 1, :]
            p, ds = grads(ok, kk, vv, qq, dd, lse, delta)
            dk_sum = dk_sum + mm_nn(ds, qq)
            dv_sum = dv_sum + mm_nn(p, dd)
        dk_sum = dk_sum * SCALE
        dk[:, c] = dk_sum
        dv[:, c] = dv_sum
        dk_top[:, c] = dk_sum[:PROMPT]
        dv_top[:, c] = dv_sum[:PROMPT]


def finish_kernel(info, part, other, dk_top, dv_top, dk_in, dv_in, dk, dv, dk_buf, dv_buf, sems):
    first = info[0] == 0
    dk_buf[...] = dk_top[...] + jnp.where(first, part[...], 0.0)
    dv_buf[...] = dv_top[...] + jnp.where(first, other[...].astype(F32), 0.0)
    rows = pl.ds(0, PROMPT)
    copies = [
        pltpu.make_async_copy(dk_buf, dk.at[rows], sems.at[0]),
        pltpu.make_async_copy(dv_buf, dv.at[rows], sems.at[1]),
    ]
    for copy in copies:
        copy.start()
    for copy in copies:
        copy.wait()


def call(kernel, outs, scalars, flops, *args):
    smem = pl.BlockSpec(memory_space=pltpu.SMEM)
    vmem = pl.BlockSpec(memory_space=pltpu.VMEM)
    return pl.pallas_call(
        kernel,
        out_shape=[jax.ShapeDtypeStruct(s, t) for s, t in outs],
        in_specs=[smem] * scalars + [vmem] * (len(args) - scalars),
        out_specs=[vmem] * len(outs),
        compiler_params=pltpu.CompilerParams(vmem_limit_bytes=VMEM_LIMIT),
        cost_estimate=pl.CostEstimate(flops=flops, bytes_accessed=4 << 20, transcendentals=1 << 20),
    )(*args)


def shift(x, by):
    return lax.ppermute(x, "ctx", [(i, (i + by) % NCTX) for i in range(NCTX)])


def swap(x):
    return lax.ppermute(x, "ctx", [(i, i ^ 1) for i in range(NCTX)])


def at(y, z, c):
    return (y * 8 + z) * 2 + c


def deliver(x, pairs):
    return lax.ppermute(x, "ctx", pairs)


def exchange(x, pairs):
    to = {i: i ^ 1 for i in range(NCTX)}
    for a, b in pairs:
        to[a], to[b] = b, a
    return lax.ppermute(x, "ctx", sorted(to.items()))


Z_ORDER = (4, 5, 3, 6, 2, 7, 1)
Y_ORDER = (2, 3, 1)
SPREAD = (
    ([(at(0, 0, 0), at(0, 4, 0))],),
    tuple([(at(0, n, 0), at(0, n + k, 0)) for n in (0, 4)] for k in (3, 2, 1)),
    tuple([(at(0, n, 0), at(k, n, 0)) for n in range(8)] for k in Y_ORDER),
)


def spread(held, own, steps):
    for step in steps:
        got = [deliver(held, pairs) for pairs in step]
        for pairs, g in zip(step, got):
            takes = sum([own == b for _, b in pairs], jnp.int32(0)) > 0
            held = jnp.where(takes, g, held)
    return held


def gather_cores(pk, pv, c):
    other = swap(jnp.where(c == 0, pv, pk))
    return jnp.where(c == 0, pk, pv).astype(F32) + other.astype(F32)


def gather_z(part):
    route = exchange if Z_FILL else deliver
    return [
        route(part, [(at(m, n, i), at(m, 0, i)) for m in range(4) for i in range(2)]) for n in Z_ORDER
    ]


def gather_y(part):
    route = exchange if Y_FILL else deliver
    return [route(part, [(at(m, 0, i), at(0, 0, i)) for i in range(2)]) for m in Y_ORDER]


def total_of(part, got):
    return sum([g.astype(F32) for g in got], part)


def on_device(q, k, v, do, doc_lengths):
    own = lax.axis_index("ctx")
    c = own % 2
    core0 = c == 0
    info = jnp.stack([own, c]).astype(jnp.int32)
    ends = jnp.cumsum(doc_lengths).astype(jnp.int32)
    blocks = own + jnp.arange(8, dtype=jnp.int32)
    pos = blocks[:, None] * TOK + jnp.arange(TOK, dtype=jnp.int32)[None, :]
    starts = jnp.max(jnp.where(ends[:, None, None] <= pos[None], ends[:, None, None], 0), axis=0)
    lo = jnp.where(blocks[:, None] < NCTX, jnp.maximum(starts, PROMPT), FAR)

    tok, rows8, prompt, pair = (TOK, WIDE), (8, TOK), (PROMPT, WIDE), (2 * TOK, WIDE)
    turned = (WIDE, TOK)
    smem = pl.BlockSpec(memory_space=pltpu.SMEM)
    vmem = pl.BlockSpec(memory_space=pltpu.VMEM)
    anywhere = pl.BlockSpec(memory_space=pl.ANY)
    kv, qd, sel, held = pl.pallas_call(
        pack_kernel,
        out_shape=[jax.ShapeDtypeStruct(s, BF16) for s in (pair, pair, pair, (2 * PROMPT, WIDE))],
        in_specs=[smem] + [anywhere] * 4,
        out_specs=[vmem] * 4,
        scratch_shapes=[pltpu.SemaphoreType.DMA((4,))],
    )(info, k, v, q, do)

    kv2, qd2 = shift(kv, 2), shift(qd, -2)
    first = swap(sel)
    stat, acc, do_t = call(
        own_kernel, [(rows8, F32), (turned, F32), (turned, F32)], 1, 140_000_000, info, lo, q, k, v, do
    )
    if SPREAD_GATE:
        held, first = lax.optimization_barrier((held, first))
    held = spread(held, own, SPREAD[:2])
    second = jnp.where(core0, qd2, kv2)
    kv2, qd2, first, second, held, stat, acc, do_t = lax.optimization_barrier(
        (kv2, qd2, first, second, held, stat, acc, do_t)
    )

    held = spread(held, own, SPREAD[2:])
    second, kv3, qd3 = swap(second), shift(kv2, 1), shift(qd2, -1)
    kvp = jnp.where(core0, held, swap(held))
    stat, acc = call(
        near_kernel, [(rows8, F32), (turned, F32)], 1, 280_000_000,
        info, lo, stat, acc, q, second, first, kv2,
    )
    if HALO_DONE:
        kv3, qd3, stat, acc = lax.optimization_barrier((kv3, qd3, stat, acc))
    out_t, rows, pk, pv = call(
        last_kernel, [(turned, F32), (rows8, F32), (prompt, BF16), (prompt, BF16)], 1, 300_000_000,
        info, lo, stat, acc, q, do, do_t, kv3, kvp,
    )

    part = gather_cores(pk, pv, c)
    part = total_of(part, gather_z(part.astype(BF16)))
    sent = part.astype(BF16)
    rows_sent, rows_used = rows, rows
    if GATE_R:
        sent, rows_sent = lax.optimization_barrier((sent, rows_sent))
    if GATE_DQ:
        sent, rows_used = lax.optimization_barrier((sent, rows_used))
    got = gather_y(sent)
    r1, r2, r3 = shift(rows_sent, -1), shift(rows_sent, -2), shift(rows_sent, -3)
    att, dq, dk, dv = call(
        query_grad_kernel, [(tok, F32)] * 4, 1, 1_000_000_000,
        info, lo, rows_used, out_t, q, do, k, v, second, first, kv2, kv3, kvp,
    )
    if GATE_Y:
        got[0], dq, att = lax.optimization_barrier((got[0], dq, att))
    part = total_of(part, got)
    if GATE_DK:
        part, r1, r2, r3 = lax.optimization_barrier((part, r1, r2, r3))
    dk, dv, dk_top, dv_top = call(
        key_grad_kernel, [(tok, F32), (tok, F32), (prompt, F32), (prompt, F32)], 1, 900_000_000,
        info, lo, r1, r2, r3, dk, dv, k, v, first, second, qd2, qd3,
    )
    other = swap(part.astype(BF16))
    dk, dv = pl.pallas_call(
        finish_kernel,
        out_shape=[jax.ShapeDtypeStruct(tok, F32)] * 2,
        in_specs=[smem] + [vmem] * 4 + [anywhere] * 2,
        out_specs=[anywhere] * 2,
        scratch_shapes=[pltpu.VMEM(prompt, F32), pltpu.VMEM(prompt, F32), pltpu.SemaphoreType.DMA((2,))],
        input_output_aliases={5: 0, 6: 1},
        compiler_params=pltpu.CompilerParams(vmem_limit_bytes=VMEM_LIMIT),
    )(info, part, other, dk_top, dv_top, dk, dv)
    return att, dq, dk, dv


def solution(mesh):
    spec = P("ctx", "head")
    return jax.shard_map(
        on_device, mesh=mesh, in_specs=(spec,) * 4 + (P(),), out_specs=(spec,) * 4, check_vma=False
    )
```

time: 95.3 us -> 82.3 us (0.86); the launches traced: 93.6 us -> 82.1 us
  starting transfers between devices: 55.3 us -> 38.8 us
  waiting for transfers between devices: 11.9 us -> 19.4 us
  Pallas kernels: 15.8 us -> 20.4 us
  local copies, waits for them, and re-layouts: 4.45 us -> 0.13 us
  other arithmetic: 5.17 us -> 2.14 us
    ppermute x20 -> x17, starting transfers between devices: 23 us -> 15.8 us  [the longest x10 9.88 us: exchange(): return lax.ppermute(x, 'ctx', sorted(to.items()))]
    ppermute x7, waiting for transfers between devices: 4.61 us -> 11.6 us  [shift(): return lax.ppermute(x, 'ctx', [(i, (i + by) % NCTX) for i in range(NCTX)])]
    ppermute x5, starting transfers between devices: 20.6 us -> 14.5 us  [swap(): return lax.ppermute(x, 'ctx', [(i, i ^ 1) for i in range(NCTX)])]
    unnamed x18, local copies, waits for them, and re-layouts: 3.48 us -> 0.04 us
    ppermute x7, starting transfers between devices: 11.8 us -> 8.55 us  [shift(): return lax.ppermute(x, 'ctx', [(i, (i + by) % NCTX) for i in range(NCTX)])]
    pallas_call x1 -> x2, Pallas kernels: 1.83 us -> 4.48 us  [the longest x1 3.2 us: on_device(): pl.pallas_call(pack_kernel, out_shape=[jax.ShapeDtypeStruct(s, BF16) for...]
    add x2 -> x1, other arithmetic: 2.23 us -> 0.03 us  [total_of(): return sum([g.astype(F32) for g in got], part)]
    pallas_call x3 -> x5, Pallas kernels: 13.9 us -> 15.9 us  [call(): pl.pallas_call(kernel, out_shape=[jax.ShapeDtypeStruct(s, t) for s, t in...]
  transfers between devices with their start and end apart: 32 -> 29, of which waited for: 7 -> 10; matrix products, arithmetic and copies ran while one was open for 5% -> 2% of each run, Pallas kernels for 10% -> 17%
where the time goes in v2:
time: 82.3 us; the launch traced here: 82.1 us
  starting transfers between devices  38.8 us (47%)
  Pallas kernels  20.4 us (25%)
  waiting for transfers between devices  19.4 us (24%)
  other arithmetic  2.14 us (3%)
  between operations  1.15 us (1%)
    pallas_call x5, Pallas kernels, call(): pl.pallas_call(kernel, out_shape=[jax.ShapeDtypeStruct(s, t) for s, t in...  15.9 us
    ppermute x5, starting transfers between devices, swap(): return lax.ppermute(x, 'ctx', [(i, i ^ 1) for i in range(NCTX)])  14.5 us
    ppermute x7, waiting for transfers between devices, shift(): return lax.ppermute(x, 'ctx', [(i, (i + by) % NCTX) for i in range(NCTX)])  11.6 us
    ppermute x10, starting transfers between devices, exchange(): return lax.ppermute(x, 'ctx', sorted(to.items()))  9.88 us
    ppermute x7, starting transfers between devices, shift(): return lax.ppermute(x, 'ctx', [(i, (i + by) % NCTX) for i in range(NCTX)])  8.55 us
    ppermute x7, starting transfers between devices, deliver(): return lax.ppermute(x, 'ctx', pairs)  5.96 us
    ppermute x10, waiting for transfers between devices, exchange(): return lax.ppermute(x, 'ctx', sorted(to.items()))  5.88 us
    pallas_call x1, Pallas kernels, on_device(): pl.pallas_call(pack_kernel, out_shape=[jax.ShapeDtypeStruct(s, BF16) for...  3.2 us
  transfers between devices with their start and end apart: 29, of which 10 were waited for; matrix products, arithmetic and copies ran while one was open for 2% of the time, Pallas kernels for 17%

profile of v2, /device:TPU:1, one launch (start us, length us, event | category | flops | bytes accessed | tf_op | source)
XLA Modules:
  0.0 82.1 jit_solution(5977065108635724078)
XLA Ops:
  1.2 3.2 %shard_map.84 = (bf16[512,512]{1,0:T(8,128)(2,1)}, bf16[512,512]{1,0:T(8,128)(2,1)}, bf16[512,512]{1,0:T(8,128)(2,1)}, bf16[128,512]{1,0:T(8,128)(2,1)}) custom-call(s32[2]{0:T(128)} %pad_add_fusion.info, bf16[256,512]{1,0:T(8,128)(2,1)} %k.7, bf16[256,512]{1,0:T(8,128)(2,1)} %v.7, bf16[256,512]{1,0:T(8,128)(2,1)} %q.9, bf16[256,512]{1,0:T(8,128)(2,1)} %do.7), custom_call_target="tpu_custom_call" | custom-call | tf_op jit(solution)/shard_map/pallas_call | solution.py:314
  4.5 3.3 %collective-permute-start.2 = (bf16[512,512]{1,0:T(8,128)(2,1)}, bf16[512,512]{1,0:T(8,128)(2,1)S(1)}, u32[]{:S(2)}, u32[]{:S(2)}) collective-permute-start(bf16[512,512]{1,0:T(8,128)(2,1)} %get-tuple-element.53), channel_id=1, source_target_pairs={{0,4},{4,0},{8,12},{12,8},{16,20},{20,16},{24,28},{28,24},{32,36},... | collective-permute-start | bytes 1572872 | tf_op jit(solution)/shard_map/ppermute | solution.py:241
  7.8 6.3 %collective-permute-start.1 = (bf16[512,512]{1,0:T(8,128)(2,1)}, bf16[512,512]{1,0:T(8,128)(2,1)S(1)}, u32[]{:S(2)}, u32[]{:S(2)}) collective-permute-start(bf16[512,512]{1,0:T(8,128)(2,1)} %get-tuple-element.51), channel_id=1, source_target_pairs={{0,248},{4,252},{8,0},{12,4},{16,8},{20,12},{24,16},{28,20},{32,24... | collective-permute-start | bytes 1572872 | tf_op jit(solution)/shard_map/ppermute | solution.py:237
  15.4 1.9 %shard_map.85 = (f32[8,256]{1,0:T(8,128)S(1)}, f32[512,256]{1,0:T(8,128)S(1)}, f32[512,256]{1,0:T(8,128)S(1)}) custom-call(s32[2]{0:T(128)S(1)} %copy-done.6, s32[8,256]{1,0:T(8,128)S(1)} %maximum_select_fusion.lo_ref, bf16[256,512]{1,0:T(8,128)(2,1)S(1)} %copy-done, bf16[256,512]{1,0:T(8,128)(2,1)S(1)} %copy-done.2, bf16[256,512]{1,0:T(8,128)(2,1)S(1)} %copy-done.3, ...), custom_call_target="tpu_custom_call" | custom-call | flops 140000000 | bytes 4194304 | tf_op jit(solution)/shard_map/pallas_call | solution.py:226
  19.3 7.2 %collective-permute-done.kv2 = bf16[512,512]{1,0:T(8,128)(2,1)S(1)} collective-permute-done((bf16[512,512]{1,0:T(8,128)(2,1)}, bf16[512,512]{1,0:T(8,128)(2,1)S(1)}, u32[]{:S(2)}, u32[]{:S(2)}) %collective-permute-start) | collective-permute-done | bytes 524320 | tf_op jit(solution)/shard_map/ppermute | solution.py:237
  28.1 1.3 %collective-permute-start.11 = (bf16[128,512]{1,0:T(8,128)(2,1)S(1)}, bf16[128,512]{1,0:T(8,128)(2,1)}, u32[]{:S(2)}, u32[]{:S(2)}) collective-permute-start(bf16[128,512]{1,0:T(8,128)(2,1)S(1)} %select_select_fusion.1), channel_id=1, source_target_pairs={{0,192},{8,200},{16,208},{24,216},{32,224},{40,232},{48,240},{56,2... | collective-permute-start | bytes 393224 | tf_op jit(solution)/shard_map/ppermute | solution.py:249
  29.4 1.3 %collective-permute-start.12 = (bf16[128,512]{1,0:T(8,128)(2,1)S(1)}, bf16[128,512]{1,0:T(8,128)(2,1)}, u32[]{:S(2)}, u32[]{:S(2)}) collective-permute-start(bf16[128,512]{1,0:T(8,128)(2,1)S(1)} %select_select_fusion.1), channel_id=1, source_target_pairs={{0,128},{8,136},{16,144},{24,152},{32,160},{40,168},{48,176},{56,1... | collective-permute-start | bytes 393224 | tf_op jit(solution)/shard_map/ppermute | solution.py:249
  30.7 3.3 %collective-permute-start.9 = (bf16[512,512]{1,0:T(8,128)(2,1)}, bf16[512,512]{1,0:T(8,128)(2,1)S(1)}, u32[]{:S(2)}, u32[]{:S(2)}) collective-permute-start(bf16[512,512]{1,0:T(8,128)(2,1)} %broadcast_select_fusion), channel_id=1, source_target_pairs={{0,4},{4,0},{8,12},{12,8},{16,20},{20,16},{24,28},{28,24},{32,36},... | collective-permute-start | bytes 1572872 | tf_op jit(solution)/shard_map/ppermute | solution.py:241
  34.6 4.6 %collective-permute-start.13 = (bf16[128,512]{1,0:T(8,128)(2,1)S(1)}, bf16[128,512]{1,0:T(8,128)(2,1)S(1)}, u32[]{:S(2)}, u32[]{:S(2)}) collective-permute-start(bf16[128,512]{1,0:T(8,128)(2,1)S(1)} %select_select_fusion), channel_id=1, source_target_pairs={{0,4},{4,0},{8,12},{12,8},{16,20},{20,16},{24,28},{28,24},{32,36},... | collective-permute-start | bytes 393224 | tf_op jit(solution)/shard_map/ppermute | solution.py:241
  39.2 1.0 %collective-permute-done.13 = bf16[128,512]{1,0:T(8,128)(2,1)S(1)} collective-permute-done((bf16[128,512]{1,0:T(8,128)(2,1)S(1)}, bf16[128,512]{1,0:T(8,128)(2,1)S(1)}, u32[]{:S(2)}, u32[]{:S(2)}) %collective-permute-start.13) | collective-permute-done | bytes 131104 | tf_op jit(solution)/shard_map/ppermute | solution.py:241
  40.2 2.1 %shard_map.86 = (f32[8,256]{1,0:T(8,128)S(1)}, f32[512,256]{1,0:T(8,128)S(1)}) custom-call(s32[2]{0:T(128)S(1)} %copy-done.6, s32[8,256]{1,0:T(8,128)S(1)} %maximum_select_fusion.lo_ref, f32[8,256]{1,0:T(8,128)S(1)} %get-tuple-element.61.stat_in, f32[512,256]{1,0:T(8,128)S(1)} %copy-done.5, bf16[256,512]{1,0:T(8,128)(2,1)S(1)} %copy-done, ...), custom_call_target="tpu_custom_call" | custom-call | flops 280000000 | bytes 4194304 | tf_op jit(solution)/shard_map/pallas_call | solution.py:226
  42.9 2.1 %shard_map.87 = (f32[512,256]{1,0:T(8,128)S(1)}, f32[8,256]{1,0:T(8,128)S(1)}, bf16[64,512]{1,0:T(8,128)(2,1)S(1)}, bf16[64,512]{1,0:T(8,128)(2,1)S(1)}) custom-call(s32[2]{0:T(128)S(1)} %copy-done.6, s32[8,256]{1,0:T(8,128)S(1)} %maximum_select_fusion.lo_ref, f32[8,256]{1,0:T(8,128)S(1)} %get-tuple-element.67.stat, f32[512,256]{1,0:T(8,128)S(1)} %get-tuple-element.68.acc, ...), custom_call_target="tpu_custom_call" | custom-call | flops 300000000 | bytes 4194304 | tf_op jit(solution)/shard_map/pallas_call | solution.py:226
  45.0 3.1 %collective-permute-start.14 = (bf16[64,512]{1,0:T(8,128)(2,1)S(1)}, bf16[64,512]{1,0:T(8,128)(2,1)S(1)}, u32[]{:S(2)}, u32[]{:S(2)}) collective-permute-start(bf16[64,512]{1,0:T(8,128)(2,1)S(1)} %broadcast_select_fusion.3), channel_id=1, source_target_pairs={{0,4},{4,0},{8,12},{12,8},{16,20},{20,16},{24,28},{28,24},{32,36},... | collective-permute-start | bytes 196616 | tf_op jit(solution)/shard_map/ppermute | solution.py:241
  49.0 3.7 %collective-permute-start.15 = (bf16[64,512]{1,0:T(8,128)(2,1)S(1)}, bf16[64,512]{1,0:T(8,128)(2,1)S(1)}, u32[]{:S(2)}, u32[]{:S(2)}) collective-permute-start(bf16[64,512]{1,0:T(8,128)(2,1)S(1)} %fusion), channel_id=1, source_target_pairs={{0,32},{4,36},{8,12},{12,8},{16,20},{20,16},{24,28},{28,24},{32,0}... | collective-permute-start | bytes 196616 | tf_op jit(solution)/shard_map/ppermute | solution.py:256
  52.7 1.0 %collective-permute-start.17 = (bf16[64,512]{1,0:T(8,128)(2,1)S(1)}, bf16[64,512]{1,0:T(8,128)(2,1)S(1)}, u32[]{:S(2)}, u32[]{:S(2)}) collective-permute-start(bf16[64,512]{1,0:T(8,128)(2,1)S(1)} %fusion), channel_id=1, source_target_pairs={{0,24},{4,28},{8,12},{12,8},{16,20},{20,16},{24,0},{28,4},{32,36},... | collective-permute-start | bytes 196616 | tf_op jit(solution)/shard_map/ppermute | solution.py:256
  54.6 1.6 %collective-permute-done.15 = bf16[64,512]{1,0:T(8,128)(2,1)S(1)} collective-permute-done((bf16[64,512]{1,0:T(8,128)(2,1)S(1)}, bf16[64,512]{1,0:T(8,128)(2,1)S(1)}, u32[]{:S(2)}, u32[]{:S(2)}) %collective-permute-start.15) | collective-permute-done | bytes 65568 | tf_op jit(solution)/shard_map/ppermute | solution.py:256
  56.2 2.7 %collective-permute-done.16 = bf16[64,512]{1,0:T(8,128)(2,1)S(1)} collective-permute-done((bf16[64,512]{1,0:T(8,128)(2,1)S(1)}, bf16[64,512]{1,0:T(8,128)(2,1)S(1)}, u32[]{:S(2)}, u32[]{:S(2)}) %collective-permute-start.16) | collective-permute-done | bytes 65568 | tf_op jit(solution)/shard_map/ppermute | solution.py:256
  58.9 1.7 %collective-permute-start.25 = (f32[8,256]{1,0:T(8,128)S(1)}, f32[8,256]{1,0:T(8,128)S(1)}, u32[]{:S(2)}, u32[]{:S(2)}) collective-permute-start(f32[8,256]{1,0:T(8,128)S(1)} %get-tuple-element.76.rows), channel_id=1, source_target_pairs={{0,252},{4,0},{8,4},{12,8},{16,12},{20,16},{24,20},{28,24},{32,28}... | collective-permute-start | bytes 24584 | tf_op jit(solution)/shard_map/ppermute | solution.py:237
  62.4 3.3 %collective-permute-start.22 = (bf16[64,512]{1,0:T(8,128)(2,1)S(1)}, bf16[64,512]{1,0:T(8,128)(2,1)S(1)}, u32[]{:S(2)}, u32[]{:S(2)}) collective-permute-start(bf16[64,512]{1,0:T(8,128)(2,1)S(1)} %get-tuple-element.75), channel_id=1, source_target_pairs={{0,128},{4,132},{8,12},{12,8},{16,20},{20,16},{24,28},{28,24},{32,... | collective-permute-start | bytes 196616 | tf_op jit(solution)/shard_map/ppermute | solution.py:256
  65.6 1.0 %collective-permute-start.24 = (bf16[64,512]{1,0:T(8,128)(2,1)S(1)}, bf16[64,512]{1,0:T(8,128)(2,1)S(1)}, u32[]{:S(2)}, u32[]{:S(2)}) collective-permute-start(bf16[64,512]{1,0:T(8,128)(2,1)S(1)} %get-tuple-element.75), channel_id=1, source_target_pairs={{0,64},{4,68},{8,12},{12,8},{16,20},{20,16},{24,28},{28,24},{32,36... | collective-permute-start | bytes 196616 | tf_op jit(solution)/shard_map/ppermute | solution.py:256
  66.6 5.5 %shard_map.88 = (f32[256,512]{1,0:T(8,128)}, f32[256,512]{1,0:T(8,128)}, f32[256,512]{1,0:T(8,128)S(1)}, f32[256,512]{1,0:T(8,128)S(1)}) custom-call(s32[2]{0:T(128)S(1)} %copy-done.6, s32[8,256]{1,0:T(8,128)S(1)} %maximum_select_fusion.lo_ref, f32[8,256]{1,0:T(8,128)S(1)} %get-tuple-element.76.rows, f32[512,256]{1,0:T(8,128)S(1)} %get-tuple-element.77.out_t, ...), custom_call_target="tpu_custom_call" | custom-call | flops 1000000000 | bytes 4194304 | tf_op jit(solution)/shard_map/pallas_call | solution.py:226
  72.2 3.9 %collective-permute-done.27.r3 = f32[8,256]{1,0:T(8,128)S(1)} collective-permute-done((f32[8,256]{1,0:T(8,128)S(1)}, f32[8,256]{1,0:T(8,128)S(1)}, u32[]{:S(2)}, u32[]{:S(2)}) %collective-permute-start.27) | collective-permute-done | bytes 8224 | tf_op jit(solution)/shard_map/ppermute | solution.py:237
  76.2 4.5 %shard_map.89 = (f32[256,512]{1,0:T(8,128)}, f32[256,512]{1,0:T(8,128)}, f32[64,512]{1,0:T(8,128)S(1)}, f32[64,512]{1,0:T(8,128)S(1)}) custom-call(s32[2]{0:T(128)S(1)} %copy-done.6, s32[8,256]{1,0:T(8,128)S(1)} %maximum_select_fusion.lo_ref, f32[8,256]{1,0:T(8,128)S(1)} %collective-permute-done.25.r1, f32[8,256]{1,0:T(8,128)S(1)} %collective-permute-done.26.r2, ...), custom_call_target="tpu_custom_call" | custom-call | flops 900000000 | bytes 4194304 | tf_op jit(solution)/shard_map/pallas_call | solution.py:226
  80.6 1.3 %shard_map.90 = (f32[256,512]{1,0:T(8,128)}, f32[256,512]{1,0:T(8,128)}) custom-call(s32[2]{0:T(128)S(1)} %copy-done.6, f32[64,512]{1,0:T(8,128)S(1)} %convert_add_fusion.part, bf16[64,512]{1,0:T(8,128)(2,1)S(1)} %collective-permute-done.28.other, f32[64,512]{1,0:T(8,128)S(1)} %get-tuple-element.90.dk_top, ...), custom_call_target="tpu_custom_call", output_to_operand_aliasing={{0}: (5, {}), {1}: (6, {})} | custom-call | tf_op jit(solution)/shard_map/pallas_call | solution.py:373
  (78 shorter events, 10.3 us)
Async XLA Ops:
  4.5 10.1 %collective-permute-start.2 = (bf16[512,512]{1,0:T(8,128)(2,1)}, bf16[512,512]{1,0:T(8,128)(2,1)S(1)}, u32[]{:S(2)}, u32[]{:S(2)}) collective-permute-start(bf16[512,512]{1,0:T(8,128)(2,1)} %get-tuple-element.53), channel_id=1, source_target_pairs={{0,4},{4,0},{8,12},{12,8},{16,20},{20,16},{24,28},{28,24},{32,36},... | collective-permute-start | bytes 1572872 | tf_op jit(solution)/shard_map/ppermute | solution.py:241
  7.8 18.7 %collective-permute-start = (bf16[512,512]{1,0:T(8,128)(2,1)}, bf16[512,512]{1,0:T(8,128)(2,1)S(1)}, u32[]{:S(2)}, u32[]{:S(2)}) collective-permute-start(bf16[512,512]{1,0:T(8,128)(2,1)} %get-tuple-element.50), channel_id=1, source_target_pairs={{0,8},{4,12},{8,16},{12,20},{16,24},{20,28},{24,32},{28,36},{32,40... | collective-permute-start | bytes 1572872 | tf_op jit(solution)/shard_map/ppermute | solution.py:237
  7.8 18.7 %collective-permute-start.1 = (bf16[512,512]{1,0:T(8,128)(2,1)}, bf16[512,512]{1,0:T(8,128)(2,1)S(1)}, u32[]{:S(2)}, u32[]{:S(2)}) collective-permute-start(bf16[512,512]{1,0:T(8,128)(2,1)} %get-tuple-element.51), channel_id=1, source_target_pairs={{0,248},{4,252},{8,0},{12,4},{16,8},{20,12},{24,16},{28,20},{32,24... | collective-permute-start | bytes 1572872 | tf_op jit(solution)/shard_map/ppermute | solution.py:237
  17.3 10.0 %collective-permute-start.4 = (bf16[128,512]{1,0:T(8,128)(2,1)S(1)}, bf16[128,512]{1,0:T(8,128)(2,1)S(1)}, u32[]{:S(2)}, u32[]{:S(2)}) collective-permute-start(bf16[128,512]{1,0:T(8,128)(2,1)S(1)} %broadcast_select_fusion.2), channel_id=1, source_target_pairs={{0,8},{32,40},{1,9},{33,41},{2,10},{34,42},{3,11},{35,43}} | collective-permute-start | bytes 393224 | tf_op jit(solution)/shard_map/ppermute | solution.py:249
  18.0 9.4 %collective-permute-start.5 = (bf16[128,512]{1,0:T(8,128)(2,1)S(1)}, bf16[128,512]{1,0:T(8,128)(2,1)S(1)}, u32[]{:S(2)}, u32[]{:S(2)}) collective-permute-start(bf16[128,512]{1,0:T(8,128)(2,1)S(1)} %broadcast_select_fusion.2), channel_id=1, source_target_pairs={{0,16},{32,48},{1,17},{33,49},{2,18},{34,50},{3,19},{35,51}} | collective-permute-start | bytes 393224 | tf_op jit(solution)/shard_map/ppermute | solution.py:249
  18.7 8.7 %collective-permute-start.6 = (bf16[128,512]{1,0:T(8,128)(2,1)S(1)}, bf16[128,512]{1,0:T(8,128)(2,1)S(1)}, u32[]{:S(2)}, u32[]{:S(2)}) collective-permute-start(bf16[128,512]{1,0:T(8,128)(2,1)S(1)} %broadcast_select_fusion.2), channel_id=1, source_target_pairs={{0,24},{32,56},{1,25},{33,57},{2,26},{34,58},{3,27},{35,59}} | collective-permute-start | bytes 393224 | tf_op jit(solution)/shard_map/ppermute | solution.py:249
  27.4 6.6 %collective-permute-start.10 = (bf16[128,512]{1,0:T(8,128)(2,1)S(1)}, bf16[128,512]{1,0:T(8,128)(2,1)S(1)}, u32[]{:S(2)}, u32[]{:S(2)}) collective-permute-start(bf16[128,512]{1,0:T(8,128)(2,1)S(1)} %select_select_fusion.1), channel_id=1, source_target_pairs={{0,64},{8,72},{16,80},{24,88},{32,96},{40,104},{48,112},{56,120},{... | collective-permute-start | bytes 393224 | tf_op jit(solution)/shard_map/ppermute | solution.py:249
  28.1 6.4 %collective-permute-start.11 = (bf16[128,512]{1,0:T(8,128)(2,1)S(1)}, bf16[128,512]{1,0:T(8,128)(2,1)}, u32[]{:S(2)}, u32[]{:S(2)}) collective-permute-start(bf16[128,512]{1,0:T(8,128)(2,1)S(1)} %select_select_fusion.1), channel_id=1, source_target_pairs={{0,192},{8,200},{16,208},{24,216},{32,224},{40,232},{48,240},{56,2... | collective-permute-start | bytes 393224 | tf_op jit(solution)/shard_map/ppermute | solution.py:249
  29.4 5.1 %collective-permute-start.12 = (bf16[128,512]{1,0:T(8,128)(2,1)S(1)}, bf16[128,512]{1,0:T(8,128)(2,1)}, u32[]{:S(2)}, u32[]{:S(2)}) collective-permute-start(bf16[128,512]{1,0:T(8,128)(2,1)S(1)} %select_select_fusion.1), channel_id=1, source_target_pairs={{0,128},{8,136},{16,144},{24,152},{32,160},{40,168},{48,176},{56,1... | collective-permute-start | bytes 393224 | tf_op jit(solution)/shard_map/ppermute | solution.py:249
  30.7 9.5 %collective-permute-start.9 = (bf16[512,512]{1,0:T(8,128)(2,1)}, bf16[512,512]{1,0:T(8,128)(2,1)S(1)}, u32[]{:S(2)}, u32[]{:S(2)}) collective-permute-start(bf16[512,512]{1,0:T(8,128)(2,1)} %broadcast_select_fusion), channel_id=1, source_target_pairs={{0,4},{4,0},{8,12},{12,8},{16,20},{20,16},{24,28},{28,24},{32,36},... | collective-permute-start | bytes 1572872 | tf_op jit(solution)/shard_map/ppermute | solution.py:241
  34.0 8.4 %collective-permute-start.7 = (bf16[512,512]{1,0:T(8,128)(2,1)S(1)}, bf16[512,512]{1,0:T(8,128)(2,1)S(1)}, u32[]{:S(2)}, u32[]{:S(2)}) collective-permute-start(bf16[512,512]{1,0:T(8,128)(2,1)S(1)} %collective-permute-done.kv2), channel_id=1, source_target_pairs={{0,4},{4,8},{8,12},{12,16},{16,20},{20,24},{24,28},{28,32},{32,36}... | collective-permute-start | bytes 1572872 | tf_op jit(solution)/shard_map/ppermute | solution.py:237
  34.0 8.9 %collective-permute-start.8 = (bf16[512,512]{1,0:T(8,128)(2,1)S(1)}, bf16[512,512]{1,0:T(8,128)(2,1)S(1)}, u32[]{:S(2)}, u32[]{:S(2)}) collective-permute-start(bf16[512,512]{1,0:T(8,128)(2,1)S(1)} %collective-permute-done.1.qd2), channel_id=1, source_target_pairs={{0,252},{4,0},{8,4},{12,8},{16,12},{20,16},{24,20},{28,24},{32,28}... | collective-permute-start | bytes 1572872 | tf_op jit(solution)/shard_map/ppermute | solution.py:237
  34.6 5.6 %collective-permute-start.13 = (bf16[128,512]{1,0:T(8,128)(2,1)S(1)}, bf16[128,512]{1,0:T(8,128)(2,1)S(1)}, u32[]{:S(2)}, u32[]{:S(2)}) collective-permute-start(bf16[128,512]{1,0:T(8,128)(2,1)S(1)} %select_select_fusion), channel_id=1, source_target_pairs={{0,4},{4,0},{8,12},{12,8},{16,20},{20,16},{24,28},{28,24},{32,36},... | collective-permute-start | bytes 393224 | tf_op jit(solution)/shard_map/ppermute | solution.py:241
  49.0 7.1 %collective-permute-start.15 = (bf16[64,512]{1,0:T(8,128)(2,1)S(1)}, bf16[64,512]{1,0:T(8,128)(2,1)S(1)}, u32[]{:S(2)}, u32[]{:S(2)}) collective-permute-start(bf16[64,512]{1,0:T(8,128)(2,1)S(1)} %fusion), channel_id=1, source_target_pairs={{0,32},{4,36},{8,12},{12,8},{16,20},{20,16},{24,28},{28,24},{32,0}... | collective-permute-start | bytes 196616 | tf_op jit(solution)/shard_map/ppermute | solution.py:256
  52.7 6.2 %collective-permute-start.16 = (bf16[64,512]{1,0:T(8,128)(2,1)S(1)}, bf16[64,512]{1,0:T(8,128)(2,1)S(1)}, u32[]{:S(2)}, u32[]{:S(2)}) collective-permute-start(bf16[64,512]{1,0:T(8,128)(2,1)S(1)} %fusion), channel_id=1, source_target_pairs={{0,40},{4,44},{8,12},{12,8},{16,20},{20,16},{24,28},{28,24},{32,36... | collective-permute-start | bytes 196616 | tf_op jit(solution)/shard_map/ppermute | solution.py:256
  52.7 6.2 %collective-permute-start.17 = (bf16[64,512]{1,0:T(8,128)(2,1)S(1)}, bf16[64,512]{1,0:T(8,128)(2,1)S(1)}, u32[]{:S(2)}, u32[]{:S(2)}) collective-permute-start(bf16[64,512]{1,0:T(8,128)(2,1)S(1)} %fusion), channel_id=1, source_target_pairs={{0,24},{4,28},{8,12},{12,8},{16,20},{20,16},{24,0},{28,4},{32,36},... | collective-permute-start | bytes 196616 | tf_op jit(solution)/shard_map/ppermute | solution.py:256
  53.7 7.2 %collective-permute-start.18 = (bf16[64,512]{1,0:T(8,128)(2,1)S(1)}, bf16[64,512]{1,0:T(8,128)(2,1)S(1)}, u32[]{:S(2)}, u32[]{:S(2)}) collective-permute-start(bf16[64,512]{1,0:T(8,128)(2,1)S(1)} %fusion), channel_id=1, source_target_pairs={{0,48},{4,52},{8,12},{12,8},{16,20},{20,16},{24,28},{28,24},{32,36... | collective-permute-start | bytes 196616 | tf_op jit(solution)/shard_map/ppermute | solution.py:256
  54.6 6.3 %collective-permute-start.19 = (bf16[64,512]{1,0:T(8,128)(2,1)S(1)}, bf16[64,512]{1,0:T(8,128)(2,1)S(1)}, u32[]{:S(2)}, u32[]{:S(2)}) collective-permute-start(bf16[64,512]{1,0:T(8,128)(2,1)S(1)} %fusion), channel_id=1, source_target_pairs={{0,16},{4,20},{8,12},{12,8},{16,0},{20,4},{24,28},{28,24},{32,36},... | collective-permute-start | bytes 196616 | tf_op jit(solution)/shard_map/ppermute | solution.py:256
  56.1 5.5 %collective-permute-start.20 = (bf16[64,512]{1,0:T(8,128)(2,1)S(1)}, bf16[64,512]{1,0:T(8,128)(2,1)S(1)}, u32[]{:S(2)}, u32[]{:S(2)}) collective-permute-start(bf16[64,512]{1,0:T(8,128)(2,1)S(1)} %fusion), channel_id=1, source_target_pairs={{0,56},{4,60},{8,12},{12,8},{16,20},{20,16},{24,28},{28,24},{32,36... | collective-permute-start | bytes 196616 | tf_op jit(solution)/shard_map/ppermute | solution.py:256
  58.9 13.3 %collective-permute-start.25 = (f32[8,256]{1,0:T(8,128)S(1)}, f32[8,256]{1,0:T(8,128)S(1)}, u32[]{:S(2)}, u32[]{:S(2)}) collective-permute-start(f32[8,256]{1,0:T(8,128)S(1)} %get-tuple-element.76.rows), channel_id=1, source_target_pairs={{0,252},{4,0},{8,4},{12,8},{16,12},{20,16},{24,20},{28,24},{32,28}... | collective-permute-start | bytes 24584 | tf_op jit(solution)/shard_map/ppermute | solution.py:237
  60.9 11.3 %collective-permute-start.26 = (f32[8,256]{1,0:T(8,128)S(1)}, f32[8,256]{1,0:T(8,128)S(1)}, u32[]{:S(2)}, u32[]{:S(2)}) collective-permute-start(f32[8,256]{1,0:T(8,128)S(1)} %get-tuple-element.76.rows), channel_id=1, source_target_pairs={{0,248},{4,252},{8,0},{12,4},{16,8},{20,12},{24,16},{28,20},{32,24... | collective-permute-start | bytes 24584 | tf_op jit(solution)/shard_map/ppermute | solution.py:237
  62.4 9.7 %collective-permute-start.22 = (bf16[64,512]{1,0:T(8,128)(2,1)S(1)}, bf16[64,512]{1,0:T(8,128)(2,1)S(1)}, u32[]{:S(2)}, u32[]{:S(2)}) collective-permute-start(bf16[64,512]{1,0:T(8,128)(2,1)S(1)} %get-tuple-element.75), channel_id=1, source_target_pairs={{0,128},{4,132},{8,12},{12,8},{16,20},{20,16},{24,28},{28,24},{32,... | collective-permute-start | bytes 196616 | tf_op jit(solution)/shard_map/ppermute | solution.py:256
  65.6 6.5 %collective-permute-start.23 = (bf16[64,512]{1,0:T(8,128)(2,1)S(1)}, bf16[64,512]{1,0:T(8,128)(2,1)S(1)}, u32[]{:S(2)}, u32[]{:S(2)}) collective-permute-start(bf16[64,512]{1,0:T(8,128)(2,1)S(1)} %get-tuple-element.75), channel_id=1, source_target_pairs={{0,192},{4,196},{8,12},{12,8},{16,20},{20,16},{24,28},{28,24},{32,... | collective-permute-start | bytes 196616 | tf_op jit(solution)/shard_map/ppermute | solution.py:256
  65.6 6.5 %collective-permute-start.24 = (bf16[64,512]{1,0:T(8,128)(2,1)S(1)}, bf16[64,512]{1,0:T(8,128)(2,1)S(1)}, u32[]{:S(2)}, u32[]{:S(2)}) collective-permute-start(bf16[64,512]{1,0:T(8,128)(2,1)S(1)} %get-tuple-element.75), channel_id=1, source_target_pairs={{0,64},{4,68},{8,12},{12,8},{16,20},{20,16},{24,28},{28,24},{32,36... | collective-permute-start | bytes 196616 | tf_op jit(solution)/shard_map/ppermute | solution.py:256
  (14 other events, 118.6 us)

commit v3 on v2

--- a/solution.py
+++ b/solution.py
@@ -20,9 +20,12 @@
 F32 = jnp.float32
 BF16 = jnp.bfloat16
 VMEM_LIMIT = 40 * 1024 * 1024
-GATE_R = False
-GATE_DQ = True
-GATE_Y = True
+R_AT = "sent"
+DK_WINDOW = False
+QD_WRAP = True
+KV_WRAP = True
+GATE_Z = True
+GATE_Y2 = False
 GATE_DK = True
 SPREAD_GATE = True
 HALO_DONE = True
@@ -152,57 +155,73 @@
 
 
 def query_grad_kernel(
-    info, lo_ref, rows, out_t, q, do, k, v, kv1a, kv1b, kv2, kv3, kvp, att, dq, dk, dv
+    info, lo_ref, rows, out_t, q, do, k, v, kv1a, kv1b, kv2, kv3, kvp, att, dq, dk, dv, acc
 ):
     own = info[0]
-    core0 = info[1] == 0
+    low = lo_ref[0:1, :]
+    q_pos = query_index(own)
+
+    def add(h, ok, kk, vv):
+        c = head(h)
+        lse, delta = rows[h : h + 1, :], rows[HEADS + h : HEADS + h + 1, :]
+        p, ds = grads(ok, kk, vv, q[:, c], do[:, c], lse, delta)
+        return p, ds, mm_tn(kk, ds)
+
     k_pos = key_index(own * TOK, TOK)
-    low = lo_ref[0:1, :]
-    masks = [(k_pos >= low) & (k_pos <= query_index(own))]
-    masks += [key_index((own - d) * TOK, TOK) >= low for d in (1, 2, 3)]
-    masks.append(key_index(0, PROMPT) <= query_index(own))
-    for h in range(HEADS):
-        c = head(h)
-        qh, doh = q[:, c], do[:, c]
-        lse, delta = rows[h : h + 1, :], rows[HEADS + h : HEADS + h + 1, :]
-        keys = [k[:, c], jnp.where(core0, kv1a[:TOK, c], kv1b[:TOK, c]), kv2[:TOK, c], kv3[:TOK, c]]
-        vals = [v[:, c], jnp.where(core0, kv1a[TOK:, c], kv1b[TOK:, c]), kv2[TOK:, c], kv3[TOK:, c]]
-        keys.append(kvp[:PROMPT, c])
-        vals.append(kvp[PROMPT:, c])
-        total = jnp.zeros((HD, TOK), F32)
-        for i, (ok, kk, vv) in enumerate(zip(masks, keys, vals)):
-            p, ds = grads(ok, kk, vv, qh, doh, lse, delta)
-            total = total + mm_tn(kk, ds)
-            if i == 0:
-                dk[:, c] = mm_nn(ds, qh)
-                dv[:, c] = mm_nn(p, doh)
-        dq[:, c] = jnp.transpose(total * SCALE)
+    ok_own = (k_pos >= low) & (k_pos <= q_pos)
+    ok_prompt = key_index(0, PROMPT) <= q_pos
+    for h in range(HEADS):
+        c = head(h)
+        p, ds, mine = add(h, ok_own, k[:, c], v[:, c])
+        dk[:, c] = mm_nn(ds, q[:, c])
+        dv[:, c] = mm_nn(p, do[:, c])
+        _, _, other = add(h, ok_prompt, kvp[:PROMPT, c], kvp[PROMPT:, c])
+        acc[c, :] = mine + other
         att[:, c] = jnp.transpose(out_t[c, :])
 
+    def tile(d, source):
+        @pl.when(info[2] < (own - d + 1) * TOK)
+        def _():
+            ok = key_index((own - d) * TOK, TOK) >= low
+            for h in range(HEADS):
+                c = head(h)
+                acc[c, :] += add(h, ok, source(pl.ds(0, TOK), c), source(pl.ds(TOK, TOK), c))[2]
+
+    tile(1, lambda r, c: jnp.where(info[1] == 0, kv1a[r, c], kv1b[r, c]))
+    tile(2, lambda r, c: kv2[r, c])
+    tile(3, lambda r, c: kv3[r, c])
+    for h in range(HEADS):
+        c = head(h)
+        dq[:, c] = jnp.transpose(acc[c, :] * SCALE)
+
 
 def key_grad_kernel(
-    info, lo_ref, r1, r2, r3, dk_own, dv_own, k, v, qd1a, qd1b, qd2, qd3, dk, dv, dk_top, dv_top
+    info, lo_ref, r1, r2, r3, dk_own, dv_own, k, v, qd1a, qd1b, qd2, qd3, dk, dv, dk_top, dv_top, dk_acc, dv_acc
 ):
     own = info[0]
-    core0 = info[1] == 0
     k_pos = key_index(own * TOK, TOK)
-    masks = [k_pos >= lo_ref[d : d + 1, :] for d in (1, 2, 3)]
-    for h in range(HEADS):
-        c = head(h)
-        kk, vv = k[:, c], v[:, c]
-        qs = [jnp.where(core0, qd1a[:TOK, c], qd1b[:TOK, c]), qd2[:TOK, c], qd3[:TOK, c]]
-        dos = [jnp.where(core0, qd1a[TOK:, c], qd1b[TOK:, c]), qd2[TOK:, c], qd3[TOK:, c]]
-        dk_sum, dv_sum = dk_own[:, c], dv_own[:, c]
-        for ok, qq, dd, r in zip(masks, qs, dos, (r1, r2, r3)):
-            lse, delta = r[h : h + 1, :], r[HEADS + h : HEADS + h + 1, :]
-            p, ds = grads(ok, kk, vv, qq, dd, lse, delta)
-            dk_sum = dk_sum + mm_nn(ds, qq)
-            dv_sum = dv_sum + mm_nn(p, dd)
-        dk_sum = dk_sum * SCALE
-        dk[:, c] = dk_sum
-        dv[:, c] = dv_sum
-        dk_top[:, c] = dk_sum[:PROMPT]
-        dv_top[:, c] = dv_sum[:PROMPT]
+    dk_acc[...] = dk_own[...]
+    dv_acc[...] = dv_own[...]
+
+    def tile(d, r, source):
+        @pl.when(info[2 + d] < (own + 1) * TOK)
+        def _():
+            ok = k_pos >= lo_ref[d : d + 1, :]
+            for h in range(HEADS):
+                c = head(h)
+                qq, dd = source(pl.ds(0, TOK), c), source(pl.ds(TOK, TOK), c)
+                lse, delta = r[h : h + 1, :], r[HEADS + h : HEADS + h + 1, :]
+                p, ds = grads(ok, k[:, c], v[:, c], qq, dd, lse, delta)
+                dk_acc[:, c] += mm_nn(ds, qq)
+                dv_acc[:, c] += mm_nn(p, dd)
+
+    tile(1, r1, lambda r, c: jnp.where(info[1] == 0, qd1a[r, c], qd1b[r, c]))
+    tile(2, r2, lambda r, c: qd2[r, c])
+    tile(3, r3, lambda r, c: qd3[r, c])
+    dk[...] = dk_acc[...] * SCALE
+    dv[...] = dv_acc[...]
+    dk_top[...] = dk_acc[:PROMPT, :] * SCALE
+    dv_top[...] = dv_acc[:PROMPT, :]
 
 
 def finish_kernel(info, part, other, dk_top, dv_top, dk_in, dv_in, dk, dv, dk_buf, dv_buf, sems):
@@ -220,7 +239,7 @@
         copy.wait()
 
 
-def call(kernel, outs, scalars, flops, *args):
+def call(kernel, outs, scalars, flops, *args, scratch=()):
     smem = pl.BlockSpec(memory_space=pltpu.SMEM)
     vmem = pl.BlockSpec(memory_space=pltpu.VMEM)
     return pl.pallas_call(
@@ -228,6 +247,7 @@
         out_shape=[jax.ShapeDtypeStruct(s, t) for s, t in outs],
         in_specs=[smem] * scalars + [vmem] * (len(args) - scalars),
         out_specs=[vmem] * len(outs),
+        scratch_shapes=list(scratch),
         compiler_params=pltpu.CompilerParams(vmem_limit_bytes=VMEM_LIMIT),
         cost_estimate=pl.CostEstimate(flops=flops, bytes_accessed=4 << 20, transcendentals=1 << 20),
     )(*args)
@@ -235,6 +255,12 @@
 
 def shift(x, by):
     return lax.ppermute(x, "ctx", [(i, (i + by) % NCTX) for i in range(NCTX)])
+
+
+def slide(x, by, wrap):
+    if wrap:
+        return shift(x, by)
+    return lax.ppermute(x, "ctx", [(i, i + by) for i in range(NCTX) if 0 <= i + by < NCTX])
 
 
 def swap(x):
@@ -299,12 +325,14 @@
     own = lax.axis_index("ctx")
     c = own % 2
     core0 = c == 0
-    info = jnp.stack([own, c]).astype(jnp.int32)
     ends = jnp.cumsum(doc_lengths).astype(jnp.int32)
     blocks = own + jnp.arange(8, dtype=jnp.int32)
     pos = blocks[:, None] * TOK + jnp.arange(TOK, dtype=jnp.int32)[None, :]
     starts = jnp.max(jnp.where(ends[:, None, None] <= pos[None], ends[:, None, None], 0), axis=0)
     lo = jnp.where(blocks[:, None] < NCTX, jnp.maximum(starts, PROMPT), FAR)
+
+    info = jnp.concatenate([jnp.stack([own, c]).astype(jnp.int32), lo[:4, 0]])
+    place = jnp.stack([own, c]).astype(jnp.int32)
 
     tok, rows8, prompt, pair = (TOK, WIDE), (8, TOK), (PROMPT, WIDE), (2 * TOK, WIDE)
     turned = (WIDE, TOK)
@@ -317,9 +345,9 @@
         in_specs=[smem] + [anywhere] * 4,
         out_specs=[vmem] * 4,
         scratch_shapes=[pltpu.SemaphoreType.DMA((4,))],
-    )(info, k, v, q, do)
-
-    kv2, qd2 = shift(kv, 2), shift(qd, -2)
+    )(place, k, v, q, do)
+
+    kv2, qd2 = slide(kv, 2, KV_WRAP), slide(qd, -2, QD_WRAP)
     first = swap(sel)
     stat, acc, do_t = call(
         own_kernel, [(rows8, F32), (turned, F32), (turned, F32)], 1, 140_000_000, info, lo, q, k, v, do
@@ -332,8 +360,10 @@
         (kv2, qd2, first, second, held, stat, acc, do_t)
     )
 
+    second, kv3, qd3 = swap(second), slide(kv2, 1, KV_WRAP), slide(qd2, -1, QD_WRAP)
+    if GATE_Y2:
+        held, second = lax.optimization_barrier((held, second))
     held = spread(held, own, SPREAD[2:])
-    second, kv3, qd3 = swap(second), shift(kv2, 1), shift(qd2, -1)
     kvp = jnp.where(core0, held, swap(held))
     stat, acc = call(
         near_kernel, [(rows8, F32), (turned, F32)], 1, 280_000_000,
@@ -347,28 +377,39 @@
     )
 
     part = gather_cores(pk, pv, c)
-    part = total_of(part, gather_z(part.astype(BF16)))
-    sent = part.astype(BF16)
-    rows_sent, rows_used = rows, rows
-    if GATE_R:
-        sent, rows_sent = lax.optimization_barrier((sent, rows_sent))
-    if GATE_DQ:
-        sent, rows_used = lax.optimization_barrier((sent, rows_used))
-    got = gather_y(sent)
-    r1, r2, r3 = shift(rows_sent, -1), shift(rows_sent, -2), shift(rows_sent, -3)
+    rows_sent = rows
+    if R_AT == "part":
+        part, rows_sent = lax.optimization_barrier((part, rows_sent))
+    got = gather_z(part.astype(BF16))
+    if R_AT == "got":
+        got[6], rows_sent = lax.optimization_barrier((got[6], rows_sent))
     att, dq, dk, dv = call(
         query_grad_kernel, [(tok, F32)] * 4, 1, 1_000_000_000,
-        info, lo, rows_used, out_t, q, do, k, v, second, first, kv2, kv3, kvp,
-    )
-    if GATE_Y:
-        got[0], dq, att = lax.optimization_barrier((got[0], dq, att))
+        info, lo, rows, out_t, q, do, k, v, second, first, kv2, kv3, kvp,
+        scratch=[pltpu.VMEM(turned, F32)],
+    )
+    if GATE_Z:
+        got[0], att, dq, dk, dv = lax.optimization_barrier((got[0], att, dq, dk, dv))
     part = total_of(part, got)
-    if GATE_DK:
-        part, r1, r2, r3 = lax.optimization_barrier((part, r1, r2, r3))
+    sent = part.astype(BF16)
+    if R_AT == "sent":
+        sent, rows_sent = lax.optimization_barrier((sent, rows_sent))
+    r1, r2, r3 = shift(rows_sent, -1), shift(rows_sent, -2), shift(rows_sent, -3)
+    if DK_WINDOW:
+        sent, r1, r2, r3 = lax.optimization_barrier((sent, r1, r2, r3))
+    got = gather_y(sent)
+    if not DK_WINDOW:
+        part = total_of(part, got)
+        if GATE_DK:
+            part, r1, r2, r3 = lax.optimization_barrier((part, r1, r2, r3))
     dk, dv, dk_top, dv_top = call(
         key_grad_kernel, [(tok, F32), (tok, F32), (prompt, F32), (prompt, F32)], 1, 900_000_000,
         info, lo, r1, r2, r3, dk, dv, k, v, first, second, qd2, qd3,
-    )
+        scratch=[pltpu.VMEM(tok, F32), pltpu.VMEM(tok, F32)],
+    )
+    if DK_WINDOW:
+        got[0], dk, dv = lax.optimization_barrier((got[0], dk, dv))
+        part = total_of(part, got)
     other = swap(part.astype(BF16))
     dk, dv = pl.pallas_call(
         finish_kernel,

time: 82.3 us -> 79.2 us (0.962)
  waiting for transfers between devices: 19.4 us -> 16.6 us
  Pallas kernels: 20.4 us -> 17.8 us
  starting transfers between devices: 38.8 us -> 40.3 us
    pallas_call x5, Pallas kernels: 15.9 us -> 13.3 us  [call(): pl.pallas_call(kernel, out_shape=[jax.ShapeDtypeStruct(s, t) for s, t in...]
    ppermute x7, waiting for transfers between devices: 11.6 us -> 9.47 us  [shift(): return lax.ppermute(x, 'ctx', [(i, (i + by) % NCTX) for i in range(NCTX)])]
    ppermute x10, starting transfers between devices: 9.88 us -> 11.3 us  [exchange(): return lax.ppermute(x, 'ctx', sorted(to.items()))]
    ppermute x5, starting transfers between devices: 14.5 us -> 15.5 us  [swap(): return lax.ppermute(x, 'ctx', [(i, i ^ 1) for i in range(NCTX)])]
    ppermute x7, starting transfers between devices: 8.55 us -> 7.5 us  [shift(): return lax.ppermute(x, 'ctx', [(i, (i + by) % NCTX) for i in range(NCTX)])]
  transfers between devices with their start and end apart: 29 -> 29, of which waited for: 10 -> 11; matrix products, arithmetic and copies ran while one was open for 2% -> 2% of each run, Pallas kernels for 17% -> 14%
where the time goes in v3:
time: 79.2 us; the launch traced here: 79 us
  starting transfers between devices  40.3 us (51%)
  Pallas kernels  17.8 us (22%)
  waiting for transfers between devices  16.6 us (21%)
  other arithmetic  2.27 us (3%)
  between operations  1.1 us (1%)
  local copies, waits for them, and re-layouts  0.88 us (1%)
    ppermute x5, starting transfers between devices, swap(): return lax.ppermute(x, 'ctx', [(i, i ^ 1) for i in range(NCTX)])  15.5 us
    pallas_call x5, Pallas kernels, call(): pl.pallas_call(kernel, out_shape=[jax.ShapeDtypeStruct(s, t) for s, t in...  13.3 us
    ppermute x10, starting transfers between devices, exchange(): return lax.ppermute(x, 'ctx', sorted(to.items()))  11.3 us
    ppermute x7, waiting for transfers between devices, shift(): return lax.ppermute(x, 'ctx', [(i, (i + by) % NCTX) for i in range(NCTX)])  9.47 us
    ppermute x7, starting transfers between devices, shift(): return lax.ppermute(x, 'ctx', [(i, (i + by) % NCTX) for i in range(NCTX)])  7.5 us
    ppermute x7, starting transfers between devices, deliver(): return lax.ppermute(x, 'ctx', pairs)  5.95 us
    ppermute x10, waiting for transfers between devices, exchange(): return lax.ppermute(x, 'ctx', sorted(to.items()))  5.24 us
    pallas_call x1, Pallas kernels, on_device(): pl.pallas_call(pack_kernel, out_shape=[jax.ShapeDtypeStruct(s, BF16) for...  3.2 us
  transfers between devices with their start and end apart: 29, of which 11 were waited for; matrix products, arithmetic and copies ran while one was open for 2% of the time, Pallas kernels for 14%

profile of v3, /device:TPU:1, one launch (start us, length us, event | category | flops | bytes accessed | tf_op | source)
XLA Modules:
  0.0 79.0 jit_solution(14464294430388224803)
XLA Ops:
  1.3 3.2 %shard_map.84 = (bf16[512,512]{1,0:T(8,128)(2,1)}, bf16[512,512]{1,0:T(8,128)(2,1)}, bf16[512,512]{1,0:T(8,128)(2,1)}, bf16[128,512]{1,0:T(8,128)(2,1)}) custom-call(s32[2]{0:T(128)} %pad_add_fusion.1.info, bf16[256,512]{1,0:T(8,128)(2,1)} %k.7, bf16[256,512]{1,0:T(8,128)(2,1)} %v.7, bf16[256,512]{1,0:T(8,128)(2,1)} %q.9, bf16[256,512]{1,0:T(8,128)(2,1)} %do.7), custom_call_target="tpu_custom_call" | custom-call | tf_op jit(solution)/shard_map/pallas_call | solution.py:342
  4.5 3.3 %collective-permute-start.2 = (bf16[512,512]{1,0:T(8,128)(2,1)}, bf16[512,512]{1,0:T(8,128)(2,1)S(1)}, u32[]{:S(2)}, u32[]{:S(2)}) collective-permute-start(bf16[512,512]{1,0:T(8,128)(2,1)} %get-tuple-element.55), channel_id=1, source_target_pairs={{0,4},{4,0},{8,12},{12,8},{16,20},{20,16},{24,28},{28,24},{32,36},... | collective-permute-start | bytes 1572872 | tf_op jit(solution)/shard_map/ppermute | solution.py:267
  7.8 6.3 %collective-permute-start.1 = (bf16[512,512]{1,0:T(8,128)(2,1)}, bf16[512,512]{1,0:T(8,128)(2,1)S(1)}, u32[]{:S(2)}, u32[]{:S(2)}) collective-permute-start(bf16[512,512]{1,0:T(8,128)(2,1)} %get-tuple-element.53), channel_id=1, source_target_pairs={{0,248},{4,252},{8,0},{12,4},{16,8},{20,12},{24,16},{28,20},{32,24... | collective-permute-start | bytes 1572872 | tf_op jit(solution)/shard_map/ppermute | solution.py:257
  16.2 1.9 %shard_map.85 = (f32[8,256]{1,0:T(8,128)S(1)}, f32[512,256]{1,0:T(8,128)S(1)}, f32[512,256]{1,0:T(8,128)S(1)}) custom-call(s32[6]{0:T(128)S(1)} %pad_add_fusion.info, s32[8,256]{1,0:T(8,128)S(1)} %maximum_select_fusion.lo_ref, bf16[256,512]{1,0:T(8,128)(2,1)S(1)} %copy-done, bf16[256,512]{1,0:T(8,128)(2,1)S(1)} %copy-done.2, bf16[256,512]{1,0:T(8,128)(2,1)S(1)} %copy-done.3, ...), custom_call_target="tpu_custom_call" | custom-call | flops 140000000 | bytes 4194304 | tf_op jit(solution)/shard_map/pallas_call | solution.py:245
  20.2 6.3 %collective-permute-done.kv2 = bf16[512,512]{1,0:T(8,128)(2,1)S(1)} collective-permute-done((bf16[512,512]{1,0:T(8,128)(2,1)}, bf16[512,512]{1,0:T(8,128)(2,1)S(1)}, u32[]{:S(2)}, u32[]{:S(2)}) %collective-permute-start) | collective-permute-done | bytes 524320 | tf_op jit(solution)/shard_map/ppermute | solution.py:257
  28.1 1.3 %collective-permute-start.11 = (bf16[128,512]{1,0:T(8,128)(2,1)S(1)}, bf16[128,512]{1,0:T(8,128)(2,1)}, u32[]{:S(2)}, u32[]{:S(2)}) collective-permute-start(bf16[128,512]{1,0:T(8,128)(2,1)S(1)} %select_select_fusion.1), channel_id=1, source_target_pairs={{0,192},{8,200},{16,208},{24,216},{32,224},{40,232},{48,240},{56,2... | collective-permute-start | bytes 393224 | tf_op jit(solution)/shard_map/ppermute | solution.py:275
  29.4 1.3 %collective-permute-start.12 = (bf16[128,512]{1,0:T(8,128)(2,1)S(1)}, bf16[128,512]{1,0:T(8,128)(2,1)}, u32[]{:S(2)}, u32[]{:S(2)}) collective-permute-start(bf16[128,512]{1,0:T(8,128)(2,1)S(1)} %select_select_fusion.1), channel_id=1, source_target_pairs={{0,128},{8,136},{16,144},{24,152},{32,160},{40,168},{48,176},{56,1... | collective-permute-start | bytes 393224 | tf_op jit(solution)/shard_map/ppermute | solution.py:275
  30.7 3.6 %collective-permute-start.9 = (bf16[512,512]{1,0:T(8,128)(2,1)}, bf16[512,512]{1,0:T(8,128)(2,1)S(1)}, u32[]{:S(2)}, u32[]{:S(2)}) collective-permute-start(bf16[512,512]{1,0:T(8,128)(2,1)} %broadcast_select_fusion), channel_id=1, source_target_pairs={{0,4},{4,0},{8,12},{12,8},{16,20},{20,16},{24,28},{28,24},{32,36},... | collective-permute-start | bytes 1572872 | tf_op jit(solution)/shard_map/ppermute | solution.py:267
  34.9 4.6 %collective-permute-start.13 = (bf16[128,512]{1,0:T(8,128)(2,1)S(1)}, bf16[128,512]{1,0:T(8,128)(2,1)S(1)}, u32[]{:S(2)}, u32[]{:S(2)}) collective-permute-start(bf16[128,512]{1,0:T(8,128)(2,1)S(1)} %select_select_fusion), channel_id=1, source_target_pairs={{0,4},{4,0},{8,12},{12,8},{16,20},{20,16},{24,28},{28,24},{32,36},... | collective-permute-start | bytes 393224 | tf_op jit(solution)/shard_map/ppermute | solution.py:267
  39.5 1.0 %collective-permute-done.13 = bf16[128,512]{1,0:T(8,128)(2,1)S(1)} collective-permute-done((bf16[128,512]{1,0:T(8,128)(2,1)S(1)}, bf16[128,512]{1,0:T(8,128)(2,1)S(1)}, u32[]{:S(2)}, u32[]{:S(2)}) %collective-permute-start.13) | collective-permute-done | bytes 131104 | tf_op jit(solution)/shard_map/ppermute | solution.py:267
  40.6 2.1 %shard_map.86 = (f32[8,256]{1,0:T(8,128)S(1)}, f32[512,256]{1,0:T(8,128)S(1)}) custom-call(s32[6]{0:T(128)S(1)} %pad_add_fusion.info, s32[8,256]{1,0:T(8,128)S(1)} %maximum_select_fusion.lo_ref, f32[8,256]{1,0:T(8,128)S(1)} %get-tuple-element.63.stat_in, f32[512,256]{1,0:T(8,128)S(1)} %copy-done.5, bf16[256,512]{1,0:T(8,128)(2,1)S(1)} %copy-done, ...), custom_call_target="tpu_custom_call" | custom-call | flops 280000000 | bytes 4194304 | tf_op jit(solution)/shard_map/pallas_call | solution.py:245
  43.2 2.1 %shard_map.87 = (f32[512,256]{1,0:T(8,128)S(1)}, f32[8,256]{1,0:T(8,128)S(1)}, bf16[64,512]{1,0:T(8,128)(2,1)S(1)}, bf16[64,512]{1,0:T(8,128)(2,1)S(1)}) custom-call(s32[6]{0:T(128)S(1)} %pad_add_fusion.info, s32[8,256]{1,0:T(8,128)S(1)} %maximum_select_fusion.lo_ref, f32[8,256]{1,0:T(8,128)S(1)} %get-tuple-element.69.stat, ...), custom_call_target="tpu_custom_call" | custom-call | flops 300000000 | bytes 4194304 | tf_op jit(solution)/shard_map/pallas_call | solution.py:245
  45.3 3.1 %collective-permute-start.14 = (bf16[64,512]{1,0:T(8,128)(2,1)S(1)}, bf16[64,512]{1,0:T(8,128)(2,1)S(1)}, u32[]{:S(2)}, u32[]{:S(2)}) collective-permute-start(bf16[64,512]{1,0:T(8,128)(2,1)S(1)} %broadcast_select_fusion.3), channel_id=1, source_target_pairs={{0,4},{4,0},{8,12},{12,8},{16,20},{20,16},{24,28},{28,24},{32,36},... | collective-permute-start | bytes 196616 | tf_op jit(solution)/shard_map/ppermute | solution.py:267
  49.3 4.1 %collective-permute-start.15 = (bf16[64,512]{1,0:T(8,128)(2,1)S(1)}, bf16[64,512]{1,0:T(8,128)(2,1)S(1)}, u32[]{:S(2)}, u32[]{:S(2)}) collective-permute-start(bf16[64,512]{1,0:T(8,128)(2,1)S(1)} %fusion), channel_id=1, source_target_pairs={{0,32},{4,36},{8,12},{12,8},{16,20},{20,16},{24,28},{28,24},{32,0}... | collective-permute-start | bytes 196616 | tf_op jit(solution)/shard_map/ppermute | solution.py:282
  53.4 1.0 %collective-permute-start.17 = (bf16[64,512]{1,0:T(8,128)(2,1)S(1)}, bf16[64,512]{1,0:T(8,128)(2,1)S(1)}, u32[]{:S(2)}, u32[]{:S(2)}) collective-permute-start(bf16[64,512]{1,0:T(8,128)(2,1)S(1)} %fusion), channel_id=1, source_target_pairs={{0,24},{4,28},{8,12},{12,8},{16,20},{20,16},{24,0},{28,4},{32,36},... | collective-permute-start | bytes 196616 | tf_op jit(solution)/shard_map/ppermute | solution.py:282
  55.3 1.2 %collective-permute-done.15 = bf16[64,512]{1,0:T(8,128)(2,1)S(1)} collective-permute-done((bf16[64,512]{1,0:T(8,128)(2,1)S(1)}, bf16[64,512]{1,0:T(8,128)(2,1)S(1)}, u32[]{:S(2)}, u32[]{:S(2)}) %collective-permute-start.15) | collective-permute-done | bytes 65568 | tf_op jit(solution)/shard_map/ppermute | solution.py:282
  56.9 2.7 %collective-permute-done.16 = bf16[64,512]{1,0:T(8,128)(2,1)S(1)} collective-permute-done((bf16[64,512]{1,0:T(8,128)(2,1)S(1)}, bf16[64,512]{1,0:T(8,128)(2,1)S(1)}, u32[]{:S(2)}, u32[]{:S(2)}) %collective-permute-start.16) | collective-permute-done | bytes 65568 | tf_op jit(solution)/shard_map/ppermute | solution.py:282
  59.6 4.6 %shard_map.88 = (f32[256,512]{1,0:T(8,128)}, f32[256,512]{1,0:T(8,128)}, f32[256,512]{1,0:T(8,128)S(1)}, f32[256,512]{1,0:T(8,128)S(1)}) custom-call(s32[6]{0:T(128)S(1)} %pad_add_fusion.info, s32[8,256]{1,0:T(8,128)S(1)} %maximum_select_fusion.lo_ref, f32[8,256]{1,0:T(8,128)S(1)} %get-tuple-element.86.rows, f32[512,256]{1,0:T(8,128)S(1)} %get-tuple-element.77.out_t, ...), custom_call_target="tpu_custom_call" | custom-call | flops 1000000000 | bytes 4194304 | tf_op jit(solution)/shard_map/pallas_call | solution.py:245
  64.3 1.5 %collective-permute-start.22 = (bf16[64,512]{1,0:T(8,128)(2,1)S(1)}, bf16[64,512]{1,0:T(8,128)(2,1)S(1)}, u32[]{:S(2)}, u32[]{:S(2)}) collective-permute-start(bf16[64,512]{1,0:T(8,128)(2,1)S(1)} %get-tuple-element.85), channel_id=1, source_target_pairs={{0,128},{4,132},{8,12},{12,8},{16,20},{20,16},{24,28},{28,24},{32,... | collective-permute-start | bytes 196616 | tf_op jit(solution)/shard_map/ppermute | solution.py:282
  65.8 3.4 %collective-permute-start.24 = (bf16[64,512]{1,0:T(8,128)(2,1)S(1)}, bf16[64,512]{1,0:T(8,128)(2,1)S(1)}, u32[]{:S(2)}, u32[]{:S(2)}) collective-permute-start(bf16[64,512]{1,0:T(8,128)(2,1)S(1)} %get-tuple-element.85), channel_id=1, source_target_pairs={{0,64},{4,68},{8,12},{12,8},{16,20},{20,16},{24,28},{28,24},{32,36... | collective-permute-start | bytes 196616 | tf_op jit(solution)/shard_map/ppermute | solution.py:282
  70.2 1.2 %collective-permute-done.24 = bf16[64,512]{1,0:T(8,128)(2,1)S(1)} collective-permute-done((bf16[64,512]{1,0:T(8,128)(2,1)S(1)}, bf16[64,512]{1,0:T(8,128)(2,1)S(1)}, u32[]{:S(2)}, u32[]{:S(2)}) %collective-permute-start.24) | collective-permute-done | bytes 65568 | tf_op jit(solution)/shard_map/ppermute | solution.py:282
  72.4 1.5 %collective-permute-done.27.r3 = f32[8,256]{1,0:T(8,128)S(1)} collective-permute-done((f32[8,256]{1,0:T(8,128)S(1)}, f32[8,256]{1,0:T(8,128)S(1)}, u32[]{:S(2)}, u32[]{:S(2)}) %collective-permute-start.27) | collective-permute-done | bytes 8224 | tf_op jit(solution)/shard_map/ppermute | solution.py:257
  74.8 2.7 %shard_map.89 = (f32[256,512]{1,0:T(8,128)}, f32[256,512]{1,0:T(8,128)}, f32[64,512]{1,0:T(8,128)S(1)}, f32[64,512]{1,0:T(8,128)S(1)}) custom-call(s32[6]{0:T(128)S(1)} %pad_add_fusion.info, s32[8,256]{1,0:T(8,128)S(1)} %maximum_select_fusion.lo_ref, f32[8,256]{1,0:T(8,128)S(1)} %collective-permute-done.25.r1, f32[8,256]{1,0:T(8,128)S(1)} %collective-permute-done.26.r2, ...), custom_call_target="tpu_custom_call" | custom-call | flops 900000000 | bytes 4194304 | tf_op jit(solution)/shard_map/pallas_call | solution.py:245
  77.5 1.3 %shard_map.90 = (f32[256,512]{1,0:T(8,128)}, f32[256,512]{1,0:T(8,128)}) custom-call(s32[6]{0:T(128)S(1)} %pad_add_fusion.info, f32[64,512]{1,0:T(8,128)S(1)} %convert_add_fusion.part, bf16[64,512]{1,0:T(8,128)(2,1)S(1)} %collective-permute-done.28.other, f32[64,512]{1,0:T(8,128)S(1)} %get-tuple-element.94.dk_top, ...), custom_call_target="tpu_custom_call", output_to_operand_aliasing={{0}: (5, {}), {1}: (6, {})} | custom-call | tf_op jit(solution)/shard_map/pallas_call | solution.py:414
  (78 shorter events, 12.7 us)
Async XLA Ops:
  4.5 10.8 %collective-permute-start.2 = (bf16[512,512]{1,0:T(8,128)(2,1)}, bf16[512,512]{1,0:T(8,128)(2,1)S(1)}, u32[]{:S(2)}, u32[]{:S(2)}) collective-permute-start(bf16[512,512]{1,0:T(8,128)(2,1)} %get-tuple-element.55), channel_id=1, source_target_pairs={{0,4},{4,0},{8,12},{12,8},{16,20},{20,16},{24,28},{28,24},{32,36},... | collective-permute-start | bytes 1572872 | tf_op jit(solution)/shard_map/ppermute | solution.py:267
  7.8 18.7 %collective-permute-start = (bf16[512,512]{1,0:T(8,128)(2,1)}, bf16[512,512]{1,0:T(8,128)(2,1)S(1)}, u32[]{:S(2)}, u32[]{:S(2)}) collective-permute-start(bf16[512,512]{1,0:T(8,128)(2,1)} %get-tuple-element.52), channel_id=1, source_target_pairs={{0,8},{4,12},{8,16},{12,20},{16,24},{20,28},{24,32},{28,36},{32,40... | collective-permute-start | bytes 1572872 | tf_op jit(solution)/shard_map/ppermute | solution.py:257
  7.8 18.7 %collective-permute-start.1 = (bf16[512,512]{1,0:T(8,128)(2,1)}, bf16[512,512]{1,0:T(8,128)(2,1)S(1)}, u32[]{:S(2)}, u32[]{:S(2)}) collective-permute-start(bf16[512,512]{1,0:T(8,128)(2,1)} %get-tuple-element.53), channel_id=1, source_target_pairs={{0,248},{4,252},{8,0},{12,4},{16,8},{20,12},{24,16},{28,20},{32,24... | collective-permute-start | bytes 1572872 | tf_op jit(solution)/shard_map/ppermute | solution.py:257
  18.1 9.3 %collective-permute-start.4 = (bf16[128,512]{1,0:T(8,128)(2,1)S(1)}, bf16[128,512]{1,0:T(8,128)(2,1)S(1)}, u32[]{:S(2)}, u32[]{:S(2)}) collective-permute-start(bf16[128,512]{1,0:T(8,128)(2,1)S(1)} %broadcast_select_fusion.2), channel_id=1, source_target_pairs={{0,8},{32,40},{1,9},{33,41},{2,10},{34,42},{3,11},{35,43}} | collective-permute-start | bytes 393224 | tf_op jit(solution)/shard_map/ppermute | solution.py:275
  18.8 8.6 %collective-permute-start.5 = (bf16[128,512]{1,0:T(8,128)(2,1)S(1)}, bf16[128,512]{1,0:T(8,128)(2,1)S(1)}, u32[]{:S(2)}, u32[]{:S(2)}) collective-permute-start(bf16[128,512]{1,0:T(8,128)(2,1)S(1)} %broadcast_select_fusion.2), channel_id=1, source_target_pairs={{0,16},{32,48},{1,17},{33,49},{2,18},{34,50},{3,19},{35,51}} | collective-permute-start | bytes 393224 | tf_op jit(solution)/shard_map/ppermute | solution.py:275
  19.5 7.9 %collective-permute-start.6 = (bf16[128,512]{1,0:T(8,128)(2,1)S(1)}, bf16[128,512]{1,0:T(8,128)(2,1)S(1)}, u32[]{:S(2)}, u32[]{:S(2)}) collective-permute-start(bf16[128,512]{1,0:T(8,128)(2,1)S(1)} %broadcast_select_fusion.2), channel_id=1, source_target_pairs={{0,24},{32,56},{1,25},{33,57},{2,26},{34,58},{3,27},{35,59}} | collective-permute-start | bytes 393224 | tf_op jit(solution)/shard_map/ppermute | solution.py:275
  27.4 6.9 %collective-permute-start.10 = (bf16[128,512]{1,0:T(8,128)(2,1)S(1)}, bf16[128,512]{1,0:T(8,128)(2,1)S(1)}, u32[]{:S(2)}, u32[]{:S(2)}) collective-permute-start(bf16[128,512]{1,0:T(8,128)(2,1)S(1)} %select_select_fusion.1), channel_id=1, source_target_pairs={{0,64},{8,72},{16,80},{24,88},{32,96},{40,104},{48,112},{56,120},{... | collective-permute-start | bytes 393224 | tf_op jit(solution)/shard_map/ppermute | solution.py:275
  28.1 6.7 %collective-permute-start.11 = (bf16[128,512]{1,0:T(8,128)(2,1)S(1)}, bf16[128,512]{1,0:T(8,128)(2,1)}, u32[]{:S(2)}, u32[]{:S(2)}) collective-permute-start(bf16[128,512]{1,0:T(8,128)(2,1)S(1)} %select_select_fusion.1), channel_id=1, source_target_pairs={{0,192},{8,200},{16,208},{24,216},{32,224},{40,232},{48,240},{56,2... | collective-permute-start | bytes 393224 | tf_op jit(solution)/shard_map/ppermute | solution.py:275
  29.4 5.4 %collective-permute-start.12 = (bf16[128,512]{1,0:T(8,128)(2,1)S(1)}, bf16[128,512]{1,0:T(8,128)(2,1)}, u32[]{:S(2)}, u32[]{:S(2)}) collective-permute-start(bf16[128,512]{1,0:T(8,128)(2,1)S(1)} %select_select_fusion.1), channel_id=1, source_target_pairs={{0,128},{8,136},{16,144},{24,152},{32,160},{40,168},{48,176},{56,1... | collective-permute-start | bytes 393224 | tf_op jit(solution)/shard_map/ppermute | solution.py:275
  30.7 9.8 %collective-permute-start.9 = (bf16[512,512]{1,0:T(8,128)(2,1)}, bf16[512,512]{1,0:T(8,128)(2,1)S(1)}, u32[]{:S(2)}, u32[]{:S(2)}) collective-permute-start(bf16[512,512]{1,0:T(8,128)(2,1)} %broadcast_select_fusion), channel_id=1, source_target_pairs={{0,4},{4,0},{8,12},{12,8},{16,20},{20,16},{24,28},{28,24},{32,36},... | collective-permute-start | bytes 1572872 | tf_op jit(solution)/shard_map/ppermute | solution.py:267
  34.3 8.4 %collective-permute-start.7 = (bf16[512,512]{1,0:T(8,128)(2,1)S(1)}, bf16[512,512]{1,0:T(8,128)(2,1)S(1)}, u32[]{:S(2)}, u32[]{:S(2)}) collective-permute-start(bf16[512,512]{1,0:T(8,128)(2,1)S(1)} %collective-permute-done.kv2), channel_id=1, source_target_pairs={{0,4},{4,8},{8,12},{12,16},{16,20},{20,24},{24,28},{28,32},{32,36}... | collective-permute-start | bytes 1572872 | tf_op jit(solution)/shard_map/ppermute | solution.py:257
  34.3 8.9 %collective-permute-start.8 = (bf16[512,512]{1,0:T(8,128)(2,1)S(1)}, bf16[512,512]{1,0:T(8,128)(2,1)S(1)}, u32[]{:S(2)}, u32[]{:S(2)}) collective-permute-start(bf16[512,512]{1,0:T(8,128)(2,1)S(1)} %collective-permute-done.1.qd2), channel_id=1, source_target_pairs={{0,252},{4,0},{8,4},{12,8},{16,12},{20,16},{24,20},{28,24},{32,28}... | collective-permute-start | bytes 1572872 | tf_op jit(solution)/shard_map/ppermute | solution.py:257
  34.9 5.6 %collective-permute-start.13 = (bf16[128,512]{1,0:T(8,128)(2,1)S(1)}, bf16[128,512]{1,0:T(8,128)(2,1)S(1)}, u32[]{:S(2)}, u32[]{:S(2)}) collective-permute-start(bf16[128,512]{1,0:T(8,128)(2,1)S(1)} %select_select_fusion), channel_id=1, source_target_pairs={{0,4},{4,0},{8,12},{12,8},{16,20},{20,16},{24,28},{28,24},{32,36},... | collective-permute-start | bytes 393224 | tf_op jit(solution)/shard_map/ppermute | solution.py:267
  45.3 4.0 %collective-permute-start.14 = (bf16[64,512]{1,0:T(8,128)(2,1)S(1)}, bf16[64,512]{1,0:T(8,128)(2,1)S(1)}, u32[]{:S(2)}, u32[]{:S(2)}) collective-permute-start(bf16[64,512]{1,0:T(8,128)(2,1)S(1)} %broadcast_select_fusion.3), channel_id=1, source_target_pairs={{0,4},{4,0},{8,12},{12,8},{16,20},{20,16},{24,28},{28,24},{32,36},... | collective-permute-start | bytes 196616 | tf_op jit(solution)/shard_map/ppermute | solution.py:267
  49.3 7.1 %collective-permute-start.15 = (bf16[64,512]{1,0:T(8,128)(2,1)S(1)}, bf16[64,512]{1,0:T(8,128)(2,1)S(1)}, u32[]{:S(2)}, u32[]{:S(2)}) collective-permute-start(bf16[64,512]{1,0:T(8,128)(2,1)S(1)} %fusion), channel_id=1, source_target_pairs={{0,32},{4,36},{8,12},{12,8},{16,20},{20,16},{24,28},{28,24},{32,0}... | collective-permute-start | bytes 196616 | tf_op jit(solution)/shard_map/ppermute | solution.py:282
  53.4 6.2 %collective-permute-start.16 = (bf16[64,512]{1,0:T(8,128)(2,1)S(1)}, bf16[64,512]{1,0:T(8,128)(2,1)S(1)}, u32[]{:S(2)}, u32[]{:S(2)}) collective-permute-start(bf16[64,512]{1,0:T(8,128)(2,1)S(1)} %fusion), channel_id=1, source_target_pairs={{0,40},{4,44},{8,12},{12,8},{16,20},{20,16},{24,28},{28,24},{32,36... | collective-permute-start | bytes 196616 | tf_op jit(solution)/shard_map/ppermute | solution.py:282
  53.4 10.8 %collective-permute-start.17 = (bf16[64,512]{1,0:T(8,128)(2,1)S(1)}, bf16[64,512]{1,0:T(8,128)(2,1)S(1)}, u32[]{:S(2)}, u32[]{:S(2)}) collective-permute-start(bf16[64,512]{1,0:T(8,128)(2,1)S(1)} %fusion), channel_id=1, source_target_pairs={{0,24},{4,28},{8,12},{12,8},{16,20},{20,16},{24,0},{28,4},{32,36},... | collective-permute-start | bytes 196616 | tf_op jit(solution)/shard_map/ppermute | solution.py:282
  54.4 9.8 %collective-permute-start.18 = (bf16[64,512]{1,0:T(8,128)(2,1)S(1)}, bf16[64,512]{1,0:T(8,128)(2,1)S(1)}, u32[]{:S(2)}, u32[]{:S(2)}) collective-permute-start(bf16[64,512]{1,0:T(8,128)(2,1)S(1)} %fusion), channel_id=1, source_target_pairs={{0,48},{4,52},{8,12},{12,8},{16,20},{20,16},{24,28},{28,24},{32,36... | collective-permute-start | bytes 196616 | tf_op jit(solution)/shard_map/ppermute | solution.py:282
  55.3 8.9 %collective-permute-start.19 = (bf16[64,512]{1,0:T(8,128)(2,1)S(1)}, bf16[64,512]{1,0:T(8,128)(2,1)S(1)}, u32[]{:S(2)}, u32[]{:S(2)}) collective-permute-start(bf16[64,512]{1,0:T(8,128)(2,1)S(1)} %fusion), channel_id=1, source_target_pairs={{0,16},{4,20},{8,12},{12,8},{16,0},{20,4},{24,28},{28,24},{32,36},... | collective-permute-start | bytes 196616 | tf_op jit(solution)/shard_map/ppermute | solution.py:282
  56.5 7.7 %collective-permute-start.20 = (bf16[64,512]{1,0:T(8,128)(2,1)S(1)}, bf16[64,512]{1,0:T(8,128)(2,1)S(1)}, u32[]{:S(2)}, u32[]{:S(2)}) collective-permute-start(bf16[64,512]{1,0:T(8,128)(2,1)S(1)} %fusion), channel_id=1, source_target_pairs={{0,56},{4,60},{8,12},{12,8},{16,20},{20,16},{24,28},{28,24},{32,36... | collective-permute-start | bytes 196616 | tf_op jit(solution)/shard_map/ppermute | solution.py:282
  59.6 4.6 %collective-permute-start.21 = (bf16[64,512]{1,0:T(8,128)(2,1)S(1)}, bf16[64,512]{1,0:T(8,128)(2,1)S(1)}, u32[]{:S(2)}, u32[]{:S(2)}) collective-permute-start(bf16[64,512]{1,0:T(8,128)(2,1)S(1)} %fusion), channel_id=1, source_target_pairs={{0,8},{4,12},{8,0},{12,4},{16,20},{20,16},{24,28},{28,24},{32,36},... | collective-permute-start | bytes 196616 | tf_op jit(solution)/shard_map/ppermute | solution.py:282
  64.3 5.6 %collective-permute-start.22 = (bf16[64,512]{1,0:T(8,128)(2,1)S(1)}, bf16[64,512]{1,0:T(8,128)(2,1)S(1)}, u32[]{:S(2)}, u32[]{:S(2)}) collective-permute-start(bf16[64,512]{1,0:T(8,128)(2,1)S(1)} %get-tuple-element.85), channel_id=1, source_target_pairs={{0,128},{4,132},{8,12},{12,8},{16,20},{20,16},{24,28},{28,24},{32,... | collective-permute-start | bytes 196616 | tf_op jit(solution)/shard_map/ppermute | solution.py:282
  65.8 4.3 %collective-permute-start.23 = (bf16[64,512]{1,0:T(8,128)(2,1)S(1)}, bf16[64,512]{1,0:T(8,128)(2,1)S(1)}, u32[]{:S(2)}, u32[]{:S(2)}) collective-permute-start(bf16[64,512]{1,0:T(8,128)(2,1)S(1)} %get-tuple-element.85), channel_id=1, source_target_pairs={{0,192},{4,196},{8,12},{12,8},{16,20},{20,16},{24,28},{28,24},{32,... | collective-permute-start | bytes 196616 | tf_op jit(solution)/shard_map/ppermute | solution.py:282
  65.8 5.5 %collective-permute-start.24 = (bf16[64,512]{1,0:T(8,128)(2,1)S(1)}, bf16[64,512]{1,0:T(8,128)(2,1)S(1)}, u32[]{:S(2)}, u32[]{:S(2)}) collective-permute-start(bf16[64,512]{1,0:T(8,128)(2,1)S(1)} %get-tuple-element.85), channel_id=1, source_target_pairs={{0,64},{4,68},{8,12},{12,8},{16,20},{20,16},{24,28},{28,24},{32,36... | collective-permute-start | bytes 196616 | tf_op jit(solution)/shard_map/ppermute | solution.py:282
  (13 other events, 97.3 us)

commit v4 on v3

--- a/solution.py
+++ b/solution.py
@@ -21,6 +21,7 @@
 BF16 = jnp.bfloat16
 VMEM_LIMIT = 40 * 1024 * 1024
 R_AT = "sent"
+FAN = ((2, 6), (7, 3), (1, 5))
 DK_WINDOW = False
 QD_WRAP = True
 KV_WRAP = True
@@ -282,11 +283,11 @@
     return lax.ppermute(x, "ctx", sorted(to.items()))
 
 
-Z_ORDER = (4, 5, 3, 6, 2, 7, 1)
+Z_ORDER = (1, 7, 2, 6, 3, 5, 4)
 Y_ORDER = (2, 3, 1)
 SPREAD = (
     ([(at(0, 0, 0), at(0, 4, 0))],),
-    tuple([(at(0, n, 0), at(0, n + k, 0)) for n in (0, 4)] for k in (3, 2, 1)),
+    tuple([(at(0, 0, 0), at(0, a, 0)), (at(0, 4, 0), at(0, b, 0))] for a, b in FAN),
     tuple([(at(0, n, 0), at(k, n, 0)) for n in range(8)] for k in Y_ORDER),
 )
 
@@ -388,6 +389,8 @@
         info, lo, rows, out_t, q, do, k, v, second, first, kv2, kv3, kvp,
         scratch=[pltpu.VMEM(turned, F32)],
     )
+    if R_AT == "dq":
+        rows_sent = lax.optimization_barrier((rows, dq))[0]
     if GATE_Z:
         got[0], att, dq, dk, dv = lax.optimization_barrier((got[0], att, dq, dk, dv))
     part = total_of(part, got)
@@ -396,12 +399,12 @@
         sent, rows_sent = lax.optimization_barrier((sent, rows_sent))
     r1, r2, r3 = shift(rows_sent, -1), shift(rows_sent, -2), shift(rows_sent, -3)
     if DK_WINDOW:
-        sent, r1, r2, r3 = lax.optimization_barrier((sent, r1, r2, r3))
+        r1 = lax.optimization_barrier((r1, sent))[0]
     got = gather_y(sent)
     if not DK_WINDOW:
         part = total_of(part, got)
         if GATE_DK:
-            part, r1, r2, r3 = lax.optimization_barrier((part, r1, r2, r3))
+            r1 = lax.optimization_barrier((r1, part))[0]
     dk, dv, dk_top, dv_top = call(
         key_grad_kernel, [(tok, F32), (tok, F32), (prompt, F32), (prompt, F32)], 1, 900_000_000,
         info, lo, r1, r2, r3, dk, dv, k, v, first, second, qd2, qd3,

time: 79.2 us -> 77.4 us (0.977); the launches traced: 79 us -> 76 us
  waiting for transfers between devices: 16.6 us -> 13.4 us
    ppermute x7, waiting for transfers between devices: 9.47 us -> 7.54 us  [shift(): return lax.ppermute(x, 'ctx', [(i, (i + by) % NCTX) for i in range(NCTX)])]
    ppermute x10, starting transfers between devices: 11.3 us -> 9.88 us  [exchange(): return lax.ppermute(x, 'ctx', sorted(to.items()))]
    ppermute x10, waiting for transfers between devices: 5.24 us -> 3.91 us  [exchange(): return lax.ppermute(x, 'ctx', sorted(to.items()))]
    ppermute x7, starting transfers between devices: 7.5 us -> 8.73 us  [shift(): return lax.ppermute(x, 'ctx', [(i, (i + by) % NCTX) for i in range(NCTX)])]
  transfers between devices with their start and end apart: 29 -> 29, of which waited for: 11 -> 9; matrix products, arithmetic and copies ran while one was open for 2% -> 2% of each run, Pallas kernels for 14% -> 15%
where the time goes in v4:
time: 77.4 us; the launch traced here: 76 us
  starting transfers between devices  40.6 us (52%)
  Pallas kernels  17.8 us (23%)
  waiting for transfers between devices  13.4 us (17%)
  other arithmetic  2.22 us (3%)
  between operations  1.08 us (1%)
  local copies, waits for them, and re-layouts  0.88 us (1%)
    ppermute x5, starting transfers between devices, swap(): return lax.ppermute(x, 'ctx', [(i, i ^ 1) for i in range(NCTX)])  16.1 us
    pallas_call x5, Pallas kernels, call(): pl.pallas_call(kernel, out_shape=[jax.ShapeDtypeStruct(s, t) for s, t in...  13.3 us
    ppermute x10, starting transfers between devices, exchange(): return lax.ppermute(x, 'ctx', sorted(to.items()))  9.88 us
    ppermute x7, starting transfers between devices, shift(): return lax.ppermute(x, 'ctx', [(i, (i + by) % NCTX) for i in range(NCTX)])  8.73 us
    ppermute x7, waiting for transfers between devices, shift(): return lax.ppermute(x, 'ctx', [(i, (i + by) % NCTX) for i in range(NCTX)])  7.54 us
    ppermute x7, starting transfers between devices, deliver(): return lax.ppermute(x, 'ctx', pairs)  5.95 us
    ppermute x10, waiting for transfers between devices, exchange(): return lax.ppermute(x, 'ctx', sorted(to.items()))  3.91 us
    pallas_call x1, Pallas kernels, on_device(): pl.pallas_call(pack_kernel, out_shape=[jax.ShapeDtypeStruct(s, BF16) for...  3.2 us
  transfers between devices with their start and end apart: 29, of which 9 were waited for; matrix products, arithmetic and copies ran while one was open for 2% of the time, Pallas kernels for 15%

profile of v4, /device:TPU:1, one launch (start us, length us, event | category | flops | bytes accessed | tf_op | source)
XLA Modules:
  0.0 76.0 jit_solution(14933539860208243523)
XLA Ops:
  1.2 3.2 %shard_map.84 = (bf16[512,512]{1,0:T(8,128)(2,1)}, bf16[512,512]{1,0:T(8,128)(2,1)}, bf16[512,512]{1,0:T(8,128)(2,1)}, bf16[128,512]{1,0:T(8,128)(2,1)}) custom-call(s32[2]{0:T(128)} %pad_add_fusion.1.info, bf16[256,512]{1,0:T(8,128)(2,1)} %k.7, bf16[256,512]{1,0:T(8,128)(2,1)} %v.7, bf16[256,512]{1,0:T(8,128)(2,1)} %q.9, bf16[256,512]{1,0:T(8,128)(2,1)} %do.7), custom_call_target="tpu_custom_call" | custom-call | tf_op jit(solution)/shard_map/pallas_call | solution.py:343
  4.4 3.3 %collective-permute-start.2 = (bf16[512,512]{1,0:T(8,128)(2,1)}, bf16[512,512]{1,0:T(8,128)(2,1)S(1)}, u32[]{:S(2)}, u32[]{:S(2)}) collective-permute-start(bf16[512,512]{1,0:T(8,128)(2,1)} %get-tuple-element.52), channel_id=1, source_target_pairs={{0,4},{4,0},{8,12},{12,8},{16,20},{20,16},{24,28},{28,24},{32,36},... | collective-permute-start | bytes 1572872 | tf_op jit(solution)/shard_map/ppermute | solution.py:268
  7.8 6.3 %collective-permute-start.1 = (bf16[512,512]{1,0:T(8,128)(2,1)}, bf16[512,512]{1,0:T(8,128)(2,1)S(1)}, u32[]{:S(2)}, u32[]{:S(2)}) collective-permute-start(bf16[512,512]{1,0:T(8,128)(2,1)} %get-tuple-element.50), channel_id=1, source_target_pairs={{0,248},{4,252},{8,0},{12,4},{16,8},{20,12},{24,16},{28,20},{32,24... | collective-permute-start | bytes 1572872 | tf_op jit(solution)/shard_map/ppermute | solution.py:258
  16.2 1.9 %shard_map.85 = (f32[8,256]{1,0:T(8,128)S(1)}, f32[512,256]{1,0:T(8,128)S(1)}, f32[512,256]{1,0:T(8,128)S(1)}) custom-call(s32[6]{0:T(128)S(1)} %pad_add_fusion.info, s32[8,256]{1,0:T(8,128)S(1)} %maximum_select_fusion.lo_ref, bf16[256,512]{1,0:T(8,128)(2,1)S(1)} %copy-done, bf16[256,512]{1,0:T(8,128)(2,1)S(1)} %copy-done.2, bf16[256,512]{1,0:T(8,128)(2,1)S(1)} %copy-done.3, ...), custom_call_target="tpu_custom_call" | custom-call | flops 140000000 | bytes 4194304 | tf_op jit(solution)/shard_map/pallas_call | solution.py:246
  20.1 6.3 %collective-permute-done.kv2 = bf16[512,512]{1,0:T(8,128)(2,1)S(1)} collective-permute-done((bf16[512,512]{1,0:T(8,128)(2,1)}, bf16[512,512]{1,0:T(8,128)(2,1)S(1)}, u32[]{:S(2)}, u32[]{:S(2)}) %collective-permute-start) | collective-permute-done | bytes 524320 | tf_op jit(solution)/shard_map/ppermute | solution.py:258
  28.1 1.3 %collective-permute-start.11 = (bf16[128,512]{1,0:T(8,128)(2,1)S(1)}, bf16[128,512]{1,0:T(8,128)(2,1)}, u32[]{:S(2)}, u32[]{:S(2)}) collective-permute-start(bf16[128,512]{1,0:T(8,128)(2,1)S(1)} %select_select_fusion.1), channel_id=1, source_target_pairs={{0,192},{8,200},{16,208},{24,216},{32,224},{40,232},{48,240},{56,2... | collective-permute-start | bytes 393224 | tf_op jit(solution)/shard_map/ppermute | solution.py:276
  29.4 1.3 %collective-permute-start.12 = (bf16[128,512]{1,0:T(8,128)(2,1)S(1)}, bf16[128,512]{1,0:T(8,128)(2,1)}, u32[]{:S(2)}, u32[]{:S(2)}) collective-permute-start(bf16[128,512]{1,0:T(8,128)(2,1)S(1)} %select_select_fusion.1), channel_id=1, source_target_pairs={{0,128},{8,136},{16,144},{24,152},{32,160},{40,168},{48,176},{56,1... | collective-permute-start | bytes 393224 | tf_op jit(solution)/shard_map/ppermute | solution.py:276
  30.7 3.4 %collective-permute-start.9 = (bf16[512,512]{1,0:T(8,128)(2,1)}, bf16[512,512]{1,0:T(8,128)(2,1)S(1)}, u32[]{:S(2)}, u32[]{:S(2)}) collective-permute-start(bf16[512,512]{1,0:T(8,128)(2,1)} %broadcast_select_fusion), channel_id=1, source_target_pairs={{0,4},{4,0},{8,12},{12,8},{16,20},{20,16},{24,28},{28,24},{32,36},... | collective-permute-start | bytes 1572872 | tf_op jit(solution)/shard_map/ppermute | solution.py:268
  34.7 4.6 %collective-permute-start.13 = (bf16[128,512]{1,0:T(8,128)(2,1)S(1)}, bf16[128,512]{1,0:T(8,128)(2,1)S(1)}, u32[]{:S(2)}, u32[]{:S(2)}) collective-permute-start(bf16[128,512]{1,0:T(8,128)(2,1)S(1)} %select_select_fusion), channel_id=1, source_target_pairs={{0,4},{4,0},{8,12},{12,8},{16,20},{20,16},{24,28},{28,24},{32,36},... | collective-permute-start | bytes 393224 | tf_op jit(solution)/shard_map/ppermute | solution.py:268
  39.3 1.0 %collective-permute-done.13 = bf16[128,512]{1,0:T(8,128)(2,1)S(1)} collective-permute-done((bf16[128,512]{1,0:T(8,128)(2,1)S(1)}, bf16[128,512]{1,0:T(8,128)(2,1)S(1)}, u32[]{:S(2)}, u32[]{:S(2)}) %collective-permute-start.13) | collective-permute-done | bytes 131104 | tf_op jit(solution)/shard_map/ppermute | solution.py:268
  40.3 2.1 %shard_map.86 = (f32[8,256]{1,0:T(8,128)S(1)}, f32[512,256]{1,0:T(8,128)S(1)}) custom-call(s32[6]{0:T(128)S(1)} %pad_add_fusion.info, s32[8,256]{1,0:T(8,128)S(1)} %maximum_select_fusion.lo_ref, f32[8,256]{1,0:T(8,128)S(1)} %get-tuple-element.60.stat_in, f32[512,256]{1,0:T(8,128)S(1)} %copy-done.5, bf16[256,512]{1,0:T(8,128)(2,1)S(1)} %copy-done, ...), custom_call_target="tpu_custom_call" | custom-call | flops 280000000 | bytes 4194304 | tf_op jit(solution)/shard_map/pallas_call | solution.py:246
  43.0 2.1 %shard_map.87 = (f32[512,256]{1,0:T(8,128)S(1)}, f32[8,256]{1,0:T(8,128)S(1)}, bf16[64,512]{1,0:T(8,128)(2,1)S(1)}, bf16[64,512]{1,0:T(8,128)(2,1)S(1)}) custom-call(s32[6]{0:T(128)S(1)} %pad_add_fusion.info, s32[8,256]{1,0:T(8,128)S(1)} %maximum_select_fusion.lo_ref, f32[8,256]{1,0:T(8,128)S(1)} %get-tuple-element.66.stat, ...), custom_call_target="tpu_custom_call" | custom-call | flops 300000000 | bytes 4194304 | tf_op jit(solution)/shard_map/pallas_call | solution.py:246
  45.1 3.1 %collective-permute-start.14 = (bf16[64,512]{1,0:T(8,128)(2,1)S(1)}, bf16[64,512]{1,0:T(8,128)(2,1)S(1)}, u32[]{:S(2)}, u32[]{:S(2)}) collective-permute-start(bf16[64,512]{1,0:T(8,128)(2,1)S(1)} %broadcast_select_fusion.3), channel_id=1, source_target_pairs={{0,4},{4,0},{8,12},{12,8},{16,20},{20,16},{24,28},{28,24},{32,36},... | collective-permute-start | bytes 196616 | tf_op jit(solution)/shard_map/ppermute | solution.py:268
  48.2 0.9 %collective-permute-done.14 = bf16[64,512]{1,0:T(8,128)(2,1)S(1)} collective-permute-done((bf16[64,512]{1,0:T(8,128)(2,1)S(1)}, bf16[64,512]{1,0:T(8,128)(2,1)S(1)}, u32[]{:S(2)}, u32[]{:S(2)}) %collective-permute-start.14) | collective-permute-done | bytes 65568 | tf_op jit(solution)/shard_map/ppermute | solution.py:268
  49.5 3.5 %collective-permute-start.16 = (bf16[64,512]{1,0:T(8,128)(2,1)S(1)}, bf16[64,512]{1,0:T(8,128)(2,1)S(1)}, u32[]{:S(2)}, u32[]{:S(2)}) collective-permute-start(bf16[64,512]{1,0:T(8,128)(2,1)S(1)} %fusion), channel_id=1, source_target_pairs={{0,56},{4,60},{8,12},{12,8},{16,20},{20,16},{24,28},{28,24},{32,36... | collective-permute-start | bytes 196616 | tf_op jit(solution)/shard_map/ppermute | solution.py:283
  53.0 1.0 %collective-permute-start.18 = (bf16[64,512]{1,0:T(8,128)(2,1)S(1)}, bf16[64,512]{1,0:T(8,128)(2,1)S(1)}, u32[]{:S(2)}, u32[]{:S(2)}) collective-permute-start(bf16[64,512]{1,0:T(8,128)(2,1)S(1)} %fusion), channel_id=1, source_target_pairs={{0,48},{4,52},{8,12},{12,8},{16,20},{20,16},{24,28},{28,24},{32,36... | collective-permute-start | bytes 196616 | tf_op jit(solution)/shard_map/ppermute | solution.py:283
  55.7 4.6 %shard_map.88 = (f32[256,512]{1,0:T(8,128)}, f32[256,512]{1,0:T(8,128)}, f32[256,512]{1,0:T(8,128)S(1)}, f32[256,512]{1,0:T(8,128)S(1)}) custom-call(s32[6]{0:T(128)S(1)} %pad_add_fusion.info, s32[8,256]{1,0:T(8,128)S(1)} %maximum_select_fusion.lo_ref, f32[8,256]{1,0:T(8,128)S(1)} %get-tuple-element.83.rows, f32[512,256]{1,0:T(8,128)S(1)} %get-tuple-element.74.out_t, ...), custom_call_target="tpu_custom_call" | custom-call | flops 1000000000 | bytes 4194304 | tf_op jit(solution)/shard_map/pallas_call | solution.py:246
  60.9 1.8 %collective-permute-done.21 = bf16[64,512]{1,0:T(8,128)(2,1)S(1)} collective-permute-done((bf16[64,512]{1,0:T(8,128)(2,1)S(1)}, bf16[64,512]{1,0:T(8,128)(2,1)S(1)}, u32[]{:S(2)}, u32[]{:S(2)}) %collective-permute-start.21) | collective-permute-done | bytes 65568 | tf_op jit(solution)/shard_map/ppermute | solution.py:283
  62.9 3.3 %collective-permute-start.23 = (bf16[64,512]{1,0:T(8,128)(2,1)S(1)}, bf16[64,512]{1,0:T(8,128)(2,1)S(1)}, u32[]{:S(2)}, u32[]{:S(2)}) collective-permute-start(bf16[64,512]{1,0:T(8,128)(2,1)S(1)} %get-tuple-element.82), channel_id=1, source_target_pairs={{0,192},{4,196},{8,12},{12,8},{16,20},{20,16},{24,28},{28,24},{32,... | collective-permute-start | bytes 196616 | tf_op jit(solution)/shard_map/ppermute | solution.py:283
  66.5 1.3 %collective-permute-start.27 = (f32[8,256]{1,0:T(8,128)S(1)}, f32[8,256]{1,0:T(8,128)S(1)}, u32[]{:S(2)}, u32[]{:S(2)}) collective-permute-start(f32[8,256]{1,0:T(8,128)S(1)} %get-tuple-element.83.rows), channel_id=1, source_target_pairs={{0,248},{4,252},{8,0},{12,4},{16,8},{20,12},{24,16},{28,20},{32,24... | collective-permute-start | bytes 24584 | tf_op jit(solution)/shard_map/ppermute | solution.py:258
  68.2 1.4 %collective-permute-done.24 = bf16[64,512]{1,0:T(8,128)(2,1)S(1)} collective-permute-done((bf16[64,512]{1,0:T(8,128)(2,1)S(1)}, bf16[64,512]{1,0:T(8,128)(2,1)S(1)}, u32[]{:S(2)}, u32[]{:S(2)}) %collective-permute-start.24) | collective-permute-done | bytes 65568 | tf_op jit(solution)/shard_map/ppermute | solution.py:283
  69.6 1.6 %collective-permute-start.25 = (bf16[64,512]{1,0:T(8,128)(2,1)S(1)}, bf16[64,512]{1,0:T(8,128)(2,1)S(1)}, u32[]{:S(2)}, u32[]{:S(2)}) collective-permute-start(bf16[64,512]{1,0:T(8,128)(2,1)S(1)} %get-tuple-element.94), channel_id=1, source_target_pairs={{0,4},{4,0},{8,12},{12,8},{16,20},{20,16},{24,28},{28,24},{32,36},... | collective-permute-start | bytes 196616 | tf_op jit(solution)/shard_map/ppermute | solution.py:268
  71.8 2.7 %shard_map.89 = (f32[256,512]{1,0:T(8,128)}, f32[256,512]{1,0:T(8,128)}, f32[64,512]{1,0:T(8,128)S(1)}, f32[64,512]{1,0:T(8,128)S(1)}) custom-call(s32[6]{0:T(128)S(1)} %pad_add_fusion.info, s32[8,256]{1,0:T(8,128)S(1)} %maximum_select_fusion.lo_ref, f32[8,256]{1,0:T(8,128)S(1)} %collective-permute-done.26.r1, f32[8,256]{1,0:T(8,128)S(1)} %collective-permute-done.27.r2, ...), custom_call_target="tpu_custom_call" | custom-call | flops 900000000 | bytes 4194304 | tf_op jit(solution)/shard_map/pallas_call | solution.py:246
  74.5 1.3 %shard_map.90 = (f32[256,512]{1,0:T(8,128)}, f32[256,512]{1,0:T(8,128)}) custom-call(s32[6]{0:T(128)S(1)} %pad_add_fusion.info, f32[64,512]{1,0:T(8,128)S(1)} %get-tuple-element.95.part, bf16[64,512]{1,0:T(8,128)(2,1)S(1)} %collective-permute-done.25.other, f32[64,512]{1,0:T(8,128)S(1)} %get-tuple-element.88.dk_top, ...), custom_call_target="tpu_custom_call", output_to_operand_aliasing={{0}: (5, {}), {1}: (6, {})} | custom-call | tf_op jit(solution)/shard_map/pallas_call | solution.py:417
  (77 shorter events, 11.6 us)
Async XLA Ops:
  4.4 10.8 %collective-permute-start.2 = (bf16[512,512]{1,0:T(8,128)(2,1)}, bf16[512,512]{1,0:T(8,128)(2,1)S(1)}, u32[]{:S(2)}, u32[]{:S(2)}) collective-permute-start(bf16[512,512]{1,0:T(8,128)(2,1)} %get-tuple-element.52), channel_id=1, source_target_pairs={{0,4},{4,0},{8,12},{12,8},{16,20},{20,16},{24,28},{28,24},{32,36},... | collective-permute-start | bytes 1572872 | tf_op jit(solution)/shard_map/ppermute | solution.py:268
  7.8 18.7 %collective-permute-start = (bf16[512,512]{1,0:T(8,128)(2,1)}, bf16[512,512]{1,0:T(8,128)(2,1)S(1)}, u32[]{:S(2)}, u32[]{:S(2)}) collective-permute-start(bf16[512,512]{1,0:T(8,128)(2,1)} %get-tuple-element.49), channel_id=1, source_target_pairs={{0,8},{4,12},{8,16},{12,20},{16,24},{20,28},{24,32},{28,36},{32,40... | collective-permute-start | bytes 1572872 | tf_op jit(solution)/shard_map/ppermute | solution.py:258
  7.8 18.7 %collective-permute-start.1 = (bf16[512,512]{1,0:T(8,128)(2,1)}, bf16[512,512]{1,0:T(8,128)(2,1)S(1)}, u32[]{:S(2)}, u32[]{:S(2)}) collective-permute-start(bf16[512,512]{1,0:T(8,128)(2,1)} %get-tuple-element.50), channel_id=1, source_target_pairs={{0,248},{4,252},{8,0},{12,4},{16,8},{20,12},{24,16},{28,20},{32,24... | collective-permute-start | bytes 1572872 | tf_op jit(solution)/shard_map/ppermute | solution.py:258
  18.1 9.3 %collective-permute-start.4 = (bf16[128,512]{1,0:T(8,128)(2,1)S(1)}, bf16[128,512]{1,0:T(8,128)(2,1)S(1)}, u32[]{:S(2)}, u32[]{:S(2)}) collective-permute-start(bf16[128,512]{1,0:T(8,128)(2,1)S(1)} %broadcast_select_fusion.2), channel_id=1, source_target_pairs={{0,8},{32,40},{1,9},{33,41},{2,10},{34,42},{3,11},{35,43}} | collective-permute-start | bytes 393224 | tf_op jit(solution)/shard_map/ppermute | solution.py:276
  18.8 8.6 %collective-permute-start.5 = (bf16[128,512]{1,0:T(8,128)(2,1)S(1)}, bf16[128,512]{1,0:T(8,128)(2,1)S(1)}, u32[]{:S(2)}, u32[]{:S(2)}) collective-permute-start(bf16[128,512]{1,0:T(8,128)(2,1)S(1)} %broadcast_select_fusion.2), channel_id=1, source_target_pairs={{0,56},{32,24},{1,57},{33,25},{2,58},{34,26},{3,59},{35,27}} | collective-permute-start | bytes 393224 | tf_op jit(solution)/shard_map/ppermute | solution.py:276
  19.4 7.9 %collective-permute-start.6 = (bf16[128,512]{1,0:T(8,128)(2,1)S(1)}, bf16[128,512]{1,0:T(8,128)(2,1)S(1)}, u32[]{:S(2)}, u32[]{:S(2)}) collective-permute-start(bf16[128,512]{1,0:T(8,128)(2,1)S(1)} %broadcast_select_fusion.2), channel_id=1, source_target_pairs={{0,16},{32,48},{1,17},{33,49},{2,18},{34,50},{3,19},{35,51}} | collective-permute-start | bytes 393224 | tf_op jit(solution)/shard_map/ppermute | solution.py:276
  27.4 6.7 %collective-permute-start.10 = (bf16[128,512]{1,0:T(8,128)(2,1)S(1)}, bf16[128,512]{1,0:T(8,128)(2,1)S(1)}, u32[]{:S(2)}, u32[]{:S(2)}) collective-permute-start(bf16[128,512]{1,0:T(8,128)(2,1)S(1)} %select_select_fusion.1), channel_id=1, source_target_pairs={{0,64},{8,72},{16,80},{24,88},{32,96},{40,104},{48,112},{56,120},{... | collective-permute-start | bytes 393224 | tf_op jit(solution)/shard_map/ppermute | solution.py:276
  28.1 6.5 %collective-permute-start.11 = (bf16[128,512]{1,0:T(8,128)(2,1)S(1)}, bf16[128,512]{1,0:T(8,128)(2,1)}, u32[]{:S(2)}, u32[]{:S(2)}) collective-permute-start(bf16[128,512]{1,0:T(8,128)(2,1)S(1)} %select_select_fusion.1), channel_id=1, source_target_pairs={{0,192},{8,200},{16,208},{24,216},{32,224},{40,232},{48,240},{56,2... | collective-permute-start | bytes 393224 | tf_op jit(solution)/shard_map/ppermute | solution.py:276
  29.4 5.2 %collective-permute-start.12 = (bf16[128,512]{1,0:T(8,128)(2,1)S(1)}, bf16[128,512]{1,0:T(8,128)(2,1)}, u32[]{:S(2)}, u32[]{:S(2)}) collective-permute-start(bf16[128,512]{1,0:T(8,128)(2,1)S(1)} %select_select_fusion.1), channel_id=1, source_target_pairs={{0,128},{8,136},{16,144},{24,152},{32,160},{40,168},{48,176},{56,1... | collective-permute-start | bytes 393224 | tf_op jit(solution)/shard_map/ppermute | solution.py:276
  30.7 9.6 %collective-permute-start.9 = (bf16[512,512]{1,0:T(8,128)(2,1)}, bf16[512,512]{1,0:T(8,128)(2,1)S(1)}, u32[]{:S(2)}, u32[]{:S(2)}) collective-permute-start(bf16[512,512]{1,0:T(8,128)(2,1)} %broadcast_select_fusion), channel_id=1, source_target_pairs={{0,4},{4,0},{8,12},{12,8},{16,20},{20,16},{24,28},{28,24},{32,36},... | collective-permute-start | bytes 1572872 | tf_op jit(solution)/shard_map/ppermute | solution.py:268
  34.1 8.4 %collective-permute-start.7 = (bf16[512,512]{1,0:T(8,128)(2,1)S(1)}, bf16[512,512]{1,0:T(8,128)(2,1)S(1)}, u32[]{:S(2)}, u32[]{:S(2)}) collective-permute-start(bf16[512,512]{1,0:T(8,128)(2,1)S(1)} %collective-permute-done.kv2), channel_id=1, source_target_pairs={{0,4},{4,8},{8,12},{12,16},{16,20},{20,24},{24,28},{28,32},{32,36}... | collective-permute-start | bytes 1572872 | tf_op jit(solution)/shard_map/ppermute | solution.py:258
  34.1 8.9 %collective-permute-start.8 = (bf16[512,512]{1,0:T(8,128)(2,1)S(1)}, bf16[512,512]{1,0:T(8,128)(2,1)S(1)}, u32[]{:S(2)}, u32[]{:S(2)}) collective-permute-start(bf16[512,512]{1,0:T(8,128)(2,1)S(1)} %collective-permute-done.1.qd2), channel_id=1, source_target_pairs={{0,252},{4,0},{8,4},{12,8},{16,12},{20,16},{24,20},{28,24},{32,28}... | collective-permute-start | bytes 1572872 | tf_op jit(solution)/shard_map/ppermute | solution.py:258
  34.7 5.6 %collective-permute-start.13 = (bf16[128,512]{1,0:T(8,128)(2,1)S(1)}, bf16[128,512]{1,0:T(8,128)(2,1)S(1)}, u32[]{:S(2)}, u32[]{:S(2)}) collective-permute-start(bf16[128,512]{1,0:T(8,128)(2,1)S(1)} %select_select_fusion), channel_id=1, source_target_pairs={{0,4},{4,0},{8,12},{12,8},{16,20},{20,16},{24,28},{28,24},{32,36},... | collective-permute-start | bytes 393224 | tf_op jit(solution)/shard_map/ppermute | solution.py:268
  49.1 5.6 %collective-permute-start.15 = (bf16[64,512]{1,0:T(8,128)(2,1)S(1)}, bf16[64,512]{1,0:T(8,128)(2,1)S(1)}, u32[]{:S(2)}, u32[]{:S(2)}) collective-permute-start(bf16[64,512]{1,0:T(8,128)(2,1)S(1)} %fusion), channel_id=1, source_target_pairs={{0,8},{4,12},{8,0},{12,4},{16,20},{20,16},{24,28},{28,24},{32,36},... | collective-permute-start | bytes 196616 | tf_op jit(solution)/shard_map/ppermute | solution.py:283
  49.5 6.2 %collective-permute-start.16 = (bf16[64,512]{1,0:T(8,128)(2,1)S(1)}, bf16[64,512]{1,0:T(8,128)(2,1)S(1)}, u32[]{:S(2)}, u32[]{:S(2)}) collective-permute-start(bf16[64,512]{1,0:T(8,128)(2,1)S(1)} %fusion), channel_id=1, source_target_pairs={{0,56},{4,60},{8,12},{12,8},{16,20},{20,16},{24,28},{28,24},{32,36... | collective-permute-start | bytes 196616 | tf_op jit(solution)/shard_map/ppermute | solution.py:283
  53.0 7.3 %collective-permute-start.17 = (bf16[64,512]{1,0:T(8,128)(2,1)S(1)}, bf16[64,512]{1,0:T(8,128)(2,1)S(1)}, u32[]{:S(2)}, u32[]{:S(2)}) collective-permute-start(bf16[64,512]{1,0:T(8,128)(2,1)S(1)} %fusion), channel_id=1, source_target_pairs={{0,16},{4,20},{8,12},{12,8},{16,0},{20,4},{24,28},{28,24},{32,36},... | collective-permute-start | bytes 196616 | tf_op jit(solution)/shard_map/ppermute | solution.py:283
  53.0 7.3 %collective-permute-start.18 = (bf16[64,512]{1,0:T(8,128)(2,1)S(1)}, bf16[64,512]{1,0:T(8,128)(2,1)S(1)}, u32[]{:S(2)}, u32[]{:S(2)}) collective-permute-start(bf16[64,512]{1,0:T(8,128)(2,1)S(1)} %fusion), channel_id=1, source_target_pairs={{0,48},{4,52},{8,12},{12,8},{16,20},{20,16},{24,28},{28,24},{32,36... | collective-permute-start | bytes 196616 | tf_op jit(solution)/shard_map/ppermute | solution.py:283
  54.0 6.3 %collective-permute-start.19 = (bf16[64,512]{1,0:T(8,128)(2,1)S(1)}, bf16[64,512]{1,0:T(8,128)(2,1)S(1)}, u32[]{:S(2)}, u32[]{:S(2)}) collective-permute-start(bf16[64,512]{1,0:T(8,128)(2,1)S(1)} %fusion), channel_id=1, source_target_pairs={{0,24},{4,28},{8,12},{12,8},{16,20},{20,16},{24,0},{28,4},{32,36},... | collective-permute-start | bytes 196616 | tf_op jit(solution)/shard_map/ppermute | solution.py:283
  54.7 6.1 %collective-permute-start.20 = (bf16[64,512]{1,0:T(8,128)(2,1)S(1)}, bf16[64,512]{1,0:T(8,128)(2,1)S(1)}, u32[]{:S(2)}, u32[]{:S(2)}) collective-permute-start(bf16[64,512]{1,0:T(8,128)(2,1)S(1)} %fusion), channel_id=1, source_target_pairs={{0,40},{4,44},{8,12},{12,8},{16,20},{20,16},{24,28},{28,24},{32,36... | collective-permute-start | bytes 196616 | tf_op jit(solution)/shard_map/ppermute | solution.py:283
  55.6 7.0 %collective-permute-start.21 = (bf16[64,512]{1,0:T(8,128)(2,1)S(1)}, bf16[64,512]{1,0:T(8,128)(2,1)S(1)}, u32[]{:S(2)}, u32[]{:S(2)}) collective-permute-start(bf16[64,512]{1,0:T(8,128)(2,1)S(1)} %fusion), channel_id=1, source_target_pairs={{0,32},{4,36},{8,12},{12,8},{16,20},{20,16},{24,28},{28,24},{32,0}... | collective-permute-start | bytes 196616 | tf_op jit(solution)/shard_map/ppermute | solution.py:283
  62.8 5.0 %collective-permute-start.22 = (bf16[64,512]{1,0:T(8,128)(2,1)S(1)}, bf16[64,512]{1,0:T(8,128)(2,1)S(1)}, u32[]{:S(2)}, u32[]{:S(2)}) collective-permute-start(bf16[64,512]{1,0:T(8,128)(2,1)S(1)} %get-tuple-element.82), channel_id=1, source_target_pairs={{0,128},{4,132},{8,12},{12,8},{16,20},{20,16},{24,28},{28,24},{32,... | collective-permute-start | bytes 196616 | tf_op jit(solution)/shard_map/ppermute | solution.py:283
  62.9 5.3 %collective-permute-start.23 = (bf16[64,512]{1,0:T(8,128)(2,1)S(1)}, bf16[64,512]{1,0:T(8,128)(2,1)S(1)}, u32[]{:S(2)}, u32[]{:S(2)}) collective-permute-start(bf16[64,512]{1,0:T(8,128)(2,1)S(1)} %get-tuple-element.82), channel_id=1, source_target_pairs={{0,192},{4,196},{8,12},{12,8},{16,20},{20,16},{24,28},{28,24},{32,... | collective-permute-start | bytes 196616 | tf_op jit(solution)/shard_map/ppermute | solution.py:283
  66.5 4.7 %collective-permute-start.27 = (f32[8,256]{1,0:T(8,128)S(1)}, f32[8,256]{1,0:T(8,128)S(1)}, u32[]{:S(2)}, u32[]{:S(2)}) collective-permute-start(f32[8,256]{1,0:T(8,128)S(1)} %get-tuple-element.83.rows), channel_id=1, source_target_pairs={{0,248},{4,252},{8,0},{12,4},{16,8},{20,12},{24,16},{28,20},{32,24... | collective-permute-start | bytes 24584 | tf_op jit(solution)/shard_map/ppermute | solution.py:258
  69.6 4.9 %collective-permute-start.25 = (bf16[64,512]{1,0:T(8,128)(2,1)S(1)}, bf16[64,512]{1,0:T(8,128)(2,1)S(1)}, u32[]{:S(2)}, u32[]{:S(2)}) collective-permute-start(bf16[64,512]{1,0:T(8,128)(2,1)S(1)} %get-tuple-element.94), channel_id=1, source_target_pairs={{0,4},{4,0},{8,12},{12,8},{16,20},{20,16},{24,28},{28,24},{32,36},... | collective-permute-start | bytes 196616 | tf_op jit(solution)/shard_map/ppermute | solution.py:268
  (13 other events, 98.9 us)

commit v5 on v4

--- a/solution.py
+++ b/solution.py
@@ -21,7 +21,7 @@
 BF16 = jnp.bfloat16
 VMEM_LIMIT = 40 * 1024 * 1024
 R_AT = "sent"
-FAN = ((2, 6), (7, 3), (1, 5))
+FAN = ((1, 5), (7, 3), (2, 6))
 DK_WINDOW = False
 QD_WRAP = True
 KV_WRAP = True
@@ -284,7 +284,7 @@
 
 
 Z_ORDER = (1, 7, 2, 6, 3, 5, 4)
-Y_ORDER = (2, 3, 1)
+Y_ORDER = (1, 3, 2)
 SPREAD = (
     ([(at(0, 0, 0), at(0, 4, 0))],),
     tuple([(at(0, 0, 0), at(0, a, 0)), (at(0, 4, 0), at(0, b, 0))] for a, b in FAN),

time: 77.4 us -> 77.2 us (level); the launches traced: 76 us -> 77 us
  waiting for transfers between devices: 13.4 us -> 15.4 us
  starting transfers between devices: 40.6 us -> 39.6 us
    ppermute x5, starting transfers between devices: 16.1 us -> 13.6 us  [swap(): return lax.ppermute(x, 'ctx', [(i, i ^ 1) for i in range(NCTX)])]
    ppermute x7, starting transfers between devices: 8.73 us -> 9.89 us  [shift(): return lax.ppermute(x, 'ctx', [(i, (i + by) % NCTX) for i in range(NCTX)])]
    ppermute x7, waiting for transfers between devices: 7.54 us -> 8.57 us  [shift(): return lax.ppermute(x, 'ctx', [(i, (i + by) % NCTX) for i in range(NCTX)])]
    ppermute x10, waiting for transfers between devices: 3.91 us -> 4.89 us  [exchange(): return lax.ppermute(x, 'ctx', sorted(to.items()))]
  transfers between devices with their start and end apart: 29 -> 29, of which waited for: 9 -> 8; matrix products, arithmetic and copies ran while one was open for 2% -> 2% of each run, Pallas kernels for 15% -> 15%
where the time goes in v5:
time: 77.2 us; the launch traced here: 77 us
  starting transfers between devices  39.6 us (51%)
  Pallas kernels  17.8 us (23%)
  waiting for transfers between devices  15.4 us (20%)
  other arithmetic  2.22 us (3%)
  between operations  1.1 us (1%)
  local copies, waits for them, and re-layouts  0.88 us (1%)
    ppermute x5, starting transfers between devices, swap(): return lax.ppermute(x, 'ctx', [(i, i ^ 1) for i in range(NCTX)])  13.6 us
    pallas_call x5, Pallas kernels, call(): pl.pallas_call(kernel, out_shape=[jax.ShapeDtypeStruct(s, t) for s, t in...  13.3 us
    ppermute x10, starting transfers between devices, exchange(): return lax.ppermute(x, 'ctx', sorted(to.items()))  10.1 us
    ppermute x7, starting transfers between devices, shift(): return lax.ppermute(x, 'ctx', [(i, (i + by) % NCTX) for i in range(NCTX)])  9.89 us
    ppermute x7, waiting for transfers between devices, shift(): return lax.ppermute(x, 'ctx', [(i, (i + by) % NCTX) for i in range(NCTX)])  8.57 us
    ppermute x7, starting transfers between devices, deliver(): return lax.ppermute(x, 'ctx', pairs)  5.95 us
    ppermute x10, waiting for transfers between devices, exchange(): return lax.ppermute(x, 'ctx', sorted(to.items()))  4.89 us
    pallas_call x1, Pallas kernels, on_device(): pl.pallas_call(pack_kernel, out_shape=[jax.ShapeDtypeStruct(s, BF16) for...  3.2 us
  transfers between devices with their start and end apart: 29, of which 8 were waited for; matrix products, arithmetic and copies ran while one was open for 2% of the time, Pallas kernels for 15%

profile of v5, /device:TPU:1, one launch (start us, length us, event | category | flops | bytes accessed | tf_op | source)
XLA Modules:
  0.0 77.0 jit_solution(9581786345994283501)
XLA Ops:
  1.2 3.2 %shard_map.84 = (bf16[512,512]{1,0:T(8,128)(2,1)}, bf16[512,512]{1,0:T(8,128)(2,1)}, bf16[512,512]{1,0:T(8,128)(2,1)}, bf16[128,512]{1,0:T(8,128)(2,1)}) custom-call(s32[2]{0:T(128)} %pad_add_fusion.1.info, bf16[256,512]{1,0:T(8,128)(2,1)} %k.7, bf16[256,512]{1,0:T(8,128)(2,1)} %v.7, bf16[256,512]{1,0:T(8,128)(2,1)} %q.9, bf16[256,512]{1,0:T(8,128)(2,1)} %do.7), custom_call_target="tpu_custom_call" | custom-call | tf_op jit(solution)/shard_map/pallas_call | solution.py:343
  4.4 3.3 %collective-permute-start.2 = (bf16[512,512]{1,0:T(8,128)(2,1)}, bf16[512,512]{1,0:T(8,128)(2,1)S(1)}, u32[]{:S(2)}, u32[]{:S(2)}) collective-permute-start(bf16[512,512]{1,0:T(8,128)(2,1)} %get-tuple-element.52), channel_id=1, source_target_pairs={{0,4},{4,0},{8,12},{12,8},{16,20},{20,16},{24,28},{28,24},{32,36},... | collective-permute-start | bytes 1572872 | tf_op jit(solution)/shard_map/ppermute | solution.py:268
  7.8 6.3 %collective-permute-start.1 = (bf16[512,512]{1,0:T(8,128)(2,1)}, bf16[512,512]{1,0:T(8,128)(2,1)S(1)}, u32[]{:S(2)}, u32[]{:S(2)}) collective-permute-start(bf16[512,512]{1,0:T(8,128)(2,1)} %get-tuple-element.50), channel_id=1, source_target_pairs={{0,248},{4,252},{8,0},{12,4},{16,8},{20,12},{24,16},{28,20},{32,24... | collective-permute-start | bytes 1572872 | tf_op jit(solution)/shard_map/ppermute | solution.py:258
  16.2 1.9 %shard_map.85 = (f32[8,256]{1,0:T(8,128)S(1)}, f32[512,256]{1,0:T(8,128)S(1)}, f32[512,256]{1,0:T(8,128)S(1)}) custom-call(s32[6]{0:T(128)S(1)} %pad_add_fusion.info, s32[8,256]{1,0:T(8,128)S(1)} %maximum_select_fusion.lo_ref, bf16[256,512]{1,0:T(8,128)(2,1)S(1)} %copy-done, bf16[256,512]{1,0:T(8,128)(2,1)S(1)} %copy-done.2, bf16[256,512]{1,0:T(8,128)(2,1)S(1)} %copy-done.3, ...), custom_call_target="tpu_custom_call" | custom-call | flops 140000000 | bytes 4194304 | tf_op jit(solution)/shard_map/pallas_call | solution.py:246
  20.1 6.3 %collective-permute-done.kv2 = bf16[512,512]{1,0:T(8,128)(2,1)S(1)} collective-permute-done((bf16[512,512]{1,0:T(8,128)(2,1)}, bf16[512,512]{1,0:T(8,128)(2,1)S(1)}, u32[]{:S(2)}, u32[]{:S(2)}) %collective-permute-start) | collective-permute-done | bytes 524320 | tf_op jit(solution)/shard_map/ppermute | solution.py:258
  28.1 1.3 %collective-permute-start.11 = (bf16[128,512]{1,0:T(8,128)(2,1)S(1)}, bf16[128,512]{1,0:T(8,128)(2,1)}, u32[]{:S(2)}, u32[]{:S(2)}) collective-permute-start(bf16[128,512]{1,0:T(8,128)(2,1)S(1)} %select_select_fusion.1), channel_id=1, source_target_pairs={{0,192},{8,200},{16,208},{24,216},{32,224},{40,232},{48,240},{56,2... | collective-permute-start | bytes 393224 | tf_op jit(solution)/shard_map/ppermute | solution.py:276
  29.4 1.3 %collective-permute-start.12 = (bf16[128,512]{1,0:T(8,128)(2,1)S(1)}, bf16[128,512]{1,0:T(8,128)(2,1)}, u32[]{:S(2)}, u32[]{:S(2)}) collective-permute-start(bf16[128,512]{1,0:T(8,128)(2,1)S(1)} %select_select_fusion.1), channel_id=1, source_target_pairs={{0,64},{8,72},{16,80},{24,88},{32,96},{40,104},{48,112},{56,120},{... | collective-permute-start | bytes 393224 | tf_op jit(solution)/shard_map/ppermute | solution.py:276
  30.7 3.8 %collective-permute-start.9 = (bf16[512,512]{1,0:T(8,128)(2,1)}, bf16[512,512]{1,0:T(8,128)(2,1)S(1)}, u32[]{:S(2)}, u32[]{:S(2)}) collective-permute-start(bf16[512,512]{1,0:T(8,128)(2,1)} %broadcast_select_fusion), channel_id=1, source_target_pairs={{0,4},{4,0},{8,12},{12,8},{16,20},{20,16},{24,28},{28,24},{32,36},... | collective-permute-start | bytes 1572872 | tf_op jit(solution)/shard_map/ppermute | solution.py:268
  34.5 1.7 %collective-permute-start.7 = (bf16[512,512]{1,0:T(8,128)(2,1)S(1)}, bf16[512,512]{1,0:T(8,128)(2,1)S(1)}, u32[]{:S(2)}, u32[]{:S(2)}) collective-permute-start(bf16[512,512]{1,0:T(8,128)(2,1)S(1)} %collective-permute-done.kv2), channel_id=1, source_target_pairs={{0,4},{4,8},{8,12},{12,16},{16,20},{20,24},{24,28},{28,32},{32,36}... | collective-permute-start | bytes 1572872 | tf_op jit(solution)/shard_map/ppermute | solution.py:258
  36.2 3.5 %collective-permute-start.13 = (bf16[128,512]{1,0:T(8,128)(2,1)S(1)}, bf16[128,512]{1,0:T(8,128)(2,1)S(1)}, u32[]{:S(2)}, u32[]{:S(2)}) collective-permute-start(bf16[128,512]{1,0:T(8,128)(2,1)S(1)} %select_select_fusion), channel_id=1, source_target_pairs={{0,4},{4,0},{8,12},{12,8},{16,20},{20,16},{24,28},{28,24},{32,36},... | collective-permute-start | bytes 393224 | tf_op jit(solution)/shard_map/ppermute | solution.py:268
  40.7 2.1 %shard_map.86 = (f32[8,256]{1,0:T(8,128)S(1)}, f32[512,256]{1,0:T(8,128)S(1)}) custom-call(s32[6]{0:T(128)S(1)} %pad_add_fusion.info, s32[8,256]{1,0:T(8,128)S(1)} %maximum_select_fusion.lo_ref, f32[8,256]{1,0:T(8,128)S(1)} %get-tuple-element.60.stat_in, f32[512,256]{1,0:T(8,128)S(1)} %copy-done.5, bf16[256,512]{1,0:T(8,128)(2,1)S(1)} %copy-done, ...), custom_call_target="tpu_custom_call" | custom-call | flops 280000000 | bytes 4194304 | tf_op jit(solution)/shard_map/pallas_call | solution.py:246
  42.9 2.2 %collective-permute-done.8.qd3 = bf16[512,512]{1,0:T(8,128)(2,1)S(1)} collective-permute-done((bf16[512,512]{1,0:T(8,128)(2,1)S(1)}, bf16[512,512]{1,0:T(8,128)(2,1)S(1)}, u32[]{:S(2)}, u32[]{:S(2)}) %collective-permute-start.8) | collective-permute-done | bytes 524320 | tf_op jit(solution)/shard_map/ppermute | solution.py:258
  45.1 2.1 %shard_map.87 = (f32[512,256]{1,0:T(8,128)S(1)}, f32[8,256]{1,0:T(8,128)S(1)}, bf16[64,512]{1,0:T(8,128)(2,1)S(1)}, bf16[64,512]{1,0:T(8,128)(2,1)S(1)}) custom-call(s32[6]{0:T(128)S(1)} %pad_add_fusion.info, s32[8,256]{1,0:T(8,128)S(1)} %maximum_select_fusion.lo_ref, f32[8,256]{1,0:T(8,128)S(1)} %get-tuple-element.66.stat, ...), custom_call_target="tpu_custom_call" | custom-call | flops 300000000 | bytes 4194304 | tf_op jit(solution)/shard_map/pallas_call | solution.py:246
  47.1 1.5 %collective-permute-start.14 = (bf16[64,512]{1,0:T(8,128)(2,1)S(1)}, bf16[64,512]{1,0:T(8,128)(2,1)S(1)}, u32[]{:S(2)}, u32[]{:S(2)}) collective-permute-start(bf16[64,512]{1,0:T(8,128)(2,1)S(1)} %broadcast_select_fusion.3), channel_id=1, source_target_pairs={{0,4},{4,0},{8,12},{12,8},{16,20},{20,16},{24,28},{28,24},{32,36},... | collective-permute-start | bytes 196616 | tf_op jit(solution)/shard_map/ppermute | solution.py:268
  49.6 3.4 %collective-permute-start.16 = (bf16[64,512]{1,0:T(8,128)(2,1)S(1)}, bf16[64,512]{1,0:T(8,128)(2,1)S(1)}, u32[]{:S(2)}, u32[]{:S(2)}) collective-permute-start(bf16[64,512]{1,0:T(8,128)(2,1)S(1)} %fusion), channel_id=1, source_target_pairs={{0,56},{4,60},{8,12},{12,8},{16,20},{20,16},{24,28},{28,24},{32,36... | collective-permute-start | bytes 196616 | tf_op jit(solution)/shard_map/ppermute | solution.py:283
  53.0 1.7 %collective-permute-start.19 = (bf16[64,512]{1,0:T(8,128)(2,1)S(1)}, bf16[64,512]{1,0:T(8,128)(2,1)S(1)}, u32[]{:S(2)}, u32[]{:S(2)}) collective-permute-start(bf16[64,512]{1,0:T(8,128)(2,1)S(1)} %fusion), channel_id=1, source_target_pairs={{0,24},{4,28},{8,12},{12,8},{16,20},{20,16},{24,0},{28,4},{32,36},... | collective-permute-start | bytes 196616 | tf_op jit(solution)/shard_map/ppermute | solution.py:283
  55.9 4.6 %shard_map.88 = (f32[256,512]{1,0:T(8,128)}, f32[256,512]{1,0:T(8,128)}, f32[256,512]{1,0:T(8,128)S(1)}, f32[256,512]{1,0:T(8,128)S(1)}) custom-call(s32[6]{0:T(128)S(1)} %pad_add_fusion.info, s32[8,256]{1,0:T(8,128)S(1)} %maximum_select_fusion.lo_ref, f32[8,256]{1,0:T(8,128)S(1)} %get-tuple-element.83.rows, f32[512,256]{1,0:T(8,128)S(1)} %get-tuple-element.74.out_t, ...), custom_call_target="tpu_custom_call" | custom-call | flops 1000000000 | bytes 4194304 | tf_op jit(solution)/shard_map/pallas_call | solution.py:246
  60.9 1.4 %collective-permute-done.21 = bf16[64,512]{1,0:T(8,128)(2,1)S(1)} collective-permute-done((bf16[64,512]{1,0:T(8,128)(2,1)S(1)}, bf16[64,512]{1,0:T(8,128)(2,1)S(1)}, u32[]{:S(2)}, u32[]{:S(2)}) %collective-permute-start.21) | collective-permute-done | bytes 65568 | tf_op jit(solution)/shard_map/ppermute | solution.py:283
  62.5 4.0 %collective-permute-start.23 = (bf16[64,512]{1,0:T(8,128)(2,1)S(1)}, bf16[64,512]{1,0:T(8,128)(2,1)S(1)}, u32[]{:S(2)}, u32[]{:S(2)}) collective-permute-start(bf16[64,512]{1,0:T(8,128)(2,1)S(1)} %get-tuple-element.82), channel_id=1, source_target_pairs={{0,192},{4,196},{8,12},{12,8},{16,20},{20,16},{24,28},{28,24},{32,... | collective-permute-start | bytes 196616 | tf_op jit(solution)/shard_map/ppermute | solution.py:283
  66.9 1.3 %collective-permute-start.27 = (f32[8,256]{1,0:T(8,128)S(1)}, f32[8,256]{1,0:T(8,128)S(1)}, u32[]{:S(2)}, u32[]{:S(2)}) collective-permute-start(f32[8,256]{1,0:T(8,128)S(1)} %get-tuple-element.83.rows), channel_id=1, source_target_pairs={{0,248},{4,252},{8,0},{12,4},{16,8},{20,12},{24,16},{28,20},{32,24... | collective-permute-start | bytes 24584 | tf_op jit(solution)/shard_map/ppermute | solution.py:258
  68.5 2.7 %collective-permute-done.24 = bf16[64,512]{1,0:T(8,128)(2,1)S(1)} collective-permute-done((bf16[64,512]{1,0:T(8,128)(2,1)S(1)}, bf16[64,512]{1,0:T(8,128)(2,1)S(1)}, u32[]{:S(2)}, u32[]{:S(2)}) %collective-permute-start.24) | collective-permute-done | bytes 65568 | tf_op jit(solution)/shard_map/ppermute | solution.py:283
  71.2 1.6 %collective-permute-start.25 = (bf16[64,512]{1,0:T(8,128)(2,1)S(1)}, bf16[64,512]{1,0:T(8,128)(2,1)S(1)}, u32[]{:S(2)}, u32[]{:S(2)}) collective-permute-start(bf16[64,512]{1,0:T(8,128)(2,1)S(1)} %get-tuple-element.94), channel_id=1, source_target_pairs={{0,4},{4,0},{8,12},{12,8},{16,20},{20,16},{24,28},{28,24},{32,36},... | collective-permute-start | bytes 196616 | tf_op jit(solution)/shard_map/ppermute | solution.py:268
  72.8 2.7 %shard_map.89 = (f32[256,512]{1,0:T(8,128)}, f32[256,512]{1,0:T(8,128)}, f32[64,512]{1,0:T(8,128)S(1)}, f32[64,512]{1,0:T(8,128)S(1)}) custom-call(s32[6]{0:T(128)S(1)} %pad_add_fusion.info, s32[8,256]{1,0:T(8,128)S(1)} %maximum_select_fusion.lo_ref, f32[8,256]{1,0:T(8,128)S(1)} %collective-permute-done.26.r1, f32[8,256]{1,0:T(8,128)S(1)} %collective-permute-done.27.r2, ...), custom_call_target="tpu_custom_call" | custom-call | flops 900000000 | bytes 4194304 | tf_op jit(solution)/shard_map/pallas_call | solution.py:246
  75.5 1.3 %shard_map.90 = (f32[256,512]{1,0:T(8,128)}, f32[256,512]{1,0:T(8,128)}) custom-call(s32[6]{0:T(128)S(1)} %pad_add_fusion.info, f32[64,512]{1,0:T(8,128)S(1)} %get-tuple-element.95.part, bf16[64,512]{1,0:T(8,128)(2,1)S(1)} %collective-permute-done.25.other, f32[64,512]{1,0:T(8,128)S(1)} %get-tuple-element.88.dk_top, ...), custom_call_target="tpu_custom_call", output_to_operand_aliasing={{0}: (5, {}), {1}: (6, {})} | custom-call | tf_op jit(solution)/shard_map/pallas_call | solution.py:417
  (77 shorter events, 10.7 us)
Async XLA Ops:
  4.4 10.8 %collective-permute-start.2 = (bf16[512,512]{1,0:T(8,128)(2,1)}, bf16[512,512]{1,0:T(8,128)(2,1)S(1)}, u32[]{:S(2)}, u32[]{:S(2)}) collective-permute-start(bf16[512,512]{1,0:T(8,128)(2,1)} %get-tuple-element.52), channel_id=1, source_target_pairs={{0,4},{4,0},{8,12},{12,8},{16,20},{20,16},{24,28},{28,24},{32,36},... | collective-permute-start | bytes 1572872 | tf_op jit(solution)/shard_map/ppermute | solution.py:268
  7.8 18.7 %collective-permute-start = (bf16[512,512]{1,0:T(8,128)(2,1)}, bf16[512,512]{1,0:T(8,128)(2,1)S(1)}, u32[]{:S(2)}, u32[]{:S(2)}) collective-permute-start(bf16[512,512]{1,0:T(8,128)(2,1)} %get-tuple-element.49), channel_id=1, source_target_pairs={{0,8},{4,12},{8,16},{12,20},{16,24},{20,28},{24,32},{28,36},{32,40... | collective-permute-start | bytes 1572872 | tf_op jit(solution)/shard_map/ppermute | solution.py:258
  7.8 18.7 %collective-permute-start.1 = (bf16[512,512]{1,0:T(8,128)(2,1)}, bf16[512,512]{1,0:T(8,128)(2,1)S(1)}, u32[]{:S(2)}, u32[]{:S(2)}) collective-permute-start(bf16[512,512]{1,0:T(8,128)(2,1)} %get-tuple-element.50), channel_id=1, source_target_pairs={{0,248},{4,252},{8,0},{12,4},{16,8},{20,12},{24,16},{28,20},{32,24... | collective-permute-start | bytes 1572872 | tf_op jit(solution)/shard_map/ppermute | solution.py:258
  18.1 9.3 %collective-permute-start.4 = (bf16[128,512]{1,0:T(8,128)(2,1)S(1)}, bf16[128,512]{1,0:T(8,128)(2,1)S(1)}, u32[]{:S(2)}, u32[]{:S(2)}) collective-permute-start(bf16[128,512]{1,0:T(8,128)(2,1)S(1)} %broadcast_select_fusion.2), channel_id=1, source_target_pairs={{0,16},{32,48},{1,17},{33,49},{2,18},{34,50},{3,19},{35,51}} | collective-permute-start | bytes 393224 | tf_op jit(solution)/shard_map/ppermute | solution.py:276
  18.8 8.6 %collective-permute-start.5 = (bf16[128,512]{1,0:T(8,128)(2,1)S(1)}, bf16[128,512]{1,0:T(8,128)(2,1)S(1)}, u32[]{:S(2)}, u32[]{:S(2)}) collective-permute-start(bf16[128,512]{1,0:T(8,128)(2,1)S(1)} %broadcast_select_fusion.2), channel_id=1, source_target_pairs={{0,56},{32,24},{1,57},{33,25},{2,58},{34,26},{3,59},{35,27}} | collective-permute-start | bytes 393224 | tf_op jit(solution)/shard_map/ppermute | solution.py:276
  19.4 7.9 %collective-permute-start.6 = (bf16[128,512]{1,0:T(8,128)(2,1)S(1)}, bf16[128,512]{1,0:T(8,128)(2,1)S(1)}, u32[]{:S(2)}, u32[]{:S(2)}) collective-permute-start(bf16[128,512]{1,0:T(8,128)(2,1)S(1)} %broadcast_select_fusion.2), channel_id=1, source_target_pairs={{0,8},{32,40},{1,9},{33,41},{2,10},{34,42},{3,11},{35,43}} | collective-permute-start | bytes 393224 | tf_op jit(solution)/shard_map/ppermute | solution.py:276
  27.4 8.8 %collective-permute-start.10 = (bf16[128,512]{1,0:T(8,128)(2,1)S(1)}, bf16[128,512]{1,0:T(8,128)(2,1)S(1)}, u32[]{:S(2)}, u32[]{:S(2)}) collective-permute-start(bf16[128,512]{1,0:T(8,128)(2,1)S(1)} %select_select_fusion.1), channel_id=1, source_target_pairs={{0,128},{8,136},{16,144},{24,152},{32,160},{40,168},{48,176},{56,1... | collective-permute-start | bytes 393224 | tf_op jit(solution)/shard_map/ppermute | solution.py:276
  28.1 8.1 %collective-permute-start.11 = (bf16[128,512]{1,0:T(8,128)(2,1)S(1)}, bf16[128,512]{1,0:T(8,128)(2,1)}, u32[]{:S(2)}, u32[]{:S(2)}) collective-permute-start(bf16[128,512]{1,0:T(8,128)(2,1)S(1)} %select_select_fusion.1), channel_id=1, source_target_pairs={{0,192},{8,200},{16,208},{24,216},{32,224},{40,232},{48,240},{56,2... | collective-permute-start | bytes 393224 | tf_op jit(solution)/shard_map/ppermute | solution.py:276
  29.4 6.8 %collective-permute-start.12 = (bf16[128,512]{1,0:T(8,128)(2,1)S(1)}, bf16[128,512]{1,0:T(8,128)(2,1)}, u32[]{:S(2)}, u32[]{:S(2)}) collective-permute-start(bf16[128,512]{1,0:T(8,128)(2,1)S(1)} %select_select_fusion.1), channel_id=1, source_target_pairs={{0,64},{8,72},{16,80},{24,88},{32,96},{40,104},{48,112},{56,120},{... | collective-permute-start | bytes 393224 | tf_op jit(solution)/shard_map/ppermute | solution.py:276
  30.7 10.0 %collective-permute-start.9 = (bf16[512,512]{1,0:T(8,128)(2,1)}, bf16[512,512]{1,0:T(8,128)(2,1)S(1)}, u32[]{:S(2)}, u32[]{:S(2)}) collective-permute-start(bf16[512,512]{1,0:T(8,128)(2,1)} %broadcast_select_fusion), channel_id=1, source_target_pairs={{0,4},{4,0},{8,12},{12,8},{16,20},{20,16},{24,28},{28,24},{32,36},... | collective-permute-start | bytes 1572872 | tf_op jit(solution)/shard_map/ppermute | solution.py:268
  34.5 8.4 %collective-permute-start.7 = (bf16[512,512]{1,0:T(8,128)(2,1)S(1)}, bf16[512,512]{1,0:T(8,128)(2,1)S(1)}, u32[]{:S(2)}, u32[]{:S(2)}) collective-permute-start(bf16[512,512]{1,0:T(8,128)(2,1)S(1)} %collective-permute-done.kv2), channel_id=1, source_target_pairs={{0,4},{4,8},{8,12},{12,16},{16,20},{20,24},{24,28},{28,32},{32,36}... | collective-permute-start | bytes 1572872 | tf_op jit(solution)/shard_map/ppermute | solution.py:258
  36.2 8.9 %collective-permute-start.8 = (bf16[512,512]{1,0:T(8,128)(2,1)S(1)}, bf16[512,512]{1,0:T(8,128)(2,1)S(1)}, u32[]{:S(2)}, u32[]{:S(2)}) collective-permute-start(bf16[512,512]{1,0:T(8,128)(2,1)S(1)} %collective-permute-done.1.qd2), channel_id=1, source_target_pairs={{0,252},{4,0},{8,4},{12,8},{16,12},{20,16},{24,20},{28,24},{32,28}... | collective-permute-start | bytes 1572872 | tf_op jit(solution)/shard_map/ppermute | solution.py:258
  49.5 5.2 %collective-permute-start.15 = (bf16[64,512]{1,0:T(8,128)(2,1)S(1)}, bf16[64,512]{1,0:T(8,128)(2,1)S(1)}, u32[]{:S(2)}, u32[]{:S(2)}) collective-permute-start(bf16[64,512]{1,0:T(8,128)(2,1)S(1)} %fusion), channel_id=1, source_target_pairs={{0,8},{4,12},{8,0},{12,4},{16,20},{20,16},{24,28},{28,24},{32,36},... | collective-permute-start | bytes 196616 | tf_op jit(solution)/shard_map/ppermute | solution.py:283
  49.6 5.5 %collective-permute-start.16 = (bf16[64,512]{1,0:T(8,128)(2,1)S(1)}, bf16[64,512]{1,0:T(8,128)(2,1)S(1)}, u32[]{:S(2)}, u32[]{:S(2)}) collective-permute-start(bf16[64,512]{1,0:T(8,128)(2,1)S(1)} %fusion), channel_id=1, source_target_pairs={{0,56},{4,60},{8,12},{12,8},{16,20},{20,16},{24,28},{28,24},{32,36... | collective-permute-start | bytes 196616 | tf_op jit(solution)/shard_map/ppermute | solution.py:283
  53.0 7.5 %collective-permute-start.17 = (bf16[64,512]{1,0:T(8,128)(2,1)S(1)}, bf16[64,512]{1,0:T(8,128)(2,1)S(1)}, u32[]{:S(2)}, u32[]{:S(2)}) collective-permute-start(bf16[64,512]{1,0:T(8,128)(2,1)S(1)} %fusion), channel_id=1, source_target_pairs={{0,16},{4,20},{8,12},{12,8},{16,0},{20,4},{24,28},{28,24},{32,36},... | collective-permute-start | bytes 196616 | tf_op jit(solution)/shard_map/ppermute | solution.py:283
  53.0 7.5 %collective-permute-start.18 = (bf16[64,512]{1,0:T(8,128)(2,1)S(1)}, bf16[64,512]{1,0:T(8,128)(2,1)S(1)}, u32[]{:S(2)}, u32[]{:S(2)}) collective-permute-start(bf16[64,512]{1,0:T(8,128)(2,1)S(1)} %fusion), channel_id=1, source_target_pairs={{0,48},{4,52},{8,12},{12,8},{16,20},{20,16},{24,28},{28,24},{32,36... | collective-permute-start | bytes 196616 | tf_op jit(solution)/shard_map/ppermute | solution.py:283
  53.0 7.5 %collective-permute-start.19 = (bf16[64,512]{1,0:T(8,128)(2,1)S(1)}, bf16[64,512]{1,0:T(8,128)(2,1)S(1)}, u32[]{:S(2)}, u32[]{:S(2)}) collective-permute-start(bf16[64,512]{1,0:T(8,128)(2,1)S(1)} %fusion), channel_id=1, source_target_pairs={{0,24},{4,28},{8,12},{12,8},{16,20},{20,16},{24,0},{28,4},{32,36},... | collective-permute-start | bytes 196616 | tf_op jit(solution)/shard_map/ppermute | solution.py:283
  54.7 6.1 %collective-permute-start.20 = (bf16[64,512]{1,0:T(8,128)(2,1)S(1)}, bf16[64,512]{1,0:T(8,128)(2,1)S(1)}, u32[]{:S(2)}, u32[]{:S(2)}) collective-permute-start(bf16[64,512]{1,0:T(8,128)(2,1)S(1)} %fusion), channel_id=1, source_target_pairs={{0,40},{4,44},{8,12},{12,8},{16,20},{20,16},{24,28},{28,24},{32,36... | collective-permute-start | bytes 196616 | tf_op jit(solution)/shard_map/ppermute | solution.py:283
  55.2 7.1 %collective-permute-start.21 = (bf16[64,512]{1,0:T(8,128)(2,1)S(1)}, bf16[64,512]{1,0:T(8,128)(2,1)S(1)}, u32[]{:S(2)}, u32[]{:S(2)}) collective-permute-start(bf16[64,512]{1,0:T(8,128)(2,1)S(1)} %fusion), channel_id=1, source_target_pairs={{0,32},{4,36},{8,12},{12,8},{16,20},{20,16},{24,28},{28,24},{32,0}... | collective-permute-start | bytes 196616 | tf_op jit(solution)/shard_map/ppermute | solution.py:283
  62.4 5.8 %collective-permute-start.22 = (bf16[64,512]{1,0:T(8,128)(2,1)S(1)}, bf16[64,512]{1,0:T(8,128)(2,1)S(1)}, u32[]{:S(2)}, u32[]{:S(2)}) collective-permute-start(bf16[64,512]{1,0:T(8,128)(2,1)S(1)} %get-tuple-element.82), channel_id=1, source_target_pairs={{0,64},{4,68},{8,12},{12,8},{16,20},{20,16},{24,28},{28,24},{32,36... | collective-permute-start | bytes 196616 | tf_op jit(solution)/shard_map/ppermute | solution.py:283
  62.5 6.0 %collective-permute-start.23 = (bf16[64,512]{1,0:T(8,128)(2,1)S(1)}, bf16[64,512]{1,0:T(8,128)(2,1)S(1)}, u32[]{:S(2)}, u32[]{:S(2)}) collective-permute-start(bf16[64,512]{1,0:T(8,128)(2,1)S(1)} %get-tuple-element.82), channel_id=1, source_target_pairs={{0,192},{4,196},{8,12},{12,8},{16,20},{20,16},{24,28},{28,24},{32,... | collective-permute-start | bytes 196616 | tf_op jit(solution)/shard_map/ppermute | solution.py:283
  66.5 4.6 %collective-permute-start.24 = (bf16[64,512]{1,0:T(8,128)(2,1)S(1)}, bf16[64,512]{1,0:T(8,128)(2,1)S(1)}, u32[]{:S(2)}, u32[]{:S(2)}) collective-permute-start(bf16[64,512]{1,0:T(8,128)(2,1)S(1)} %get-tuple-element.82), channel_id=1, source_target_pairs={{0,128},{4,132},{8,12},{12,8},{16,20},{20,16},{24,28},{28,24},{32,... | collective-permute-start | bytes 196616 | tf_op jit(solution)/shard_map/ppermute | solution.py:283
  66.5 4.7 %collective-permute-start.26 = (f32[8,256]{1,0:T(8,128)S(1)}, f32[8,256]{1,0:T(8,128)S(1)}, u32[]{:S(2)}, u32[]{:S(2)}) collective-permute-start(f32[8,256]{1,0:T(8,128)S(1)} %get-tuple-element.83.rows), channel_id=1, source_target_pairs={{0,252},{4,0},{8,4},{12,8},{16,12},{20,16},{24,20},{28,24},{32,28}... | collective-permute-start | bytes 24584 | tf_op jit(solution)/shard_map/ppermute | solution.py:258
  66.9 5.9 %collective-permute-start.27 = (f32[8,256]{1,0:T(8,128)S(1)}, f32[8,256]{1,0:T(8,128)S(1)}, u32[]{:S(2)}, u32[]{:S(2)}) collective-permute-start(f32[8,256]{1,0:T(8,128)S(1)} %get-tuple-element.83.rows), channel_id=1, source_target_pairs={{0,248},{4,252},{8,0},{12,4},{16,8},{20,12},{24,16},{28,20},{32,24... | collective-permute-start | bytes 24584 | tf_op jit(solution)/shard_map/ppermute | solution.py:258
  (13 other events, 100.1 us)
